TPU v7x, 128 devices: a whole 4x4x4 slice. The times are simulated.
128 devices in a mesh: row: 8 (over z, x_hi), col: 16 (over y, x_lo, core).
Axes of the slice: x: 4 (x_hi: 2, x_lo: 2; x = x_hi * 2 + x_lo), y: 4, z: 4, core: 2. Of those that a mesh axis runs over, the one named last changes fastest.
Arguments:
- tokens: bfloat16 [1024, 8192], P('row', 'col'), may hold values from -6 to 6
- out_grad: bfloat16 [1024, 8192], P('row', 'col'), may hold values from -6 to 6
- gate_weight: bfloat16 [8192, 14336], P('col', 'row'), may hold values from -0.0625 to 0.0625
- up_weight: bfloat16 [8192, 14336], P('col', 'row'), may hold values from -0.0625 to 0.0625
- down_weight: bfloat16 [14336, 8192], P('row', 'col'), may hold values from -0.046875 to 0.046875
Outputs:
- tokens_grad: bfloat16 [1024, 8192], P('row', 'col')
- gate_grad: bfloat16 [8192, 14336], P('col', 'row')
- up_grad: bfloat16 [8192, 14336], P('col', 'row')
- down_grad: bfloat16 [14336, 8192], P('row', 'col')
All inputs are finite; a program needn't handle non-finite values.
Results may differ from a plain program's by a relative error of at most 0.005.
Values may be sent and summed in bfloat16 or wider, within the bound.
No kernel may reach another device: no remote copies, remote signals or barrier semaphores. Data moves between devices by JAX's collectives and lax.ppermute only.
A program may use at most 192 MiB of HBM per device.

v0:
```python
import jax
import jax.numpy as jnp
from jax import lax
from jax.sharding import PartitionSpec as P

contract_first = (((0,), (0,)), ((), ()))
contract_last = (((1,), (1,)), ((), ()))


def activate(sums, width):
    gate = sums[:, :width]
    upper = sums[:, width : 2 * width]
    hidden_grad = sums[:, 2 * width :]
    sig = jax.nn.sigmoid(gate)
    silu_val = gate * sig
    hidden = (silu_val * upper).astype(jnp.bfloat16)
    up_part = (hidden_grad * silu_val).astype(jnp.bfloat16)
    gate_part = (hidden_grad * upper * sig * (1.0 + gate * (1.0 - sig))).astype(jnp.bfloat16)
    return (hidden, gate_part, up_part)


def local(tokens, out_grad, gate_weight, up_weight, down_weight):
    x_rows, y_rows = (
        lax.all_gather(tokens, "row", axis=0, tiled=True),
        lax.all_gather(out_grad, "row", axis=0, tiled=True),
    )
    width = gate_weight.shape[1]
    both = jnp.concatenate([gate_weight, up_weight], axis=1)
    x_part = x_rows
    y_part = y_rows
    forward = jnp.dot(x_part, both, preferred_element_type=jnp.float32)
    backward = lax.dot_general(
        y_part, down_weight, contract_last, preferred_element_type=jnp.float32
    )
    sums = lax.psum_scatter(
        jnp.concatenate([forward, backward], axis=1), "col", scatter_dimension=0, tiled=True
    )
    hidden, gate_part, up_part = activate(sums, width)
    hid_piece = lax.all_gather(hidden, "col", axis=0, tiled=True)
    gate_piece = lax.all_gather(gate_part, "col", axis=0, tiled=True)
    up_piece = lax.all_gather(up_part, "col", axis=0, tiled=True)
    x_part = x_rows
    y_part = y_rows
    pair_piece = jnp.concatenate([gate_piece, up_piece], axis=1)
    down_sum = lax.dot_general(
        hid_piece, y_part, contract_first, preferred_element_type=jnp.float32
    )
    both_sum = lax.dot_general(
        x_part, pair_piece, contract_first, preferred_element_type=jnp.float32
    )
    input_rows = lax.dot_general(
        pair_piece, both, contract_last, preferred_element_type=jnp.float32
    )
    input_part = input_rows
    down_acc, both_acc, input_part = (down_sum, both_sum, input_part)
    tokens_grad = lax.psum_scatter(input_part, "row", scatter_dimension=0, tiled=True)
    gate_grad = both_acc[:, :width].astype(jnp.bfloat16)
    up_grad = both_acc[:, width:].astype(jnp.bfloat16)
    return (tokens_grad.astype(jnp.bfloat16), gate_grad, up_grad, down_acc.astype(jnp.bfloat16))


def solution(mesh):
    placed = (P("row", "col"), P("row", "col"), P("col", "row"), P("col", "row"), P("row", "col"))
    return jax.shard_map(
        local,
        mesh=mesh,
        in_specs=placed,
        out_specs=(P("row", "col"), P("col", "row"), P("col", "row"), P("row", "col")),
        check_vma=False,
    )
```

profile of v0, /device:TPU:0, one launch (start us, length us, event | category | flops | bytes accessed | tf_op | source)
XLA Modules:
  0.0 583.9 jit_solution(3509857053795030304)
XLA Ops:
  7.2 0.7 all-gather.8.cloned.1.call-update
  8.0 0.7 all-gather.6.cloned.1.call-update
  8.7 0.0 reduce-scatter.7.cloned.1.call-start
  8.7 3.0 constant_dynamic-update-slice_fusion.1
  11.7 1.4 constant_dynamic-update-slice_fusion
  13.1 46.2 %all-gather.8.cloned.1.call-done = bf16[1024,512]{1,0:T(8,128)(2,1)} async-done(((bf16[128,512]{1,0:T(8,128)(2,1)}), bf16[1024,512]{1,0:T(8,128)(2,1)}) %all-gather.8.cloned.1.call-update) | async-done | bytes 1048592 | tf_op jit(solution)/shard_map/all_gather | solution.py:25
  59.3 6.3 %fusion.3 = f32[1024,1792]{0,1:T(8,128)} fusion(bf16[1024,512]{1,0:T(8,128)(2,1)} %all-gather.8.cloned.1.call-done, bf16[1792,512]{1,0:T(8,128)(2,1)S(1)} %copy-done), kind=kOutput, calls=%fused_computation.15 | convolution fusion | flops 1879048192 | bytes 10223616 | tf_op jit(solution)/shard_map/dot_general | solution.py:32
  65.6 41.3 %all-gather.6.cloned.1.call-done = bf16[1024,512]{1,0:T(8,128)(2,1)} async-done(((bf16[128,512]{1,0:T(8,128)(2,1)}), bf16[1024,512]{1,0:T(8,128)(2,1)}) %all-gather.6.cloned.1.call-update) | async-done | bytes 1048592 | tf_op jit(solution)/shard_map/all_gather | solution.py:24
  106.8 6.5 %convolution_bitcast_fusion = f32[1024,3584]{0,1:T(8,128)S(1)} fusion(bf16[512,3584]{1,0:T(8,128)(2,1)} %constant_dynamic-update-slice_fusion, bf16[1024,512]{1,0:T(8,128)(2,1)} %all-gather.6.cloned.1.call-done), kind=kOutput, calls=%fused_computation.1 | convolution fusion | flops 3758096384 | bytes 19398656 | tf_op jit(solution)/shard_map/dot_general | solution.py:31
  113.4 11.9 %pad_maximum_fusion = f32[1024,5376]{0,1:T(8,128)} fusion(f32[1024,1792]{0,1:T(8,128)S(1)} %copy-done.2, f32[1024,3584]{0,1:T(8,128)S(1)} %convolution_bitcast_fusion), kind=kLoop, calls=%fused_computation | loop fusion | flops 5505024 | bytes 44040192 | tf_op jit(solution)/shard_map/concatenate | solution.py:36
  125.3 21.8 %copy.25 = f32[1024,5376]{1,0:T(8,128)} copy(f32[1024,5376]{0,1:T(8,128)} %pad_maximum_fusion) | data formatting | bytes 44040192
  147.1 0.0 all-gather.10.cloned.1.call-start
  147.2 234.0 %reduce-scatter.7.cloned.1.call-done = f32[64,5376]{1,0:T(8,128)} async-done(((f32[1024,5376]{1,0:T(8,128)}), f32[64,5376]{1,0:T(8,128)}) %reduce-scatter.7.cloned.1.call-update) | async-done | bytes 1376272 | tf_op jit(solution)/shard_map/reduce_scatter | solution.py:35
  381.2 2.3 multiply_convert_fusion
  383.6 0.0 all-gather.12.cloned.1.call-start
  383.6 0.5 all-gather.12.cloned.1.call-update
  384.2 0.0 all-gather.14.cloned.1.call-start
  384.2 0.5 all-gather.14.cloned.1.call-update
  384.7 0.2 reduce-scatter.5.cloned.1.call-start
  385.0 34.3 %all-gather.10.cloned.1.call-done = bf16[1024,1792]{1,0:T(8,128)(2,1)} async-done(((bf16[64,1792]{1,0:T(8,128)(2,1)}), bf16[1024,1792]{1,0:T(8,128)(2,1)}) %all-gather.10.cloned.1.call-update) | async-done | bytes 3670032 | tf_op jit(solution)/shard_map/all_gather | solution.py:40
  419.2 4.2 constant_dynamic-update-slice_fusion.3
  423.4 34.8 %all-gather.12.cloned.1.call-done = bf16[1024,1792]{1,0:T(8,128)(2,1)} async-done(((bf16[64,1792]{1,0:T(8,128)(2,1)}), bf16[1024,1792]{1,0:T(8,128)(2,1)}) %all-gather.12.cloned.1.call-update) | async-done | bytes 3670032 | tf_op jit(solution)/shard_map/all_gather | solution.py:41
  458.2 4.1 constant_dynamic-update-slice_fusion.2
  462.3 9.6 %fusion.4 = f32[1024,512]{1,0:T(8,128)} fusion(bf16[1024,3584]{1,0:T(8,128)(2,1)} %constant_dynamic-update-slice_fusion.2, bf16[512,3584]{1,0:T(8,128)(2,1)} %constant_dynamic-update-slice_fusion), kind=kOutput, calls=%fused_computation.16 | convolution fusion | flops 3758096384 | bytes 13107200 | tf_op jit(solution)/shard_map/dot_general | solution.py:51
  472.0 7.5 %fusion = bf16[512,3584]{0,1:T(8,128)(2,1)S(1)} fusion(bf16[1024,3584]{1,0:T(8,128)(2,1)} %constant_dynamic-update-slice_fusion.2, bf16[1024,512]{1,0:T(8,128)(2,1)S(1)} %copy-done.5), kind=kOutput, calls=%fused_computation.3 | convolution fusion | flops 3759931392 | bytes 12058624 | tf_op jit(solution)/shard_map/dot_general | solution.py:48
  479.5 1.5 fusion.2
  481.0 2.4 copy.23
  483.3 3.9 copy.22
  487.3 9.2 %all-gather.14.cloned.1.call-done = bf16[1024,1792]{1,0:T(8,128)(2,1)} async-done(((bf16[64,1792]{1,0:T(8,128)(2,1)}), bf16[1024,1792]{1,0:T(8,128)(2,1)}) %all-gather.14.cloned.1.call-update) | async-done | bytes 3670032 | tf_op jit(solution)/shard_map/all_gather | solution.py:39
  496.5 5.4 convolution_convert_fusion.1
  501.8 73.6 %reduce-scatter.5.cloned.1.call-done = f32[128,512]{1,0:T(8,128)} async-done(((f32[1024,512]{1,0:T(8,128)}), f32[128,512]{1,0:T(8,128)}) %reduce-scatter.5.cloned.1.call-update) | async-done | bytes 262160 | tf_op jit(solution)/shard_map/reduce_scatter | solution.py:56
  575.4 1.6 convert_element_type.19
  (17 shorter events, 0.2 us)
Async XLA Ops:
  7.2 52.1 %copy-start = (bf16[1792,512]{1,0:T(8,128)(2,1)S(1)}, bf16[1792,512]{1,0:T(8,128)(2,1)}, u32[]{:S(2)}) copy-start(bf16[1792,512]{1,0:T(8,128)(2,1)} %param.9) | copy-start | bytes 5505028
  7.2 52.1 %all-gather.8.cloned.1.call-start = ((), (), s32[]{:S(2)}) async-start(), calls=%async_computation.3 | async-start | bytes 1179648 | tf_op jit(solution)/shard_map/all_gather | solution.py:25
  7.9 98.9 %all-gather.6.cloned.1.call-start = ((), (), s32[]{:S(2)}) async-start(), calls=%async_computation.2 | async-start | bytes 1179648 | tf_op jit(solution)/shard_map/all_gather | solution.py:24
  8.7 372.6 %reduce-scatter.7.cloned.1.call-start = ((), (), s32[]{:S(2)}) async-start(), calls=%async_computation.8 | async-start | bytes 23396352 | tf_op jit(solution)/shard_map/reduce_scatter | solution.py:35
  8.7 3.0 copy-start.3
  106.8 6.5 %copy-start.2 = (f32[1024,1792]{0,1:T(8,128)S(1)}, f32[1024,1792]{0,1:T(8,128)}, u32[]{:S(2)}) copy-start(f32[1024,1792]{0,1:T(8,128)} %fusion.3) | copy-start | bytes 22020100
  147.1 272.1 %all-gather.10.cloned.1.call-start = ((), (), s32[]{:S(2)}) async-start(), calls=%async_computation.4 | async-start | bytes 3899392 | tf_op jit(solution)/shard_map/all_gather | solution.py:40
  383.6 74.6 %all-gather.12.cloned.1.call-start = ((), (), s32[]{:S(2)}) async-start(), calls=%async_computation.5 | async-start | bytes 3899392 | tf_op jit(solution)/shard_map/all_gather | solution.py:41
  384.2 112.3 %all-gather.14.cloned.1.call-start = ((), (), s32[]{:S(2)}) async-start(), calls=%async_computation.7 | async-start | bytes 3899392 | tf_op jit(solution)/shard_map/all_gather | solution.py:39
  384.7 190.7 %reduce-scatter.5.cloned.1.call-start = ((), (), s32[]{:S(2)}) async-start(), calls=%async_computation.6 | async-start | bytes 2359296 | tf_op jit(solution)/shard_map/reduce_scatter | solution.py:56
  462.3 9.6 %copy-start.5 = (bf16[1024,512]{1,0:T(8,128)(2,1)S(1)}, bf16[1024,512]{1,0:T(8,128)(2,1)}, u32[]{:S(2)}) copy-start(bf16[1024,512]{1,0:T(8,128)(2,1)} %all-gather.6.cloned.1.call-done) | copy-start | bytes 3145732
  481.0 15.5 %copy-start.4 = (bf16[1024,512]{1,0:T(8,128)(2,1)S(1)}, bf16[1024,512]{1,0:T(8,128)(2,1)}, u32[]{:S(2)}) copy-start(bf16[1024,512]{1,0:T(8,128)(2,1)} %all-gather.8.cloned.1.call-done) | copy-start | bytes 3145732
  483.3 93.7 %copy-start.1 = (bf16[1792,512]{1,0:T(8,128)(2,1)S(1)}, bf16[1792,512]{1,0:T(8,128)(2,1)}, u32[]{:S(2)}) copy-start(bf16[1792,512]{1,0:T(8,128)(2,1)} %param.9) | copy-start | bytes 5505028
Sparse Core Ops, SparseCore 0:
  10.4 48.8 all-gather.7
  61.6 45.1 all-gather.5
  147.3 233.9 reduce-scatter.6
  383.7 35.4 all-gather.9
  421.4 36.7 all-gather.11
  459.7 36.7 all-gather.13
  500.2 75.1 reduce-scatter.4
where the time goes:
time: 585 us; the launch traced here: 584 us
  waiting for transfers between devices  476 us (81%)
  local copies, waits for them, and re-layouts  42.3 us (7%)
  matrix products  35.3 us (6%)
  other arithmetic  15.9 us (3%)
  between operations  14.2 us (2%)
    reduce_scatter x1, waiting for transfers between devices, local(): lax.psum_scatter(jnp.concatenate([forward, backward], axis=1), 'col', sca...  234 us
    reduce_scatter x1, waiting for transfers between devices, local(): lax.psum_scatter(input_part, 'row', scatter_dimension=0, tiled=True)  73.6 us
    all_gather x1, waiting for transfers between devices, local(): lax.all_gather(out_grad, 'row', axis=0, tiled=True)  46.2 us
    all_gather x1, waiting for transfers between devices, local(): lax.all_gather(tokens, 'row', axis=0, tiled=True)  41.3 us
    unnamed x17, local copies, waits for them, and re-layouts  35.3 us
    all_gather x1, waiting for transfers between devices, local(): up_piece = lax.all_gather(up_part, 'col', axis=0, tiled=True)  34.8 us
    all_gather x1, waiting for transfers between devices, local(): gate_piece = lax.all_gather(gate_part, 'col', axis=0, tiled=True)  34.3 us
    concatenate x1, other arithmetic, local(): jnp.concatenate([forward, backward], axis=1)  11.9 us
  transfers between devices with their start and end apart: 7, of which 7 were waited for; matrix products, arithmetic and copies ran while one was open for 8% of the time, Pallas kernels for 0%

commit v1 on v0

v1 whole, which is shorter than its diff:
```python
import jax
import jax.numpy as jnp
from jax import lax
from jax.experimental import pallas as pl
from jax.experimental.pallas import tpu as pltpu
from jax.sharding import Mesh
from jax.sharding import PartitionSpec as P

AXES = {"z": 4, "xh": 2, "y": 4, "xl": 2, "core": 2}
LANE = 128
contract_first = (((0,), (0,)), ((), ()))
contract_last = (((1,), (1,)), ((), ()))
f32 = jnp.float32
bf16 = jnp.bfloat16


def move(a, axis, by):
    n = AXES[axis]
    return lax.ppermute(a, axis, [(i, (i + by) % n) for i in range(n)])


def move2(a, dz, dx):
    pairs = [(z * 2 + x, ((z + dz) % 4) * 2 + (x + dx) % 2) for z in range(4) for x in range(2)]
    return lax.ppermute(a, ("z", "xh"), pairs)


def dot(a, b, dims):
    return lax.dot_general(a, b, dims, preferred_element_type=f32)


plain = (((1,), (0,)), ((), ()))


def forward_kernel(own, oth, gu_own, gu_oth, d_own, d_oth, keep, second, plus, minus):
    half = own.shape[1] // 2
    gu = dot(own[:, :half], gu_own[...], plain) + dot(oth[:, :half], gu_oth[...], plain)
    hg = dot(own[:, half:], d_own[...], contract_last) + dot(oth[:, half:], d_oth[...], contract_last)
    for part, cols in ((gu, slice(0, 2 * LANE)), (hg, slice(2 * LANE, 3 * LANE))):
        keep[:, cols] = part[0:64]
        second[0:32, cols] = part[64:96]
        second[32:64, cols] = part[224:256]
        plus[:, cols] = part[96:160].astype(bf16)
        minus[:, cols] = part[160:224].astype(bf16)


def forward(own, oth, gu_own, gu_oth, d_own, d_oth):
    rows, both = own.shape
    depth = both // 2
    tiles = d_own.shape[0] // LANE
    wide = 3 * LANE * tiles
    whole = pl.BlockSpec((rows, both), lambda t: (0, 0))
    gu = pl.BlockSpec((depth, 2 * LANE), lambda t: (0, t))
    d = pl.BlockSpec((LANE, depth), lambda t: (t, 0))
    out = pl.BlockSpec((64, 3 * LANE), lambda t: (0, t))
    return pl.pallas_call(
        forward_kernel,
        grid=(tiles,),
        in_specs=[whole, whole, gu, gu, d, d],
        out_specs=[out] * 4,
        out_shape=[
            jax.ShapeDtypeStruct((64, wide), f32),
            jax.ShapeDtypeStruct((64, wide), f32),
            jax.ShapeDtypeStruct((64, wide), bf16),
            jax.ShapeDtypeStruct((64, wide), bf16),
        ],
        cost_estimate=pl.CostEstimate(
            flops=2 * rows * 2 * depth * wide, bytes_accessed=4 * depth * wide, transcendentals=0
        ),
        compiler_params=pltpu.CompilerParams(vmem_limit_bytes=24 << 20),
        name="forward",
    )(own, oth, gu_own, gu_oth, d_own, d_oth)


def activate_kernel(keep, minus, second, across, out):
    tiles = out.shape[1] // (3 * LANE)
    for t in range(tiles):
        def total(j):
            cols = slice((3 * t + j) * LANE, (3 * t + j + 1) * LANE)
            return (
                keep[0:32, cols]
                + minus[32:64, cols].astype(f32)
                + second[:, cols].astype(f32)
                + across[:, cols]
            )

        gate, upper, hidden_grad = total(0), total(1), total(2)
        sig = jax.nn.sigmoid(gate)
        silu = gate * sig
        base = 3 * t * LANE
        out[:, base : base + LANE] = (silu * upper).astype(bf16)
        out[:, base + LANE : base + 2 * LANE] = (
            hidden_grad * upper * sig * (1.0 + gate * (1.0 - sig))
        ).astype(bf16)
        out[:, base + 2 * LANE : base + 3 * LANE] = (hidden_grad * silu).astype(bf16)


def activate(keep, minus, second, across):
    return pl.pallas_call(
        activate_kernel,
        out_shape=jax.ShapeDtypeStruct(second.shape, bf16),
        cost_estimate=pl.CostEstimate(flops=2000000, bytes_accessed=1500000, transcendentals=30000),
        compiler_params=pltpu.CompilerParams(vmem_limit_bytes=8 << 20),
        name="activate",
    )(keep, minus, second, across)


def ordered(core, mine, other, j):
    cols = slice(j * LANE, (j + 1) * LANE)
    a, b = mine[:, cols], other[:, cols]
    first = core == 0
    return jnp.concatenate([jnp.where(first, a, b), jnp.where(first, b, a)], axis=1)


def back_kernel(core, mine, other, wg, wu, near, far, total):
    t = pl.program_id(0)

    @pl.when(t == 0)
    def _():
        total[...] = jnp.zeros_like(total)

    c = core[0]
    total[...] += dot(ordered(c, mine, other, 1), wg[...], contract_last) + dot(
        ordered(c, mine, other, 2), wu[...], contract_last
    )

    @pl.when(t == pl.num_programs(0) - 1)
    def _():
        for b in range(8):
            near[16 * b : 16 * b + 16, :] = total[32 * b : 32 * b + 16, :].astype(near.dtype)
            far[16 * b : 16 * b + 16, :] = total[32 * b + 16 : 32 * b + 32, :].astype(far.dtype)


def back(core, mine, other, wg, wu, near_type):
    rows, wide = mine.shape
    depth = wg.shape[0]
    tiles = wide // (3 * LANE)
    act = pl.BlockSpec((rows, 3 * LANE), lambda t: (0, t))
    weight = pl.BlockSpec((depth, 2 * LANE), lambda t: (0, t))
    out = pl.BlockSpec((rows // 2, depth), lambda t: (0, 0))
    return pl.pallas_call(
        back_kernel,
        grid=(tiles,),
        in_specs=[pl.BlockSpec(memory_space=pltpu.SMEM), act, act, weight, weight],
        out_specs=[out, out],
        out_shape=[
            jax.ShapeDtypeStruct((rows // 2, depth), near_type),
            jax.ShapeDtypeStruct((rows // 2, depth), bf16),
        ],
        scratch_shapes=[pltpu.VMEM((rows, depth), f32)],
        cost_estimate=pl.CostEstimate(
            flops=8 * rows * depth * tiles * 2 * LANE, bytes_accessed=8 * depth * tiles * LANE, transcendentals=0
        ),
        compiler_params=pltpu.CompilerParams(vmem_limit_bytes=24 << 20),
        name="back",
    )(core, mine, other, wg, wu)


def weights_kernel(core, *refs):
    mine, other, turned, direct = refs[0:4], refs[4:8], refs[8:12], refs[12:16]
    gate_out, up_out, down_out = refs[16:]
    c = core[0]
    half = direct[0].shape[1] // 2
    both = down = None
    for m, o, xt, xg in zip(mine, other, turned, direct):
        pair = jnp.concatenate([ordered(c, m, o, 1), ordered(c, m, o, 2)], axis=1)
        first = dot(xt[:half, :], pair, plain)
        second = dot(ordered(c, m, o, 0), xg[:, half:], contract_first)
        both = first if both is None else both + first
        down = second if down is None else down + second
    gate_out[...] = both[:, : 2 * LANE].astype(bf16)
    up_out[...] = both[:, 2 * LANE :].astype(bf16)
    down_out[...] = down.astype(bf16)


def weight_grads(core, mine, other, turned, direct):
    rows, wide = mine[0].shape
    depth = direct[0].shape[1] // 2
    tiles = wide // (3 * LANE)
    act = pl.BlockSpec((rows, 3 * LANE), lambda t: (0, t))
    return pl.pallas_call(
        weights_kernel,
        grid=(tiles,),
        in_specs=[pl.BlockSpec(memory_space=pltpu.SMEM)]
        + [act] * 8
        + [pl.BlockSpec(turned[0].shape, lambda t: (0, 0))] * 4
        + [pl.BlockSpec(direct[0].shape, lambda t: (0, 0))] * 4,
        out_specs=[
            pl.BlockSpec((depth, 2 * LANE), lambda t: (0, t)),
            pl.BlockSpec((depth, 2 * LANE), lambda t: (0, t)),
            pl.BlockSpec((2 * LANE, depth), lambda t: (t, 0)),
        ],
        out_shape=[
            jax.ShapeDtypeStruct((depth, tiles * 2 * LANE), bf16),
            jax.ShapeDtypeStruct((depth, tiles * 2 * LANE), bf16),
            jax.ShapeDtypeStruct((tiles * 2 * LANE, depth), bf16),
        ],
        cost_estimate=pl.CostEstimate(
            flops=6 * 4 * rows * depth * tiles * 2 * LANE, bytes_accessed=18000000, transcendentals=0
        ),
        compiler_params=pltpu.CompilerParams(vmem_limit_bytes=40 << 20),
        name="weight_grads",
    )(core, *mine, *other, *turned, *direct)


def local(tokens, out_grad, gate_weight, up_weight, down_weight):
    core = lax.axis_index("core")
    y = lax.axis_index("y")
    xl = lax.axis_index("xl")
    core_ref = jnp.full((1,), core, jnp.int32)
    depth, wide = gate_weight.shape
    tiles = wide // (2 * LANE)

    rows = jnp.concatenate([tokens, out_grad], axis=1)
    width = rows.shape[1]
    rows = rows.reshape(4, 2, 16, width)
    rows = lax.dynamic_slice_in_dim(jnp.concatenate([rows, rows], axis=0), y, 4, axis=0)
    rows = jnp.where(xl == 0, rows, rows[:, ::-1]).reshape(128, width)
    partner = move(rows, "xh", 1)
    pair = jnp.stack([rows.reshape(8, 16, width), partner.reshape(8, 16, width)], axis=1).reshape(256, width)

    def columns(at):
        g = lax.dynamic_index_in_dim(gate_weight.reshape(depth, tiles, 2, LANE), at, 2, keepdims=False)
        u = lax.dynamic_index_in_dim(up_weight.reshape(depth, tiles, 2, LANE), at, 2, keepdims=False)
        d = lax.dynamic_index_in_dim(down_weight.reshape(tiles, 2, LANE, depth), at, 1, keepdims=False)
        return jnp.concatenate([g, u], axis=2).reshape(depth, wide), d.reshape(tiles * LANE, depth)

    gu_own, d_own = columns(core)
    gu_send, d_send = columns(1 - core)
    gu_oth = move(gu_send, "core", 1)
    d_oth = move(d_send, "core", 1)

    pairs = [pair] + [move(pair, "z", by) for by in (3, 1, 2)]
    where = (0, 1, 3, 2)
    others = [move(p, "core", 1) for p in pairs]
    turned = [p.T for p in pairs]

    mine, other, near, far = [], [], [], []
    for k in range(4):
        keep, second, plus, minus = forward(pairs[k], others[k], gu_own, gu_oth, d_own, d_oth)
        from_low = move(plus, "y", 1)
        from_high = move(minus, "y", 3)
        up_sum = (second[0:32] + from_low[32:64].astype(f32)).astype(bf16)
        down_sum = (second[32:64] + from_high[0:32].astype(f32)).astype(bf16)
        second_low = move(up_sum, "y", 1)
        second_high = move(down_sum, "y", 3)
        beside = keep[32:64] + from_low[0:32].astype(f32) + second_high.astype(f32)
        across = move(beside, "xl", 1)
        own = activate(keep, from_high, second_low, across)
        b0 = own
        b1 = move(own, "xl", 1)
        b6 = move(own, "y", 1)
        b2 = move(own, "y", 3)
        b7 = move(b1, "y", 1)
        b3 = move(b1, "y", 3)
        b4 = move(b6, "y", 1)
        b5 = move(b3, "y", 3)
        whole = jnp.concatenate([b0, b1, b2, b3, b4, b5, b6, b7], axis=0)
        mine.append(whole)
        other.append(move(whole, "core", 1))
        n, f = back(core_ref, mine[k], other[k], gate_weight, up_weight, f32 if k == 0 else bf16)
        near.append(n if k == 0 else move(n, "z", where[k]))
        far.append(move2(f, where[k], 1))

    gate_grad, up_grad, down_grad = weight_grads(core_ref, mine, other, turned, pairs)
    total = near[0]
    for part in near[1:] + far:
        total = total + part.astype(f32)
    total = total.astype(bf16).reshape(4, 2, 16, depth)
    total = jnp.where(xl == 0, total, total[:, ::-1])
    total = lax.dynamic_slice_in_dim(jnp.concatenate([total, total], axis=0), (4 - y) % 4, 4, axis=0)
    return total.reshape(128, depth), gate_grad, up_grad, down_grad


def solution(mesh):
    fine = Mesh(mesh.devices.reshape(tuple(AXES.values())), tuple(AXES))
    row, col = ("z", "xh"), ("y", "xl", "core")
    placed = (P(row, col), P(row, col), P(col, row), P(col, row), P(row, col))
    return jax.shard_map(
        local,
        mesh=fine,
        in_specs=placed,
        out_specs=(P(row, col), P(col, row), P(col, row), P(row, col)),
        check_vma=False,
    )
```

time: 585 us -> 321 us (0.55)
  waiting for transfers between devices: 476 us -> 108 us
  starting transfers between devices: 0.45 us -> 86.7 us
  Pallas kernels: 0 us -> 59.8 us
  matrix products: 35.3 us -> 0 us
  local copies, waits for them, and re-layouts: 42.3 us -> 59.1 us
  between operations: 14.2 us -> 1.15 us
  other arithmetic: 15.9 us -> 4.67 us
    reduce_scatter x2 -> x0, waiting for transfers between devices: 308 us -> none  [the longest x1 234 us: local(): lax.psum_scatter(jnp.concatenate([forward, backward], axis=1), 'col', sca...]
    all_gather x5 -> x0, waiting for transfers between devices: 166 us -> none  [the longest x1 46.2 us: local(): lax.all_gather(out_grad, 'row', axis=0, tiled=True)]
    ppermute x0 -> x69, waiting for transfers between devices: none -> 108 us  [the longest x65 108 us: move(): return lax.ppermute(a, axis, [(i, (i + by) % n) for i in range(n)])]
    ppermute x0 -> x69, starting transfers between devices: none -> 86.7 us  [the longest x65 77.2 us: move(): return lax.ppermute(a, axis, [(i, (i + by) % n) for i in range(n)])]
    pallas_call x0 -> x13, Pallas kernels: none -> 59.8 us  [the longest x4 25.1 us: forward(): pl.pallas_call(forward_kernel, grid=(tiles,), in_specs=[whole, whole, gu,...]
    dot_general x5 -> x0, matrix products: 35.3 us -> none  [the longest x1 9.62 us: local(): lax.dot_general(pair_piece, both, contract_last, preferred_element_type=j...]
    dynamic_slice x0 -> x6, local copies, waits for them, and re-layouts: none -> 10.7 us  [the longest x3 6.15 us: columns(): lax.dynamic_index_in_dim(up_weight.reshape(depth, tiles, 2, LANE), at, 2,...]
    concatenate x1 -> x5, other arithmetic: 11.9 us -> 3.89 us  [the longest x2 3.04 us: columns(): jnp.concatenate([g, u], axis=2).reshape(depth, wide)]
  transfers between devices with their start and end apart: 7 -> 69, of which waited for: 7 -> 25; matrix products, arithmetic and copies ran while one was open for 8% -> 13% of each run, Pallas kernels for 0% -> 19%
where the time goes in v1:
time: 321 us; the launch traced here: 319 us
  waiting for transfers between devices  108 us (34%)
  starting transfers between devices  86.7 us (27%)
  Pallas kernels  59.8 us (19%)
  local copies, waits for them, and re-layouts  59.1 us (18%)
  other arithmetic  4.67 us (1%)
    ppermute x65, waiting for transfers between devices, move(): return lax.ppermute(a, axis, [(i, (i + by) % n) for i in range(n)])  108 us
    ppermute x65, starting transfers between devices, move(): return lax.ppermute(a, axis, [(i, (i + by) % n) for i in range(n)])  77.2 us
    unnamed x52, local copies, waits for them, and re-layouts  28.8 us
    pallas_call x4, Pallas kernels, forward(): pl.pallas_call(forward_kernel, grid=(tiles,), in_specs=[whole, whole, gu,...  25.1 us
    pallas_call x4, Pallas kernels, back(): pl.pallas_call(back_kernel, grid=(tiles,), in_specs=[pl.BlockSpec(memory_...  22.3 us
    pallas_call x1, Pallas kernels, weight_grads(): pl.pallas_call(weights_kernel, grid=(tiles,), in_specs=[pl.BlockSpec(memo...  11.9 us
    ppermute x4, starting transfers between devices, move2(): return lax.ppermute(a, ('z', 'xh'), pairs)  9.53 us
    reshape x2, local copies, waits for them, and re-layouts, columns(): jnp.concatenate([g, u], axis=2).reshape(depth, wide)  6.61 us
  transfers between devices with their start and end apart: 69, of which 25 were waited for; matrix products, arithmetic and copies ran while one was open for 13% of the time, Pallas kernels for 19%

profile of v1, /device:TPU:0, one launch (start us, length us, event | category | flops | bytes accessed | tf_op | source)
XLA Modules:
  0.0 319.0 jit_solution(14579749579180087657)
XLA Ops:
  0.6 4.0 %copy.28 = bf16[512,1792]{0,1:T(8,128)(2,1)} copy(bf16[512,1792]{1,0:T(8,128)(2,1)} %wg.7) | data formatting | bytes 3670016 | tf_op args[2]
  6.9 3.6 %constant_dynamic-slice_fusion.2 = (bf16[512,7,1,128]{0,3,2,1:T(8,128)(2,1)S(1)}, bf16[512,7,1,128]{0,3,2,1:T(8,128)(2,1)}, bf16[512,7,1,128]{0,3,2,1:T(8,128)(2,1)}, bf16[512,7,1,128]{0,3,2,1:T(8,128)(2,1)S(1)}) fusion(bf16[512,7,2,128]{0,3,2,1:T(8,128)(2,1)} %bitcast.42, s32[]{:T(128)S(6)} %select_n.46, s32[]{:T(128)S(6)} %select_n.45, ...), kind=kLoop, calls=%fused_computation.59 | loop fusion | bytes 7340040 | tf_op jit(solution)/shard_map/jit(dynamic_index_in_dim)/dynamic_slice | solution.py:223
  16.1 3.8 %copy.36 = bf16[512,1792]{1,0:T(8,128)(2,1)} copy(bf16[512,1792]{0,1:T(8,128)(2,1)} %bitcast.39) | data formatting | bytes 3670016 | tf_op jit(solution)/shard_map/reshape | solution.py:225
  23.4 7.1 %collective-permute-done = bf16[128,1024]{1,0:T(8,128)(2,1)S(1)} collective-permute-done((bf16[128,1024]{1,0:T(8,128)(2,1)S(1)}, bf16[128,1024]{1,0:T(8,128)(2,1)S(1)}, u32[]{:S(2)}, u32[]{:S(2)}) %collective-permute-start) | collective-permute-done | bytes 262176 | tf_op jit(solution)/shard_map/ppermute | solution.py:19
  33.8 4.1 %collective-permute-start.17 = (bf16[256,1024]{1,0:T(8,128)(2,1)S(1)}, bf16[256,1024]{1,0:T(8,128)(2,1)}, u32[]{:S(2)}, u32[]{:S(2)}) collective-permute-start(bf16[256,1024]{1,0:T(8,128)(2,1)S(1)} %bitcast.33), channel_id=1, source_target_pairs={{0,96},{32,0},{64,32},{96,64},{1,97},{33,1},{65,33},{97,65},{2,98}... | collective-permute-start | bytes 1572872 | tf_op jit(solution)/shard_map/ppermute | solution.py:19
  40.6 19.9 %collective-permute-done.17.own.refs_13_ = bf16[256,1024]{1,0:T(8,128)(2,1)} collective-permute-done((bf16[256,1024]{1,0:T(8,128)(2,1)S(1)}, bf16[256,1024]{1,0:T(8,128)(2,1)}, u32[]{:S(2)}, u32[]{:S(2)}) %collective-permute-start.17) | collective-permute-done | bytes 524320 | tf_op jit(solution)/shard_map/ppermute | solution.py:19
  60.5 3.5 %collective-permute-done.33.own.refs_14_ = bf16[256,1024]{1,0:T(8,128)(2,1)} collective-permute-done((bf16[256,1024]{1,0:T(8,128)(2,1)S(1)}, bf16[256,1024]{1,0:T(8,128)(2,1)}, u32[]{:S(2)}, u32[]{:S(2)}) %collective-permute-start.33) | collective-permute-done | bytes 524320 | tf_op jit(solution)/shard_map/ppermute | solution.py:19
  74.9 6.0 %forward.4 = (f32[64,2688]{1,0:T(8,128)S(1)}, f32[64,2688]{1,0:T(8,128)S(1)}, bf16[64,2688]{1,0:T(8,128)(2,1)S(1)}, bf16[64,2688]{1,0:T(8,128)(2,1)S(1)}) custom-call(bf16[256,1024]{1,0:T(8,128)(2,1)S(1)} %bitcast.36, bf16[256,1024]{1,0:T(8,128)(2,1)S(1)} %copy-done.4, bf16[512,1792]{1,0:T(8,128)(2,1)S(1)} %copy.39.gu_own, ...), custom_call_target="tpu_custom_call" | custom-call | flops 1409286144 | bytes 5505024 | tf_op jit(solution)/shard_map/forward/pallas_call | solution.py:55
  84.0 6.4 %forward.5 = (f32[64,2688]{1,0:T(8,128)S(1)}, f32[64,2688]{1,0:T(8,128)S(1)}, bf16[64,2688]{1,0:T(8,128)(2,1)S(1)}, bf16[64,2688]{1,0:T(8,128)(2,1)S(1)}) custom-call(bf16[256,1024]{1,0:T(8,128)(2,1)} %collective-permute-done.17.own.refs_13_, bf16[256,1024]{1,0:T(8,128)(2,1)} %collective-permute-done.18.oth, bf16[512,1792]{1,0:T(8,128)(2,1)S(1)} %copy.39.gu_own, ...), custom_call_target="tpu_custom_call" | custom-call | flops 1409286144 | bytes 5505024 | tf_op jit(solution)/shard_map/forward/pallas_call | solution.py:55
  93.6 6.4 %forward.6 = (f32[64,2688]{1,0:T(8,128)S(1)}, f32[64,2688]{1,0:T(8,128)S(1)}, bf16[64,2688]{1,0:T(8,128)(2,1)S(1)}, bf16[64,2688]{1,0:T(8,128)(2,1)S(1)}) custom-call(bf16[256,1024]{1,0:T(8,128)(2,1)} %collective-permute-done.33.own.refs_14_, bf16[256,1024]{1,0:T(8,128)(2,1)} %collective-permute-done.34.oth, bf16[512,1792]{1,0:T(8,128)(2,1)S(1)} %copy.39.gu_own, ...), custom_call_target="tpu_custom_call" | custom-call | flops 1409286144 | bytes 5505024 | tf_op jit(solution)/shard_map/forward/pallas_call | solution.py:55
  100.0 3.3 %collective-permute-start.35 = (bf16[64,2688]{1,0:T(8,128)(2,1)S(1)}, bf16[64,2688]{1,0:T(8,128)(2,1)S(1)}, u32[]{:S(2)}, u32[]{:S(2)}) collective-permute-start(bf16[64,2688]{1,0:T(8,128)(2,1)S(1)} %get-tuple-element.42), channel_id=1, source_target_pairs={{0,12},{4,0},{8,4},{12,8},{1,13},{5,1},{9,5},{13,9},{2,14},{6,2},{... | collective-permute-start | bytes 1032200 | tf_op jit(solution)/shard_map/ppermute | solution.py:19
  103.3 6.4 %forward.7 = (f32[64,2688]{1,0:T(8,128)S(1)}, f32[64,2688]{1,0:T(8,128)S(1)}, bf16[64,2688]{1,0:T(8,128)(2,1)S(1)}, bf16[64,2688]{1,0:T(8,128)(2,1)S(1)}) custom-call(bf16[256,1024]{1,0:T(8,128)(2,1)} %collective-permute-done.49.own.refs_15_, bf16[256,1024]{1,0:T(8,128)(2,1)} %collective-permute-done.50.oth, bf16[512,1792]{1,0:T(8,128)(2,1)S(1)} %copy.39.gu_own, ...), custom_call_target="tpu_custom_call" | custom-call | flops 1409286144 | bytes 5505024 | tf_op jit(solution)/shard_map/forward/pallas_call | solution.py:55
  116.5 5.4 %collective-permute-done.36 = bf16[64,2688]{1,0:T(8,128)(2,1)S(1)} collective-permute-done((bf16[64,2688]{1,0:T(8,128)(2,1)S(1)}, bf16[64,2688]{1,0:T(8,128)(2,1)S(1)}, u32[]{:S(2)}, u32[]{:S(2)}) %collective-permute-start.36) | collective-permute-done | bytes 344096 | tf_op jit(solution)/shard_map/ppermute | solution.py:19
  124.1 5.2 %collective-permute-done.52 = bf16[64,2688]{1,0:T(8,128)(2,1)S(1)} collective-permute-done((bf16[64,2688]{1,0:T(8,128)(2,1)S(1)}, bf16[64,2688]{1,0:T(8,128)(2,1)S(1)}, u32[]{:S(2)}, u32[]{:S(2)}) %collective-permute-start.52) | collective-permute-done | bytes 344096 | tf_op jit(solution)/shard_map/ppermute | solution.py:19
  138.7 7.0 %collective-permute-done.8.across = f32[32,2688]{1,0:T(8,128)S(1)} collective-permute-done((f32[32,2688]{1,0:T(8,128)S(1)}, f32[32,2688]{1,0:T(8,128)S(1)}, u32[]{:S(2)}, u32[]{:S(2)}) %collective-permute-start.8) | collective-permute-done | bytes 344096 | tf_op jit(solution)/shard_map/ppermute | solution.py:19
  148.6 4.5 %collective-permute-done.23.across = f32[32,2688]{1,0:T(8,128)S(1)} collective-permute-done((f32[32,2688]{1,0:T(8,128)S(1)}, f32[32,2688]{1,0:T(8,128)S(1)}, u32[]{:S(2)}, u32[]{:S(2)}) %collective-permute-start.23) | collective-permute-done | bytes 344096 | tf_op jit(solution)/shard_map/ppermute | solution.py:19
  156.6 3.8 %collective-permute-done.39.across = f32[32,2688]{1,0:T(8,128)S(1)} collective-permute-done((f32[32,2688]{1,0:T(8,128)S(1)}, f32[32,2688]{1,0:T(8,128)S(1)}, u32[]{:S(2)}, u32[]{:S(2)}) %collective-permute-start.39) | collective-permute-done | bytes 344096 | tf_op jit(solution)/shard_map/ppermute | solution.py:19
  162.8 4.2 %collective-permute-done.55.across = f32[32,2688]{1,0:T(8,128)S(1)} collective-permute-done((f32[32,2688]{1,0:T(8,128)S(1)}, f32[32,2688]{1,0:T(8,128)S(1)}, u32[]{:S(2)}, u32[]{:S(2)}) %collective-permute-start.55) | collective-permute-done | bytes 344096 | tf_op jit(solution)/shard_map/ppermute | solution.py:19
  180.4 3.7 %collective-permute-start.57 = (bf16[32,2688]{1,0:T(8,128)(2,1)S(1)}, bf16[32,2688]{1,0:T(8,128)(2,1)S(1)}, u32[]{:S(2)}, u32[]{:S(2)}) collective-permute-start(bf16[32,2688]{1,0:T(8,128)(2,1)S(1)} %activate.7), channel_id=1, source_target_pairs={{0,12},{4,0},{8,4},{12,8},{1,13},{5,1},{9,5},{13,9},{2,14},{6,2},{... | collective-permute-start | bytes 516104 | tf_op jit(solution)/shard_map/ppermute | solution.py:19
  187.0 3.7 %collective-permute-start.11 = (bf16[32,2688]{1,0:T(8,128)(2,1)S(1)}, bf16[32,2688]{1,0:T(8,128)(2,1)S(1)}, u32[]{:S(2)}, u32[]{:S(2)}) collective-permute-start(bf16[32,2688]{1,0:T(8,128)(2,1)S(1)} %collective-permute-done.9), channel_id=1, source_target_pairs={{0,12},{4,0},{8,4},{12,8},{1,13},{5,1},{9,5},{13,9},{2,14},{6,2},{... | collective-permute-start | bytes 516104 | tf_op jit(solution)/shard_map/ppermute | solution.py:19
  194.3 7.0 %collective-permute-done.13 = bf16[32,2688]{1,0:T(8,128)(2,1)S(1)} collective-permute-done((bf16[32,2688]{1,0:T(8,128)(2,1)S(1)}, bf16[32,2688]{1,0:T(8,128)(2,1)S(1)}, u32[]{:S(2)}, u32[]{:S(2)}) %collective-permute-start.13) | collective-permute-done | bytes 172064 | tf_op jit(solution)/shard_map/ppermute | solution.py:19
  207.4 5.9 %collective-permute-done.28 = bf16[32,2688]{1,0:T(8,128)(2,1)S(1)} collective-permute-done((bf16[32,2688]{1,0:T(8,128)(2,1)S(1)}, bf16[32,2688]{1,0:T(8,128)(2,1)S(1)}, u32[]{:S(2)}, u32[]{:S(2)}) %collective-permute-start.28) | collective-permute-done | bytes 172064 | tf_op jit(solution)/shard_map/ppermute | solution.py:19
  219.6 6.4 %collective-permute-done.44 = bf16[32,2688]{1,0:T(8,128)(2,1)S(1)} collective-permute-done((bf16[32,2688]{1,0:T(8,128)(2,1)S(1)}, bf16[32,2688]{1,0:T(8,128)(2,1)S(1)}, u32[]{:S(2)}, u32[]{:S(2)}) %collective-permute-start.44) | collective-permute-done | bytes 172064 | tf_op jit(solution)/shard_map/ppermute | solution.py:19
  232.1 5.9 %collective-permute-done.60 = bf16[32,2688]{1,0:T(8,128)(2,1)S(1)} collective-permute-done((bf16[32,2688]{1,0:T(8,128)(2,1)S(1)}, bf16[32,2688]{1,0:T(8,128)(2,1)S(1)}, u32[]{:S(2)}, u32[]{:S(2)}) %collective-permute-start.60) | collective-permute-done | bytes 172064 | tf_op jit(solution)/shard_map/ppermute | solution.py:19
  249.6 3.7 %collective-permute-start.45 = (bf16[32,2688]{1,0:T(8,128)(2,1)S(1)}, bf16[32,2688]{1,0:T(8,128)(2,1)S(1)}, u32[]{:S(2)}, u32[]{:S(2)}) collective-permute-start(bf16[32,2688]{1,0:T(8,128)(2,1)S(1)} %collective-permute-done.42), channel_id=1, source_target_pairs={{0,12},{4,0},{8,4},{12,8},{1,13},{5,1},{9,5},{13,9},{2,14},{6,2},{... | collective-permute-start | bytes 516104 | tf_op jit(solution)/shard_map/ppermute | solution.py:19
  269.3 5.6 %back.4 = (f32[128,512]{1,0:T(8,128)S(1)}, bf16[128,512]{1,0:T(8,128)(2,1)S(1)}) custom-call(s32[1]{0:T(128)} %bitcast.core, bf16[256,2688]{1,0:T(8,128)(2,1)} %constant_dynamic-update-slice_fusion.mine.refs_0_, bf16[256,2688]{1,0:T(8,128)(2,1)} %collective-permute-done.16.other.refs_4_, bf16[512,1792]{1,0:T(8,128)(2,1)S(1)} %copy-done.2, ...), custom_call_target="tpu_custom_call" | custom-call | flops 1879048192 | bytes 3670016 | tf_op jit(solution)/shard_map/back/pallas_call | solution.py:140
  276.5 5.6 %back.5 = (bf16[128,512]{1,0:T(8,128)(2,1)S(1)}, bf16[128,512]{1,0:T(8,128)(2,1)S(1)}) custom-call(s32[1]{0:T(128)} %bitcast.core, bf16[256,2688]{1,0:T(8,128)(2,1)} %constant_dynamic-update-slice_fusion.8.mine.refs_1_, bf16[256,2688]{1,0:T(8,128)(2,1)} %collective-permute-done.31.other.refs_5_, bf16[512,1792]{1,0:T(8,128)(2,1)S(1)} %copy-done.2, ...), custom_call_target="tpu_custom_call" | custom-call | flops 1879048192 | bytes 3670016 | tf_op jit(solution)/shard_map/back/pallas_call | solution.py:140
  282.2 5.6 %back.6 = (bf16[128,512]{1,0:T(8,128)(2,1)S(1)}, bf16[128,512]{1,0:T(8,128)(2,1)S(1)}) custom-call(s32[1]{0:T(128)} %bitcast.core, bf16[256,2688]{1,0:T(8,128)(2,1)} %constant_dynamic-update-slice_fusion.16.mine.refs_2_, bf16[256,2688]{1,0:T(8,128)(2,1)} %collective-permute-done.47.other.refs_6_, bf16[512,1792]{1,0:T(8,128)(2,1)S(1)} %copy-done.2, ...), custom_call_target="tpu_custom_call" | custom-call | flops 1879048192 | bytes 3670016 | tf_op jit(solution)/shard_map/back/pallas_call | solution.py:140
  287.8 4.7 %collective-permute-start.48 = (bf16[128,512]{1,0:T(8,128)(2,1)S(1)}, bf16[128,512]{1,0:T(8,128)(2,1)S(1)}, u32[]{:S(2)}, u32[]{:S(2)}) collective-permute-start(bf16[128,512]{1,0:T(8,128)(2,1)S(1)} %get-tuple-element.45), channel_id=1, source_target_pairs={{0,96},{32,0},{64,32},{96,64},{1,97},{33,1},{65,33},{97,65},{2,98}... | collective-permute-start | bytes 393224 | tf_op jit(solution)/shard_map/ppermute | solution.py:19
  295.5 5.6 %back.7 = (bf16[128,512]{1,0:T(8,128)(2,1)S(1)}, bf16[128,512]{1,0:T(8,128)(2,1)S(1)}) custom-call(s32[1]{0:T(128)} %bitcast.core, bf16[256,2688]{1,0:T(8,128)(2,1)} %constant_dynamic-update-slice_fusion.24.mine.refs_3_, bf16[256,2688]{1,0:T(8,128)(2,1)} %collective-permute-done.63.other.refs_7_, bf16[512,1792]{1,0:T(8,128)(2,1)S(1)} %copy-done.2, ...), custom_call_target="tpu_custom_call" | custom-call | flops 1879048192 | bytes 3670016 | tf_op jit(solution)/shard_map/back/pallas_call | solution.py:140
  301.2 5.0 %collective-permute-start.68 = (bf16[128,512]{1,0:T(8,128)(2,1)S(1)}, bf16[128,512]{1,0:T(8,128)(2,1)S(1)}, u32[]{:S(2)}, u32[]{:S(2)}) collective-permute-start(bf16[128,512]{1,0:T(8,128)(2,1)S(1)} %get-tuple-element.54), channel_id=1, source_target_pairs={{0,80},{16,64},{32,112},{48,96},{64,16},{80,0},{96,48},{112,32},{1... | collective-permute-start | bytes 393224 | tf_op jit(solution)/shard_map/ppermute | solution.py:24
  306.1 11.9 %weight_grads.1 = (bf16[512,1792]{1,0:T(8,128)(2,1)}, bf16[512,1792]{1,0:T(8,128)(2,1)}, bf16[1792,512]{1,0:T(8,128)(2,1)}) custom-call(s32[1]{0:T(128)} %bitcast.core, bf16[256,2688]{1,0:T(8,128)(2,1)} %constant_dynamic-update-slice_fusion.mine.refs_0_, bf16[256,2688]{1,0:T(8,128)(2,1)} %constant_dynamic-update-slice_fusion.8.mine.refs_1_, ...), custom_call_target="tpu_custom_call" | custom-call | flops 5637144576 | bytes 18000000 | tf_op jit(solution)/shard_map/weight_grads/pallas_call | solution.py:180
  (206 shorter events, 133.0 us)
Async XLA Ops:
  19.9 53.9 %collective-permute-start.2 = (bf16[512,1792]{1,0:T(8,128)(2,1)}, bf16[512,1792]{1,0:T(8,128)(2,1)}, u32[]{:S(2)}, u32[]{:S(2)}) collective-permute-start(bf16[512,1792]{1,0:T(8,128)(2,1)} %copy.36), channel_id=1, source_target_pairs={{0,1},{1,0},{2,3},{3,2},{4,5},{5,4},{6,7},{7,6},{8,9},{9,8},{10,11... | collective-permute-start | bytes 5505032 | tf_op jit(solution)/shard_map/ppermute | solution.py:19
  33.3 40.6 %collective-permute-start.3 = (bf16[896,512]{1,0:T(8,128)(2,1)}, bf16[896,512]{1,0:T(8,128)(2,1)}, u32[]{:S(2)}, u32[]{:S(2)}) collective-permute-start(bf16[896,512]{1,0:T(8,128)(2,1)} %bitcast.16), channel_id=1, source_target_pairs={{0,1},{1,0},{2,3},{3,2},{4,5},{5,4},{6,7},{7,6},{8,9},{9,8},{10,11... | collective-permute-start | bytes 2752520 | tf_op jit(solution)/shard_map/ppermute | solution.py:19
  33.8 26.7 %collective-permute-start.17 = (bf16[256,1024]{1,0:T(8,128)(2,1)S(1)}, bf16[256,1024]{1,0:T(8,128)(2,1)}, u32[]{:S(2)}, u32[]{:S(2)}) collective-permute-start(bf16[256,1024]{1,0:T(8,128)(2,1)S(1)} %bitcast.33), channel_id=1, source_target_pairs={{0,96},{32,0},{64,32},{96,64},{1,97},{33,1},{65,33},{97,65},{2,98}... | collective-permute-start | bytes 1572872 | tf_op jit(solution)/shard_map/ppermute | solution.py:19
  37.9 26.1 %collective-permute-start.33 = (bf16[256,1024]{1,0:T(8,128)(2,1)S(1)}, bf16[256,1024]{1,0:T(8,128)(2,1)}, u32[]{:S(2)}, u32[]{:S(2)}) collective-permute-start(bf16[256,1024]{1,0:T(8,128)(2,1)S(1)} %bitcast.34), channel_id=1, source_target_pairs={{0,32},{32,64},{64,96},{96,0},{1,33},{33,65},{65,97},{97,1},{2,34}... | collective-permute-start | bytes 1572872 | tf_op jit(solution)/shard_map/ppermute | solution.py:19
  38.7 27.9 %collective-permute-start.49 = (bf16[256,1024]{1,0:T(8,128)(2,1)S(1)}, bf16[256,1024]{1,0:T(8,128)(2,1)}, u32[]{:S(2)}, u32[]{:S(2)}) collective-permute-start(bf16[256,1024]{1,0:T(8,128)(2,1)S(1)} %bitcast.35), channel_id=1, source_target_pairs={{0,64},{32,96},{64,0},{96,32},{1,65},{33,97},{65,1},{97,33},{2,66}... | collective-permute-start | bytes 1572872 | tf_op jit(solution)/shard_map/ppermute | solution.py:19
  60.5 23.5 %collective-permute-start.18 = (bf16[256,1024]{1,0:T(8,128)(2,1)}, bf16[256,1024]{1,0:T(8,128)(2,1)}, u32[]{:S(2)}, u32[]{:S(2)}) collective-permute-start(bf16[256,1024]{1,0:T(8,128)(2,1)} %collective-permute-done.17.own.refs_13_), channel_id=1, source_target_pairs={{0,1},{1,0},{2,3},{3,2},{4,5},{5,4},{6,7},{7,6},{8,9},{9,8},{10,11... | collective-permute-start | bytes 1572872 | tf_op jit(solution)/shard_map/ppermute | solution.py:19
  64.0 29.6 %collective-permute-start.34 = (bf16[256,1024]{1,0:T(8,128)(2,1)}, bf16[256,1024]{1,0:T(8,128)(2,1)}, u32[]{:S(2)}, u32[]{:S(2)}) collective-permute-start(bf16[256,1024]{1,0:T(8,128)(2,1)} %collective-permute-done.33.own.refs_14_), channel_id=1, source_target_pairs={{0,1},{1,0},{2,3},{3,2},{4,5},{5,4},{6,7},{7,6},{8,9},{9,8},{10,11... | collective-permute-start | bytes 1572872 | tf_op jit(solution)/shard_map/ppermute | solution.py:19
  66.6 33.4 %collective-permute-start.50 = (bf16[256,1024]{1,0:T(8,128)(2,1)}, bf16[256,1024]{1,0:T(8,128)(2,1)}, u32[]{:S(2)}, u32[]{:S(2)}) collective-permute-start(bf16[256,1024]{1,0:T(8,128)(2,1)} %collective-permute-done.49.own.refs_15_), channel_id=1, source_target_pairs={{0,1},{1,0},{2,3},{3,2},{4,5},{5,4},{6,7},{7,6},{8,9},{9,8},{10,11... | collective-permute-start | bytes 1572872 | tf_op jit(solution)/shard_map/ppermute | solution.py:19
  80.9 28.8 %collective-permute-start.4 = (bf16[64,2688]{1,0:T(8,128)(2,1)S(1)}, bf16[64,2688]{1,0:T(8,128)(2,1)S(1)}, u32[]{:S(2)}, u32[]{:S(2)}) collective-permute-start(bf16[64,2688]{1,0:T(8,128)(2,1)S(1)} %get-tuple-element.32), channel_id=1, source_target_pairs={{0,12},{4,0},{8,4},{12,8},{1,13},{5,1},{9,5},{13,9},{2,14},{6,2},{... | collective-permute-start | bytes 1032200 | tf_op jit(solution)/shard_map/ppermute | solution.py:19
  84.0 25.8 %collective-permute-start.5 = (bf16[64,2688]{1,0:T(8,128)(2,1)S(1)}, bf16[64,2688]{1,0:T(8,128)(2,1)S(1)}, u32[]{:S(2)}, u32[]{:S(2)}) collective-permute-start(bf16[64,2688]{1,0:T(8,128)(2,1)S(1)} %get-tuple-element.34), channel_id=1, source_target_pairs={{0,4},{4,8},{8,12},{12,0},{1,5},{5,9},{9,13},{13,1},{2,6},{6,10},{... | collective-permute-start | bytes 1032200 | tf_op jit(solution)/shard_map/ppermute | solution.py:19
  90.3 22.7 %collective-permute-start.19 = (bf16[64,2688]{1,0:T(8,128)(2,1)S(1)}, bf16[64,2688]{1,0:T(8,128)(2,1)S(1)}, u32[]{:S(2)}, u32[]{:S(2)}) collective-permute-start(bf16[64,2688]{1,0:T(8,128)(2,1)S(1)} %get-tuple-element.37), channel_id=1, source_target_pairs={{0,12},{4,0},{8,4},{12,8},{1,13},{5,1},{9,5},{13,9},{2,14},{6,2},{... | collective-permute-start | bytes 1032200 | tf_op jit(solution)/shard_map/ppermute | solution.py:19
  93.6 19.5 %collective-permute-start.20 = (bf16[64,2688]{1,0:T(8,128)(2,1)S(1)}, bf16[64,2688]{1,0:T(8,128)(2,1)S(1)}, u32[]{:S(2)}, u32[]{:S(2)}) collective-permute-start(bf16[64,2688]{1,0:T(8,128)(2,1)S(1)} %get-tuple-element.39), channel_id=1, source_target_pairs={{0,4},{4,8},{8,12},{12,0},{1,5},{5,9},{9,13},{13,1},{2,6},{6,10},{... | collective-permute-start | bytes 1032200 | tf_op jit(solution)/shard_map/ppermute | solution.py:19
  116.5 22.2 %collective-permute-start.6 = (bf16[32,2688]{1,0:T(8,128)(2,1)S(1)}, bf16[32,2688]{1,0:T(8,128)(2,1)S(1)}, u32[]{:S(2)}, u32[]{:S(2)}) collective-permute-start(bf16[32,2688]{1,0:T(8,128)(2,1)S(1)} %get-tuple-element.65), channel_id=1, source_target_pairs={{0,4},{4,8},{8,12},{12,0},{1,5},{5,9},{9,13},{13,1},{2,6},{6,10},{... | collective-permute-start | bytes 516104 | tf_op jit(solution)/shard_map/ppermute | solution.py:19
  122.1 26.0 %collective-permute-start.21 = (bf16[32,2688]{1,0:T(8,128)(2,1)S(1)}, bf16[32,2688]{1,0:T(8,128)(2,1)S(1)}, u32[]{:S(2)}, u32[]{:S(2)}) collective-permute-start(bf16[32,2688]{1,0:T(8,128)(2,1)S(1)} %get-tuple-element.67), channel_id=1, source_target_pairs={{0,4},{4,8},{8,12},{12,0},{1,5},{5,9},{9,13},{13,1},{2,6},{6,10},{... | collective-permute-start | bytes 516104 | tf_op jit(solution)/shard_map/ppermute | solution.py:19
  129.4 26.0 %collective-permute-start.37 = (bf16[32,2688]{1,0:T(8,128)(2,1)S(1)}, bf16[32,2688]{1,0:T(8,128)(2,1)S(1)}, u32[]{:S(2)}, u32[]{:S(2)}) collective-permute-start(bf16[32,2688]{1,0:T(8,128)(2,1)S(1)} %get-tuple-element.69), channel_id=1, source_target_pairs={{0,4},{4,8},{8,12},{12,0},{1,5},{5,9},{9,13},{13,1},{2,6},{6,10},{... | collective-permute-start | bytes 516104 | tf_op jit(solution)/shard_map/ppermute | solution.py:19
  138.6 22.7 %collective-permute-start.53 = (bf16[32,2688]{1,0:T(8,128)(2,1)S(1)}, bf16[32,2688]{1,0:T(8,128)(2,1)S(1)}, u32[]{:S(2)}, u32[]{:S(2)}) collective-permute-start(bf16[32,2688]{1,0:T(8,128)(2,1)S(1)} %get-tuple-element.71), channel_id=1, source_target_pairs={{0,4},{4,8},{8,12},{12,0},{1,5},{5,9},{9,13},{13,1},{2,6},{6,10},{... | collective-permute-start | bytes 516104 | tf_op jit(solution)/shard_map/ppermute | solution.py:19
  160.5 30.9 %collective-permute-start.12 = (bf16[32,2688]{1,0:T(8,128)(2,1)S(1)}, bf16[32,2688]{1,0:T(8,128)(2,1)S(1)}, u32[]{:S(2)}, u32[]{:S(2)}) collective-permute-start(bf16[32,2688]{1,0:T(8,128)(2,1)S(1)} %activate.4), channel_id=1, source_target_pairs={{0,4},{4,8},{8,12},{12,0},{1,5},{5,9},{9,13},{13,1},{2,6},{6,10},{... | collective-permute-start | bytes 516104 | tf_op jit(solution)/shard_map/ppermute | solution.py:19
  169.9 33.8 %collective-permute-start.27 = (bf16[32,2688]{1,0:T(8,128)(2,1)S(1)}, bf16[32,2688]{1,0:T(8,128)(2,1)S(1)}, u32[]{:S(2)}, u32[]{:S(2)}) collective-permute-start(bf16[32,2688]{1,0:T(8,128)(2,1)S(1)} %activate.5), channel_id=1, source_target_pairs={{0,4},{4,8},{8,12},{12,0},{1,5},{5,9},{9,13},{13,1},{2,6},{6,10},{... | collective-permute-start | bytes 516104 | tf_op jit(solution)/shard_map/ppermute | solution.py:19
  176.7 40.0 %collective-permute-start.43 = (bf16[32,2688]{1,0:T(8,128)(2,1)S(1)}, bf16[32,2688]{1,0:T(8,128)(2,1)S(1)}, u32[]{:S(2)}, u32[]{:S(2)}) collective-permute-start(bf16[32,2688]{1,0:T(8,128)(2,1)S(1)} %activate.6), channel_id=1, source_target_pairs={{0,4},{4,8},{8,12},{12,0},{1,5},{5,9},{9,13},{13,1},{2,6},{6,10},{... | collective-permute-start | bytes 516104 | tf_op jit(solution)/shard_map/ppermute | solution.py:19
  184.8 43.9 %collective-permute-start.59 = (bf16[32,2688]{1,0:T(8,128)(2,1)S(1)}, bf16[32,2688]{1,0:T(8,128)(2,1)S(1)}, u32[]{:S(2)}, u32[]{:S(2)}) collective-permute-start(bf16[32,2688]{1,0:T(8,128)(2,1)S(1)} %activate.7), channel_id=1, source_target_pairs={{0,4},{4,8},{8,12},{12,0},{1,5},{5,9},{9,13},{13,1},{2,6},{6,10},{... | collective-permute-start | bytes 516104 | tf_op jit(solution)/shard_map/ppermute | solution.py:19
  191.4 63.2 %collective-permute-start.15 = (bf16[32,2688]{1,0:T(8,128)(2,1)S(1)}, bf16[32,2688]{1,0:T(8,128)(2,1)S(1)}, u32[]{:S(2)}, u32[]{:S(2)}) collective-permute-start(bf16[32,2688]{1,0:T(8,128)(2,1)S(1)} %collective-permute-done.9), channel_id=1, source_target_pairs={{0,4},{4,8},{8,12},{12,0},{1,5},{5,9},{9,13},{13,1},{2,6},{6,10},{... | collective-permute-start | bytes 516104 | tf_op jit(solution)/shard_map/ppermute | solution.py:19
  203.7 51.6 %collective-permute-start.30 = (bf16[32,2688]{1,0:T(8,128)(2,1)S(1)}, bf16[32,2688]{1,0:T(8,128)(2,1)S(1)}, u32[]{:S(2)}, u32[]{:S(2)}) collective-permute-start(bf16[32,2688]{1,0:T(8,128)(2,1)S(1)} %collective-permute-done.24), channel_id=1, source_target_pairs={{0,4},{4,8},{8,12},{12,0},{1,5},{5,9},{9,13},{13,1},{2,6},{6,10},{... | collective-permute-start | bytes 516104 | tf_op jit(solution)/shard_map/ppermute | solution.py:19
  216.7 41.3 %collective-permute-start.46 = (bf16[32,2688]{1,0:T(8,128)(2,1)S(1)}, bf16[32,2688]{1,0:T(8,128)(2,1)S(1)}, u32[]{:S(2)}, u32[]{:S(2)}) collective-permute-start(bf16[32,2688]{1,0:T(8,128)(2,1)S(1)} %collective-permute-done.40), channel_id=1, source_target_pairs={{0,4},{4,8},{8,12},{12,0},{1,5},{5,9},{9,13},{13,1},{2,6},{6,10},{... | collective-permute-start | bytes 516104 | tf_op jit(solution)/shard_map/ppermute | solution.py:19
  228.7 32.7 %collective-permute-start.62 = (bf16[32,2688]{1,0:T(8,128)(2,1)S(1)}, bf16[32,2688]{1,0:T(8,128)(2,1)S(1)}, u32[]{:S(2)}, u32[]{:S(2)}) collective-permute-start(bf16[32,2688]{1,0:T(8,128)(2,1)S(1)} %collective-permute-done.56), channel_id=1, source_target_pairs={{0,4},{4,8},{8,12},{12,0},{1,5},{5,9},{9,13},{13,1},{2,6},{6,10},{... | collective-permute-start | bytes 516104 | tf_op jit(solution)/shard_map/ppermute | solution.py:19
  256.2 20.3 %collective-permute-start.31 = (bf16[256,2688]{1,0:T(8,128)(2,1)}, bf16[256,2688]{1,0:T(8,128)(2,1)}, u32[]{:S(2)}, u32[]{:S(2)}) collective-permute-start(bf16[256,2688]{1,0:T(8,128)(2,1)} %constant_dynamic-update-slice_fusion.8.mine.refs_1_), channel_id=1, source_target_pairs={{0,1},{1,0},{2,3},{3,2},{4,5},{5,4},{6,7},{7,6},{8,9},{9,8},{10,11... | collective-permute-start | bytes 4128776 | tf_op jit(solution)/shard_map/ppermute | solution.py:19
  258.6 23.6 %collective-permute-start.47 = (bf16[256,2688]{1,0:T(8,128)(2,1)}, bf16[256,2688]{1,0:T(8,128)(2,1)}, u32[]{:S(2)}, u32[]{:S(2)}) collective-permute-start(bf16[256,2688]{1,0:T(8,128)(2,1)} %constant_dynamic-update-slice_fusion.16.mine.refs_2_), channel_id=1, source_target_pairs={{0,1},{1,0},{2,3},{3,2},{4,5},{5,4},{6,7},{7,6},{8,9},{9,8},{10,11... | collective-permute-start | bytes 4128776 | tf_op jit(solution)/shard_map/ppermute | solution.py:19
  262.1 30.4 %collective-permute-start.63 = (bf16[256,2688]{1,0:T(8,128)(2,1)}, bf16[256,2688]{1,0:T(8,128)(2,1)}, u32[]{:S(2)}, u32[]{:S(2)}) collective-permute-start(bf16[256,2688]{1,0:T(8,128)(2,1)} %constant_dynamic-update-slice_fusion.24.mine.refs_3_), channel_id=1, source_target_pairs={{0,1},{1,0},{2,3},{3,2},{4,5},{5,4},{6,7},{7,6},{8,9},{9,8},{10,11... | collective-permute-start | bytes 4128776 | tf_op jit(solution)/shard_map/ppermute | solution.py:19
  274.9 26.1 %collective-permute-start.65 = (bf16[128,512]{1,0:T(8,128)(2,1)S(1)}, bf16[128,512]{1,0:T(8,128)(2,1)S(1)}, u32[]{:S(2)}, u32[]{:S(2)}) collective-permute-start(bf16[128,512]{1,0:T(8,128)(2,1)S(1)} %get-tuple-element.51), channel_id=1, source_target_pairs={{0,16},{16,0},{32,48},{48,32},{64,80},{80,64},{96,112},{112,96},{1... | collective-permute-start | bytes 393224 | tf_op jit(solution)/shard_map/ppermute | solution.py:24
  282.1 19.1 %collective-permute-start.32 = (bf16[128,512]{1,0:T(8,128)(2,1)S(1)}, bf16[128,512]{1,0:T(8,128)(2,1)S(1)}, u32[]{:S(2)}, u32[]{:S(2)}) collective-permute-start(bf16[128,512]{1,0:T(8,128)(2,1)S(1)} %get-tuple-element.40), channel_id=1, source_target_pairs={{0,32},{32,64},{64,96},{96,0},{1,33},{33,65},{65,97},{97,1},{2,34}... | collective-permute-start | bytes 393224 | tf_op jit(solution)/shard_map/ppermute | solution.py:19
  282.1 35.9 %collective-permute-start.66 = (bf16[128,512]{1,0:T(8,128)(2,1)S(1)}, bf16[128,512]{1,0:T(8,128)(2,1)S(1)}, u32[]{:S(2)}, u32[]{:S(2)}) collective-permute-start(bf16[128,512]{1,0:T(8,128)(2,1)S(1)} %get-tuple-element.52), channel_id=1, source_target_pairs={{0,48},{16,32},{32,80},{48,64},{64,112},{80,96},{96,16},{112,0},{1... | collective-permute-start | bytes 393224 | tf_op jit(solution)/shard_map/ppermute | solution.py:24
  287.8 30.2 %collective-permute-start.48 = (bf16[128,512]{1,0:T(8,128)(2,1)S(1)}, bf16[128,512]{1,0:T(8,128)(2,1)S(1)}, u32[]{:S(2)}, u32[]{:S(2)}) collective-permute-start(bf16[128,512]{1,0:T(8,128)(2,1)S(1)} %get-tuple-element.45), channel_id=1, source_target_pairs={{0,96},{32,0},{64,32},{96,64},{1,97},{33,1},{65,33},{97,65},{2,98}... | collective-permute-start | bytes 393224 | tf_op jit(solution)/shard_map/ppermute | solution.py:19
  292.6 25.5 %collective-permute-start.67 = (bf16[128,512]{1,0:T(8,128)(2,1)S(1)}, bf16[128,512]{1,0:T(8,128)(2,1)S(1)}, u32[]{:S(2)}, u32[]{:S(2)}) collective-permute-start(bf16[128,512]{1,0:T(8,128)(2,1)S(1)} %get-tuple-element.53), channel_id=1, source_target_pairs={{0,112},{16,96},{32,16},{48,0},{64,48},{80,32},{96,80},{112,64},{1... | collective-permute-start | bytes 393224 | tf_op jit(solution)/shard_map/ppermute | solution.py:24
  (48 other events, 488.0 us)

commit v2 on v0

v2 whole, which is shorter than its diff:
```python
import jax
import jax.numpy as jnp
from jax import lax
from jax.experimental import pallas as pl
from jax.experimental.pallas import tpu as pltpu
from jax.sharding import Mesh
from jax.sharding import PartitionSpec as P

AXES = {"z": 4, "xh": 2, "y": 4, "xl": 2, "core": 2}
HALF = 896
D = 512
WIDE = 3 * HALF
f32 = jnp.float32
bf16 = jnp.bfloat16
plain = (((1,), (0,)), ((), ()))
contract_first = (((0,), (0,)), ((), ()))
contract_last = (((1,), (1,)), ((), ()))
vmem = pl.BlockSpec(memory_space=pltpu.VMEM)
anywhere = pl.BlockSpec(memory_space=pl.ANY)
smem = pl.BlockSpec(memory_space=pltpu.SMEM)

AWAY = (0, 1, 2, 3)
ACROSS = f32
ORDER = (
    ("F", 0), ("C", 3), ("C", 1), ("S1", 0), ("F", 3), ("S2", 0), ("F", 1), ("C", 2),
    ("S1", 3), ("ACT", 0), ("S1", 1), ("F", 2), ("S2", 3), ("S2", 1), ("PAIR", 0), ("S1", 2),
    ("ACT", 3), ("S2", 2), ("ACT", 1), ("PAIR", 3), ("ASM", 0), ("ACT", 2), ("PAIR", 1), ("BACK", 0),
    ("ASM", 3), ("PAIR", 2), ("ASM", 1), ("BACK", 3), ("ASM", 2), ("BACK", 1), ("WG", 0), ("BACK", 2),
)


def move(a, axis, by):
    n = AXES[axis]
    return lax.ppermute(a, axis, [(i, (i + by) % n) for i in range(n)])


def move2(a, dz, dx):
    pairs = [(z * 2 + x, ((z + dz) % 4) * 2 + (x + dx) % 2) for z in range(4) for x in range(2)]
    return lax.ppermute(a, ("z", "xh"), pairs)


def step(a, by):
    pairs = [(2 * i, 2 * ((i + by) % 4)) for i in range(4)]
    pairs += [(2 * i + 1, 2 * ((i - by) % 4) + 1) for i in range(4)]
    return lax.ppermute(a, ("y", "core"), pairs)


def dot(a, b, dims):
    return lax.dot_general(a, b, dims, preferred_element_type=f32)


def call(name, body, ids, args, outs, after=(), limit=8, flops=0, scratch=(), in_space=vmem):
    n, m = len(args), len(after)

    def kernel(*refs):
        body(*refs[: 1 + n], *refs[1 + n + m :])

    size = sum(a.size * a.dtype.itemsize for a in args) + sum(
        o.size * jnp.dtype(o.dtype).itemsize for o in outs
    )
    return pl.pallas_call(
        kernel,
        in_specs=[smem] + [in_space] * n + [anywhere] * m,
        out_specs=[vmem] * len(outs),
        out_shape=outs,
        scratch_shapes=scratch,
        cost_estimate=pl.CostEstimate(flops=flops, bytes_accessed=size, transcendentals=0),
        compiler_params=pltpu.CompilerParams(vmem_limit_bytes=limit << 20),
        name=name,
    )(ids, *args, *after)


def shape(rows, cols, dtype=bf16):
    return jax.ShapeDtypeStruct((rows, cols), dtype)


def offset(ids, other=False):
    c = ids[0]
    return pl.multiple_of((1 - c if other else c) * HALF, 128)


def home(ids, b):
    core, y, xl = ids[0], ids[1], ids[2]
    at = (y + 4 + (1 - 2 * core) * (b // 2)) % 4 * 2 + (xl + b % 2) % 2
    return pl.ds(pl.multiple_of(at * 16, 16), 16)


def rows_kernel(ids, tokens, out_grad, out, sems):
    copies = []
    for b in range(8):
        rows = slice(16 * b, 16 * b + 16)
        copies.append(pltpu.make_async_copy(tokens.at[home(ids, b), :], out.at[rows, :D], sems.at[b]))
        copies.append(pltpu.make_async_copy(out_grad.at[home(ids, b), :], out.at[rows, D:], sems.at[8 + b]))
    for c in copies:
        c.start()
    for c in copies:
        c.wait()


def pair_kernel(ids, own, partner, out, turned):
    for b in range(8):
        both = jnp.concatenate([own[16 * b : 16 * b + 16, :], partner[16 * b : 16 * b + 16, :]], axis=0)
        out[32 * b : 32 * b + 32, :] = both
        t = (4 - b // 2) % 4 * 2 + b % 2
        turned[32 * t : 32 * t + 32, :] = both


def turn_kernel(ids, rows, out):
    n = rows.shape[0] // 4
    for j in range(4):
        t = (4 - j) % 4
        out[t * n : t * n + n, :] = rows[j * n : j * n + n, :]


def send_kernel(ids, wg, wu, wd, out, turn, sems):
    at = offset(ids, True)
    copies = [
        pltpu.make_async_copy(wd.at[pl.ds(at, HALF), :], turn, sems.at[0]),
        pltpu.make_async_copy(wg.at[:, pl.ds(at, HALF)], out.at[:, :HALF], sems.at[1]),
        pltpu.make_async_copy(wu.at[:, pl.ds(at, HALF)], out.at[:, HALF : 2 * HALF], sems.at[2]),
    ]
    for c in copies:
        c.start()
    copies[0].wait()
    out[:, 2 * HALF :] = turn[...].T
    copies[1].wait()
    copies[2].wait()


def send_weights(ids, wg, wu, wd, after):
    return pl.pallas_call(
        lambda *r: send_kernel(*r[:4], *r[5:]),
        in_specs=[smem] + [anywhere] * 4,
        out_specs=vmem,
        out_shape=shape(D, WIDE),
        scratch_shapes=[pltpu.VMEM((HALF, D), bf16), pltpu.SemaphoreType.DMA((3,))],
        cost_estimate=pl.CostEstimate(flops=0, bytes_accessed=6 << 20, transcendentals=0),
        compiler_params=pltpu.CompilerParams(vmem_limit_bytes=8 << 20),
        name="send_weights",
    )(ids, wg, wu, wd, after)


def forward_kernel(ids, own, oth, wg, wu, wd, wr, keep, second, far, behind):
    at = offset(ids)
    n = own.shape[0] // 4
    for j in range(3):
        cols = slice(j * HALF, (j + 1) * HALF)
        if j < 2:
            part = dot(own[:, :D], (wg, wu)[j][:, pl.ds(at, HALF)], plain) + dot(
                oth[:, :D], wr[:, cols], plain
            )
        else:
            part = dot(own[:, D:], wd[pl.ds(at, HALF), :], contract_last) + dot(
                oth[:, D:], wr[:, cols], plain
            )
        keep[:, cols] = part[0:n]
        second[:, cols] = part[n : 2 * n]
        far[:, cols] = part[2 * n : 3 * n].astype(bf16)
        behind[:, cols] = part[3 * n :].astype(bf16)


def add_kernel(ids, second, got, out):
    out[...] = (second[...] + got[...].astype(f32)).astype(bf16)


def beside_kernel(ids, keep, ahead, got, out, base):
    u = out.shape[0]
    for rows, dst in ((slice(0, u), base), (slice(u, 2 * u), out)):
        dst[...] = (keep[rows] + ahead[rows].astype(f32) + got[rows].astype(f32)).astype(dst.dtype)


def activate_kernel(ids, base, across, out):
    def total(j):
        cols = slice(j * HALF, (j + 1) * HALF)
        return base[:, cols] + across[:, cols].astype(f32)

    gate, upper, hidden_grad = total(0), total(1), total(2)
    sig = jax.nn.sigmoid(gate)
    silu = gate * sig
    out[:, :HALF] = (silu * upper).astype(bf16)
    out[:, HALF : 2 * HALF] = (hidden_grad * upper * sig * (1.0 + gate * (1.0 - sig))).astype(bf16)
    out[:, 2 * HALF :] = (hidden_grad * silu).astype(bf16)


def both_kernel(ids, a, b, out):
    out[: a.shape[0]] = a[...]
    out[a.shape[0] :] = b[...]


def whole_kernel(ids, p0, p1, p2, p3, out, turned):
    n = p0.shape[0]
    for j, (a, b) in enumerate(((p0, p0), (p1, p3), (p2, p2), (p3, p1))):
        out[n * j : n * j + n] = a[...]
        turned[n * j : n * j + n] = b[...]


def back_kernel(ids, mine, other, wg, wu, near, far):
    a, b = pl.ds(offset(ids), HALF), pl.ds(offset(ids, True), HALF)
    total = dot(mine[:, HALF : 2 * HALF], wg[:, a], contract_last)
    total += dot(mine[:, 2 * HALF :], wu[:, a], contract_last)
    total += dot(other[:, HALF : 2 * HALF], wg[:, b], contract_last)
    total += dot(other[:, 2 * HALF :], wu[:, b], contract_last)
    for k in range(8):
        near[16 * k : 16 * k + 16, :] = total[32 * k : 32 * k + 16].astype(near.dtype)
        far[16 * k : 16 * k + 16, :] = total[32 * k + 16 : 32 * k + 32].astype(far.dtype)


def weights_kernel(n, second, ids, *refs):
    parts, rows, refs = refs[:n], refs[n : 2 * n], refs[2 * n :]
    refs = refs[3:] if second else refs
    gate_out, up_out, down_out, done, gate_buf, up_buf, down_buf, sems = refs
    copies = []

    def put(src, dst, sem):
        copies.append(pltpu.make_async_copy(src, dst, sem))
        copies[-1].start()

    at = pl.ds(offset(ids, second), HALF)
    for j, (out, buf) in enumerate(((gate_out, gate_buf), (up_out, up_buf))):
        total = None
        for p, r in zip(parts, rows):
            term = dot(r[:, :D], p[:, (j + 1) * HALF : (j + 2) * HALF], contract_first)
            total = term if total is None else total + term
        buf[...] = total.astype(bf16)
        put(buf, out.at[:, at], sems.at[j])
    total = None
    for p, r in zip(parts, rows):
        term = dot(p[:, :HALF], r[:, D:], contract_first)
        total = term if total is None else total + term
    down_buf[...] = total.astype(bf16)
    put(down_buf, down_out.at[at, :], sems.at[2])
    done[...] = jnp.zeros_like(done)
    for c in copies:
        c.wait()


def weight_grads(ids, parts, rows, old, after):
    n, second = len(parts), bool(old)
    whole = [shape(D, 2 * HALF), shape(D, 2 * HALF), shape(2 * HALF, D)]

    def kernel(*refs):
        at = 1 + 2 * n + len(old)
        weights_kernel(n, second, *refs[:at], *refs[at + len(after) :])

    return pl.pallas_call(
        kernel,
        in_specs=[smem] + [vmem] * (2 * n) + [anywhere] * (len(old) + len(after)),
        out_specs=[pl.BlockSpec(memory_space=pltpu.HBM)] * 3 + [vmem],
        out_shape=whole + [shape(8, 128, f32)],
        input_output_aliases={1 + 2 * n + i: i for i in range(len(old))},
        scratch_shapes=[pltpu.VMEM((D, HALF), bf16)] * 2 + [pltpu.VMEM((HALF, D), bf16), pltpu.SemaphoreType.DMA((3,))],
        cost_estimate=pl.CostEstimate(flops=6 * 1024 * D * HALF, bytes_accessed=10 << 20, transcendentals=0),
        compiler_params=pltpu.CompilerParams(vmem_limit_bytes=24 << 20),
        name="weight_grads",
    )(ids, *parts, *rows, *old, *after)


def sum_kernel(ids, *refs):
    out = refs[-1]
    for b in range(8):
        rows = slice(16 * b, 16 * b + 16)
        total = refs[0][rows, :].astype(f32)
        for r in refs[1:-1]:
            total = total + r[rows, :].astype(f32)
        out[home(ids, b), :] = total.astype(bf16)


def local(tokens, out_grad, wg, wu, wd):
    ids = jnp.stack([lax.axis_index(a) for a in ("core", "y", "xl")]).astype(jnp.int32)

    (rows,) = call(
        "rows", rows_kernel, ids, [tokens, out_grad], [shape(128, 2 * D)],
        scratch=[pltpu.SemaphoreType.DMA((16,))], in_space=anywhere,
    )
    partner = move(rows, "xh", 1)
    wr = move(send_weights(ids, wg, wu, wd, rows), "core", 1)
    pair, turned = call("pair", pair_kernel, ids, [rows, partner], [shape(256, 2 * D)] * 2, flops=20 << 30)
    oth = {0: move(turned, "core", 1)}
    own = {0: pair, 1: move(pair, "z", 3), 3: move(pair, "z", 1), 2: move(pair, "z", 2)}

    n = len(AWAY)
    st = [{} for _ in range(n)]
    last = ()
    near, far = [], []
    for stage, k in ORDER:
        s = st[k]
        count = own[k].shape[0]
        u = count // 8
        if stage == "C":
            outs = call("turn", turn_kernel, ids, [own[k]], [shape(count, 2 * D)], last)
            oth[k] = move(outs[0], "core", 1)
        elif stage == "F":
            outs = call(
                "forward", forward_kernel, ids, [own[k], oth[k], wg, wu, wd, wr],
                [shape(2 * u, WIDE, f32)] * 2 + [shape(2 * u, WIDE)] * 2, last, limit=24, flops=4 * count * D * WIDE,
            )
            s["keep"], s["second"] = outs[:2]
            s["got"], s["ahead"] = step(outs[2], 1), step(outs[3], -1)
        elif stage == "S1":
            outs = call("add", add_kernel, ids, [s["second"], s["got"]], [shape(2 * u, WIDE)], last)
            s["got2"] = step(outs[0], 1)
        elif stage == "S2":
            outs = call(
                "beside", beside_kernel, ids, [s["keep"], s["ahead"], s["got2"]],
                [shape(u, WIDE, ACROSS), shape(u, WIDE, f32)], last,
            )
            s["across"], s["base"] = move(outs[0], "xl", 1), outs[1]
        elif stage == "ACT":
            outs = call("activate", activate_kernel, ids, [s["base"], s["across"]], [shape(u, WIDE)], last)
            s["b0"], s["b1"] = outs[0], move(outs[0], "xl", 1)
        elif stage == "PAIR":
            outs = call("both", both_kernel, ids, [s["b0"], s["b1"]], [shape(2 * u, WIDE)], last)
            s["p0"] = outs[0]
            s["p3"], s["p1"] = step(outs[0], 1), step(outs[0], -1)
            s["p2"] = step(s["p3"], 1)
        elif stage == "ASM":
            parts = [s["p0"], s["p1"], s["p2"], s["p3"]]
            outs = call("whole", whole_kernel, ids, parts, [shape(count, WIDE)] * 2, last)
            s["mine"], s["other"] = outs[0], move(outs[1], "core", 1)
        elif stage == "WG":
            grads = weight_grads(ids, [s["mine"] for s in st], [own[k] for k in range(n)], (), last)
            outs = (grads[3],)
        else:
            last += tuple(near[-1:] + far[-1:])
            outs = call(
                "back", back_kernel, ids, [s["mine"], s["other"], wg, wu],
                [shape(128, D, f32 if AWAY[k] == 0 else bf16), shape(128, D)],
                last, limit=16, flops=8 * count * D * HALF,
            )
            near.append(outs[0] if AWAY[k] == 0 else move(outs[0], "z", AWAY[k]))
            far.append(move2(outs[1], AWAY[k], 1))
        last = (outs[0],)

    rest = weight_grads(ids, [s["other"] for s in st], [own[k] for k in range(n)], grads[:3], last)
    gate_grad, up_grad, down_grad, done = rest
    (tokens_grad,) = call("total", sum_kernel, ids, near + far, [shape(128, D)], (done,))
    return tokens_grad, gate_grad, up_grad, down_grad


def solution(mesh):
    fine = Mesh(mesh.devices.reshape(tuple(AXES.values())), tuple(AXES))
    row, col = ("z", "xh"), ("y", "xl", "core")
    placed = (P(row, col), P(row, col), P(col, row), P(col, row), P(row, col))
    return jax.shard_map(
        local,
        mesh=fine,
        in_specs=placed,
        out_specs=(P(row, col), P(col, row), P(col, row), P(row, col)),
        check_vma=False,
    )
```

time: 585 us -> 195 us (0.33)
  waiting for transfers between devices: 476 us -> 64.6 us
  starting transfers between devices: 0.45 us -> 74.2 us
  Pallas kernels: 0 us -> 45.4 us
  local copies, waits for them, and re-layouts: 42.3 us -> 6.33 us
  matrix products: 35.3 us -> 0 us
  other arithmetic: 15.9 us -> 0.08 us
  between operations: 14.2 us -> 1.2 us
    reduce_scatter x2 -> x0, waiting for transfers between devices: 308 us -> none  [the longest x1 234 us: local(): lax.psum_scatter(jnp.concatenate([forward, backward], axis=1), 'col', sca...]
    all_gather x5 -> x0, waiting for transfers between devices: 166 us -> none  [the longest x1 46.2 us: local(): lax.all_gather(out_grad, 'row', axis=0, tiled=True)]
    ppermute x0 -> x52, starting transfers between devices: none -> 74.2 us  [the longest x24 32.4 us: step(): return lax.ppermute(a, ('y', 'core'), pairs)]
    ppermute x0 -> x52, waiting for transfers between devices: none -> 64.6 us  [the longest x24 39.8 us: step(): return lax.ppermute(a, ('y', 'core'), pairs)]
    pallas_call x0 -> x37, Pallas kernels: none -> 45.4 us  [the longest x34 33.9 us: call(): pl.pallas_call(kernel, in_specs=[smem] + [in_space] * n + [anywhere] * m,...]
    dot_general x5 -> x0, matrix products: 35.3 us -> none  [the longest x1 9.62 us: local(): lax.dot_general(pair_piece, both, contract_last, preferred_element_type=j...]
    unnamed x17 -> x16, local copies, waits for them, and re-layouts: 35.3 us -> 6.33 us
    concatenate x1 -> x0, other arithmetic: 11.9 us -> none  [local(): jnp.concatenate([forward, backward], axis=1)]
  transfers between devices with their start and end apart: 7 -> 52, of which waited for: 7 -> 24; matrix products, arithmetic and copies ran while one was open for 8% -> 0% of each run, Pallas kernels for 0% -> 20%
where the time goes in v2:
time: 195 us; the launch traced here: 192 us
  starting transfers between devices  74.2 us (38%)
  waiting for transfers between devices  64.6 us (33%)
  Pallas kernels  45.4 us (23%)
  local copies, waits for them, and re-layouts  6.33 us (3%)
    ppermute x24, waiting for transfers between devices, step(): return lax.ppermute(a, ('y', 'core'), pairs)  39.8 us
    pallas_call x34, Pallas kernels, call(): pl.pallas_call(kernel, in_specs=[smem] + [in_space] * n + [anywhere] * m,...  33.9 us
    ppermute x24, starting transfers between devices, step(): return lax.ppermute(a, ('y', 'core'), pairs)  32.4 us
    ppermute x24, starting transfers between devices, move(): return lax.ppermute(a, axis, [(i, (i + by) % n) for i in range(n)])  30.5 us
    ppermute x24, waiting for transfers between devices, move(): return lax.ppermute(a, axis, [(i, (i + by) % n) for i in range(n)])  16.2 us
    ppermute x4, starting transfers between devices, move2(): return lax.ppermute(a, ('z', 'xh'), pairs)  11.4 us
    pallas_call x2, Pallas kernels, weight_grads(): pl.pallas_call(kernel, in_specs=[smem] + [vmem] * (2 * n) + [anywhere] *...  10.2 us
    ppermute x4, waiting for transfers between devices, move2(): return lax.ppermute(a, ('z', 'xh'), pairs)  8.64 us
  transfers between devices with their start and end apart: 52, of which 24 were waited for; matrix products, arithmetic and copies ran while one was open for 0% of the time, Pallas kernels for 20%

profile of v2, /device:TPU:0, one launch (start us, length us, event | category | flops | bytes accessed | tf_op | source)
XLA Modules:
  0.0 191.8 jit_solution(14239005837882766131)
XLA Ops:
  3.4 3.2 %collective-permute-start = (bf16[128,1024]{1,0:T(8,128)(2,1)S(1)}, bf16[128,1024]{1,0:T(8,128)(2,1)S(1)}, u32[]{:S(2)}, u32[]{:S(2)}) collective-permute-start(bf16[128,1024]{1,0:T(8,128)(2,1)S(1)} %rows.1.refs_1_.r_4_), channel_id=1, source_target_pairs={{0,16},{16,0},{1,17},{17,1},{2,18},{18,2},{3,19},{19,3},{4,20},{20... | collective-permute-start | bytes 786440 | tf_op jit(solution)/shard_map/ppermute | solution.py:34
  18.4 2.4 %forward.4 = (f32[64,2688]{1,0:T(8,128)S(1)}, f32[64,2688]{1,0:T(8,128)S(1)}, bf16[64,2688]{1,0:T(8,128)(2,1)S(1)}, bf16[64,2688]{1,0:T(8,128)(2,1)S(1)}) custom-call(s32[3]{0:T(128)S(1)} %pad_add_fusion.refs_0_.r_0_, bf16[256,1024]{1,0:T(8,128)(2,1)S(1)} %get-tuple-element.54.refs_1_.refs_5_, bf16[256,1024]{1,0:T(8,128)(2,1)S(1)} %collective-permute-done.1.refs_2_, ...), custom_call_target="tpu_custom_call" | custom-call | flops 1409286144 | bytes 11370496 | tf_op jit(solution)/shard_map/forward/pallas_call | solution.py:61
  22.4 8.1 %collective-permute-done.6.refs_1_.refs_8_ = bf16[256,1024]{1,0:T(8,128)(2,1)S(1)} collective-permute-done((bf16[256,1024]{1,0:T(8,128)(2,1)S(1)}, bf16[256,1024]{1,0:T(8,128)(2,1)S(1)}, u32[]{:S(2)}, u32[]{:S(2)}) %collective-permute-start.6) | collective-permute-done | bytes 524320 | tf_op jit(solution)/shard_map/ppermute | solution.py:34
  34.2 3.0 %collective-permute-start.3 = (bf16[64,2688]{1,0:T(8,128)(2,1)S(1)}, bf16[64,2688]{1,0:T(8,128)(2,1)S(1)}, u32[]{:S(2)}, u32[]{:S(2)}) collective-permute-start(bf16[64,2688]{1,0:T(8,128)(2,1)S(1)} %get-tuple-element.57), channel_id=1, source_target_pairs={{0,12},{4,0},{8,4},{12,8},{1,5},{5,9},{9,13},{13,1},{2,14},{6,2},{... | collective-permute-start | bytes 1032200 | tf_op jit(solution)/shard_map/ppermute | solution.py:45
  37.9 2.3 %forward.5 = (f32[64,2688]{1,0:T(8,128)S(1)}, f32[64,2688]{1,0:T(8,128)S(1)}, bf16[64,2688]{1,0:T(8,128)(2,1)S(1)}, bf16[64,2688]{1,0:T(8,128)(2,1)S(1)}) custom-call(s32[3]{0:T(128)S(1)} %pad_add_fusion.refs_0_.r_0_, bf16[256,1024]{1,0:T(8,128)(2,1)S(1)} %collective-permute-done.6.refs_1_.refs_8_, bf16[256,1024]{1,0:T(8,128)(2,1)S(1)} %collective-permute-done.8.refs_2_, ...), custom_call_target="tpu_custom_call" | custom-call | flops 1409286144 | bytes 11370496 | tf_op jit(solution)/shard_map/forward/pallas_call | solution.py:61
  40.3 5.3 %collective-permute-done.3.refs_2_ = bf16[64,2688]{1,0:T(8,128)(2,1)S(1)} collective-permute-done((bf16[64,2688]{1,0:T(8,128)(2,1)S(1)}, bf16[64,2688]{1,0:T(8,128)(2,1)S(1)}, u32[]{:S(2)}, u32[]{:S(2)}) %collective-permute-start.3) | collective-permute-done | bytes 344096 | tf_op jit(solution)/shard_map/ppermute | solution.py:45
  47.0 2.3 %forward.6 = (f32[64,2688]{1,0:T(8,128)S(1)}, f32[64,2688]{1,0:T(8,128)S(1)}, bf16[64,2688]{1,0:T(8,128)(2,1)S(1)}, bf16[64,2688]{1,0:T(8,128)(2,1)S(1)}) custom-call(s32[3]{0:T(128)S(1)} %pad_add_fusion.refs_0_.r_0_, bf16[256,1024]{1,0:T(8,128)(2,1)S(1)} %collective-permute-done.5.refs_1_.refs_6_, bf16[256,1024]{1,0:T(8,128)(2,1)S(1)} %collective-permute-done.12.refs_2_, ...), custom_call_target="tpu_custom_call" | custom-call | flops 1409286144 | bytes 11370496 | tf_op jit(solution)/shard_map/forward/pallas_call | solution.py:61
  55.2 3.7 %collective-permute-done.10.refs_2_ = bf16[64,2688]{1,0:T(8,128)(2,1)S(1)} collective-permute-done((bf16[64,2688]{1,0:T(8,128)(2,1)S(1)}, bf16[64,2688]{1,0:T(8,128)(2,1)S(1)}, u32[]{:S(2)}, u32[]{:S(2)}) %collective-permute-start.10) | collective-permute-done | bytes 344096 | tf_op jit(solution)/shard_map/ppermute | solution.py:45
  58.9 4.4 %collective-permute-start.14 = (bf16[64,2688]{1,0:T(8,128)(2,1)S(1)}, bf16[64,2688]{1,0:T(8,128)(2,1)S(1)}, u32[]{:S(2)}, u32[]{:S(2)}) collective-permute-start(bf16[64,2688]{1,0:T(8,128)(2,1)S(1)} %get-tuple-element.66), channel_id=1, source_target_pairs={{0,12},{4,0},{8,4},{12,8},{1,5},{5,9},{9,13},{13,1},{2,14},{6,2},{... | collective-permute-start | bytes 1032200 | tf_op jit(solution)/shard_map/ppermute | solution.py:45
  67.0 2.7 %collective-permute-start.13 = (bf16[32,2688]{1,0:T(8,128)(2,1)S(1)}, bf16[32,2688]{1,0:T(8,128)(2,1)S(1)}, u32[]{:S(2)}, u32[]{:S(2)}) collective-permute-start(bf16[32,2688]{1,0:T(8,128)(2,1)S(1)} %activate.4.refs_3_.refs_1_), channel_id=1, source_target_pairs={{0,2},{2,0},{1,3},{3,1},{4,6},{6,4},{5,7},{7,5},{8,10},{10,8},{9,1... | collective-permute-start | bytes 516104 | tf_op jit(solution)/shard_map/ppermute | solution.py:34
  69.7 2.4 %forward.7 = (f32[64,2688]{1,0:T(8,128)S(1)}, f32[64,2688]{1,0:T(8,128)S(1)}, bf16[64,2688]{1,0:T(8,128)(2,1)S(1)}, bf16[64,2688]{1,0:T(8,128)(2,1)S(1)}) custom-call(s32[3]{0:T(128)S(1)} %pad_add_fusion.refs_0_.r_0_, bf16[256,1024]{1,0:T(8,128)(2,1)S(1)} %collective-permute-done.11.refs_1_.refs_7_, bf16[256,1024]{1,0:T(8,128)(2,1)S(1)} %collective-permute-done.19.refs_2_, ...), custom_call_target="tpu_custom_call" | custom-call | flops 1409286144 | bytes 11370496 | tf_op jit(solution)/shard_map/forward/pallas_call | solution.py:61
  83.8 3.1 %collective-permute-start.20 = (bf16[64,2688]{1,0:T(8,128)(2,1)S(1)}, bf16[64,2688]{1,0:T(8,128)(2,1)S(1)}, u32[]{:S(2)}, u32[]{:S(2)}) collective-permute-start(bf16[64,2688]{1,0:T(8,128)(2,1)S(1)} %both.4.refs_3_.refs_1_), channel_id=1, source_target_pairs={{0,12},{4,0},{8,4},{12,8},{1,5},{5,9},{9,13},{13,1},{2,14},{6,2},{... | collective-permute-start | bytes 1032200 | tf_op jit(solution)/shard_map/ppermute | solution.py:45
  87.0 2.6 %collective-permute-done.21.refs_4_ = bf16[64,2688]{1,0:T(8,128)(2,1)S(1)} collective-permute-done((bf16[64,2688]{1,0:T(8,128)(2,1)S(1)}, bf16[64,2688]{1,0:T(8,128)(2,1)S(1)}, u32[]{:S(2)}, u32[]{:S(2)}) %collective-permute-start.21) | collective-permute-done | bytes 344096 | tf_op jit(solution)/shard_map/ppermute | solution.py:45
  91.8 5.2 %collective-permute-done.28.refs_3_ = bf16[64,2688]{1,0:T(8,128)(2,1)S(1)} collective-permute-done((bf16[64,2688]{1,0:T(8,128)(2,1)S(1)}, bf16[64,2688]{1,0:T(8,128)(2,1)S(1)}, u32[]{:S(2)}, u32[]{:S(2)}) %collective-permute-start.28) | collective-permute-done | bytes 344096 | tf_op jit(solution)/shard_map/ppermute | solution.py:45
  98.8 2.7 %collective-permute-done.22.refs_3_ = bf16[64,2688]{1,0:T(8,128)(2,1)S(1)} collective-permute-done((bf16[64,2688]{1,0:T(8,128)(2,1)S(1)}, bf16[64,2688]{1,0:T(8,128)(2,1)S(1)}, u32[]{:S(2)}, u32[]{:S(2)}) %collective-permute-start.22) | collective-permute-done | bytes 344096 | tf_op jit(solution)/shard_map/ppermute | solution.py:45
  104.0 3.1 %collective-permute-start.32 = (bf16[64,2688]{1,0:T(8,128)(2,1)S(1)}, bf16[64,2688]{1,0:T(8,128)(2,1)S(1)}, u32[]{:S(2)}, u32[]{:S(2)}) collective-permute-start(bf16[64,2688]{1,0:T(8,128)(2,1)S(1)} %both.5.refs_5_.refs_1_), channel_id=1, source_target_pairs={{0,12},{4,0},{8,4},{12,8},{1,5},{5,9},{9,13},{13,1},{2,14},{6,2},{... | collective-permute-start | bytes 1032200 | tf_op jit(solution)/shard_map/ppermute | solution.py:45
  107.2 6.5 %collective-permute-done.33.refs_4_ = bf16[64,2688]{1,0:T(8,128)(2,1)S(1)} collective-permute-done((bf16[64,2688]{1,0:T(8,128)(2,1)S(1)}, bf16[64,2688]{1,0:T(8,128)(2,1)S(1)}, u32[]{:S(2)}, u32[]{:S(2)}) %collective-permute-start.33) | collective-permute-done | bytes 344096 | tf_op jit(solution)/shard_map/ppermute | solution.py:45
  113.6 2.4 %collective-permute-start.30 = (bf16[32,2688]{1,0:T(8,128)(2,1)S(1)}, bf16[32,2688]{1,0:T(8,128)(2,1)S(1)}, u32[]{:S(2)}, u32[]{:S(2)}) collective-permute-start(bf16[32,2688]{1,0:T(8,128)(2,1)S(1)} %activate.6.refs_3_.refs_1_), channel_id=1, source_target_pairs={{0,2},{2,0},{1,3},{3,1},{4,6},{6,4},{5,7},{7,5},{8,10},{10,8},{9,1... | collective-permute-start | bytes 516104 | tf_op jit(solution)/shard_map/ppermute | solution.py:34
  116.7 2.8 %collective-permute-done.30.refs_2_ = bf16[32,2688]{1,0:T(8,128)(2,1)S(1)} collective-permute-done((bf16[32,2688]{1,0:T(8,128)(2,1)S(1)}, bf16[32,2688]{1,0:T(8,128)(2,1)S(1)}, u32[]{:S(2)}, u32[]{:S(2)}) %collective-permute-start.30) | collective-permute-done | bytes 172064 | tf_op jit(solution)/shard_map/ppermute | solution.py:34
  123.0 2.5 %collective-permute-start.39 = (bf16[32,2688]{1,0:T(8,128)(2,1)S(1)}, bf16[32,2688]{1,0:T(8,128)(2,1)S(1)}, u32[]{:S(2)}, u32[]{:S(2)}) collective-permute-start(bf16[32,2688]{1,0:T(8,128)(2,1)S(1)} %activate.7.refs_3_.refs_1_), channel_id=1, source_target_pairs={{0,2},{2,0},{1,3},{3,1},{4,6},{6,4},{5,7},{7,5},{8,10},{10,8},{9,1... | collective-permute-start | bytes 516104 | tf_op jit(solution)/shard_map/ppermute | solution.py:34
  125.5 3.1 %collective-permute-start.36 = (bf16[64,2688]{1,0:T(8,128)(2,1)S(1)}, bf16[64,2688]{1,0:T(8,128)(2,1)S(1)}, u32[]{:S(2)}, u32[]{:S(2)}) collective-permute-start(bf16[64,2688]{1,0:T(8,128)(2,1)S(1)} %both.6.refs_5_.refs_1_), channel_id=1, source_target_pairs={{0,12},{4,0},{8,4},{12,8},{1,5},{5,9},{9,13},{13,1},{2,14},{6,2},{... | collective-permute-start | bytes 1032200 | tf_op jit(solution)/shard_map/ppermute | solution.py:45
  128.6 2.8 %collective-permute-done.37.refs_4_ = bf16[64,2688]{1,0:T(8,128)(2,1)S(1)} collective-permute-done((bf16[64,2688]{1,0:T(8,128)(2,1)S(1)}, bf16[64,2688]{1,0:T(8,128)(2,1)S(1)}, u32[]{:S(2)}, u32[]{:S(2)}) %collective-permute-start.37) | collective-permute-done | bytes 344096 | tf_op jit(solution)/shard_map/ppermute | solution.py:45
  132.0 3.3 %collective-permute-start.44 = (bf16[64,2688]{1,0:T(8,128)(2,1)S(1)}, bf16[64,2688]{1,0:T(8,128)(2,1)S(1)}, u32[]{:S(2)}, u32[]{:S(2)}) collective-permute-start(bf16[64,2688]{1,0:T(8,128)(2,1)S(1)} %both.7.refs_5_.refs_1_), channel_id=1, source_target_pairs={{0,4},{4,8},{8,12},{12,0},{1,13},{5,1},{9,5},{13,9},{2,6},{6,10},{... | collective-permute-start | bytes 1032200 | tf_op jit(solution)/shard_map/ppermute | solution.py:45
  135.3 5.6 %collective-permute-done.38.refs_3_ = bf16[64,2688]{1,0:T(8,128)(2,1)S(1)} collective-permute-done((bf16[64,2688]{1,0:T(8,128)(2,1)S(1)}, bf16[64,2688]{1,0:T(8,128)(2,1)S(1)}, u32[]{:S(2)}, u32[]{:S(2)}) %collective-permute-start.38) | collective-permute-done | bytes 344096 | tf_op jit(solution)/shard_map/ppermute | solution.py:45
  144.6 3.5 %collective-permute-start.40 = (bf16[128,512]{1,0:T(8,128)(2,1)S(1)}, bf16[128,512]{1,0:T(8,128)(2,1)S(1)}, u32[]{:S(2)}, u32[]{:S(2)}) collective-permute-start(bf16[128,512]{1,0:T(8,128)(2,1)S(1)} %get-tuple-element.86), channel_id=1, source_target_pairs={{0,16},{16,0},{32,48},{48,32},{64,80},{80,64},{96,112},{112,96},{1... | collective-permute-start | bytes 393224 | tf_op jit(solution)/shard_map/ppermute | solution.py:39
  148.2 4.2 %collective-permute-done.40.refs_7_.refs_5_ = bf16[128,512]{1,0:T(8,128)(2,1)S(1)} collective-permute-done((bf16[128,512]{1,0:T(8,128)(2,1)S(1)}, bf16[128,512]{1,0:T(8,128)(2,1)S(1)}, u32[]{:S(2)}, u32[]{:S(2)}) %collective-permute-start.40) | collective-permute-done | bytes 131104 | tf_op jit(solution)/shard_map/ppermute | solution.py:39
  155.0 3.8 %collective-permute-start.46 = (bf16[128,512]{1,0:T(8,128)(2,1)S(1)}, bf16[128,512]{1,0:T(8,128)(2,1)S(1)}, u32[]{:S(2)}, u32[]{:S(2)}) collective-permute-start(bf16[128,512]{1,0:T(8,128)(2,1)S(1)} %get-tuple-element.90), channel_id=1, source_target_pairs={{0,112},{16,96},{32,16},{48,0},{64,48},{80,32},{96,80},{112,64},{1... | collective-permute-start | bytes 393224 | tf_op jit(solution)/shard_map/ppermute | solution.py:39
  160.4 3.0 %collective-permute-done.46.refs_7_.refs_6_ = bf16[128,512]{1,0:T(8,128)(2,1)S(1)} collective-permute-done((bf16[128,512]{1,0:T(8,128)(2,1)S(1)}, bf16[128,512]{1,0:T(8,128)(2,1)S(1)}, u32[]{:S(2)}, u32[]{:S(2)}) %collective-permute-start.46) | collective-permute-done | bytes 131104 | tf_op jit(solution)/shard_map/ppermute | solution.py:39
  163.4 2.7 %collective-permute-done.41.refs_6_.refs_2_ = bf16[128,512]{1,0:T(8,128)(2,1)S(1)} collective-permute-done((bf16[128,512]{1,0:T(8,128)(2,1)S(1)}, bf16[128,512]{1,0:T(8,128)(2,1)S(1)}, u32[]{:S(2)}, u32[]{:S(2)}) %collective-permute-start.41) | collective-permute-done | bytes 131104 | tf_op jit(solution)/shard_map/ppermute | solution.py:34
  170.6 5.1 %weight_grads.2 = (bf16[512,1792]{1,0:T(8,128)(2,1)}, bf16[512,1792]{1,0:T(8,128)(2,1)}, bf16[1792,512]{1,0:T(8,128)(2,1)}, f32[8,128]{1,0:T(8,128)S(1)}) custom-call(s32[3]{0:T(128)S(1)} %pad_add_fusion.refs_0_.r_0_, bf16[256,2688]{1,0:T(8,128)(2,1)S(1)} %get-tuple-element.79.refs_3_.refs_1_, ...), custom_call_target="tpu_custom_call" | custom-call | flops 2818572288 | bytes 10485760 | tf_op jit(solution)/shard_map/weight_grads/pallas_call | solution.py:245
  180.3 2.3 %collective-permute-start.51 = (bf16[128,512]{1,0:T(8,128)(2,1)S(1)}, bf16[128,512]{1,0:T(8,128)(2,1)S(1)}, u32[]{:S(2)}, u32[]{:S(2)}) collective-permute-start(bf16[128,512]{1,0:T(8,128)(2,1)S(1)} %get-tuple-element.96), channel_id=1, source_target_pairs={{0,80},{16,64},{32,112},{48,96},{64,16},{80,0},{96,48},{112,32},{1... | collective-permute-start | bytes 393224 | tf_op jit(solution)/shard_map/ppermute | solution.py:39
  184.8 5.1 %weight_grads.3 = (bf16[512,1792]{1,0:T(8,128)(2,1)}, bf16[512,1792]{1,0:T(8,128)(2,1)}, bf16[1792,512]{1,0:T(8,128)(2,1)}, f32[8,128]{1,0:T(8,128)S(1)}) custom-call(s32[3]{0:T(128)S(1)} %pad_add_fusion.refs_0_.r_0_, bf16[256,2688]{1,0:T(8,128)(2,1)S(1)} %collective-permute-done.29.refs_2_.refs_1_, ...), custom_call_target="tpu_custom_call", output_to_operand_aliasing={{0}: (9, {}), {1}: (10, {}), {2}: (11, {})} | custom-call | flops 2818572288 | bytes 10485760 | tf_op jit(solution)/shard_map/weight_grads/pallas_call | solution.py:245
  (126 shorter events, 75.4 us)
Async XLA Ops:
  13.7 16.8 %collective-permute-start.6 = (bf16[256,1024]{1,0:T(8,128)(2,1)S(1)}, bf16[256,1024]{1,0:T(8,128)(2,1)S(1)}, u32[]{:S(2)}, u32[]{:S(2)}) collective-permute-start(bf16[256,1024]{1,0:T(8,128)(2,1)S(1)} %get-tuple-element.54.refs_1_.refs_5_), channel_id=1, source_target_pairs={{0,32},{32,64},{64,96},{96,0},{1,33},{33,65},{65,97},{97,1},{2,34}... | collective-permute-start | bytes 1572872 | tf_op jit(solution)/shard_map/ppermute | solution.py:34
  15.9 15.3 %collective-permute-start.5 = (bf16[256,1024]{1,0:T(8,128)(2,1)S(1)}, bf16[256,1024]{1,0:T(8,128)(2,1)S(1)}, u32[]{:S(2)}, u32[]{:S(2)}) collective-permute-start(bf16[256,1024]{1,0:T(8,128)(2,1)S(1)} %get-tuple-element.54.refs_1_.refs_5_), channel_id=1, source_target_pairs={{0,96},{32,0},{64,32},{96,64},{1,97},{33,1},{65,33},{97,65},{2,98}... | collective-permute-start | bytes 1572872 | tf_op jit(solution)/shard_map/ppermute | solution.py:34
  20.7 16.5 %collective-permute-start.4 = (bf16[64,2688]{1,0:T(8,128)(2,1)S(1)}, bf16[64,2688]{1,0:T(8,128)(2,1)S(1)}, u32[]{:S(2)}, u32[]{:S(2)}) collective-permute-start(bf16[64,2688]{1,0:T(8,128)(2,1)S(1)} %get-tuple-element.59), channel_id=1, source_target_pairs={{0,4},{4,8},{8,12},{12,0},{1,13},{5,1},{9,5},{13,9},{2,6},{6,10},{... | collective-permute-start | bytes 1032200 | tf_op jit(solution)/shard_map/ppermute | solution.py:45
  31.8 15.2 %collective-permute-start.12 = (bf16[256,1024]{1,0:T(8,128)(2,1)S(1)}, bf16[256,1024]{1,0:T(8,128)(2,1)S(1)}, u32[]{:S(2)}, u32[]{:S(2)}) collective-permute-start(bf16[256,1024]{1,0:T(8,128)(2,1)S(1)} %turn.4.refs_3_), channel_id=1, source_target_pairs={{0,1},{1,0},{2,3},{3,2},{4,5},{5,4},{6,7},{7,6},{8,9},{9,8},{10,11... | collective-permute-start | bytes 1572872 | tf_op jit(solution)/shard_map/ppermute | solution.py:34
  32.3 17.0 %collective-permute-start.11 = (bf16[256,1024]{1,0:T(8,128)(2,1)S(1)}, bf16[256,1024]{1,0:T(8,128)(2,1)S(1)}, u32[]{:S(2)}, u32[]{:S(2)}) collective-permute-start(bf16[256,1024]{1,0:T(8,128)(2,1)S(1)} %get-tuple-element.54.refs_1_.refs_5_), channel_id=1, source_target_pairs={{0,64},{32,96},{64,0},{96,32},{1,65},{33,97},{65,1},{97,33},{2,66}... | collective-permute-start | bytes 1572872 | tf_op jit(solution)/shard_map/ppermute | solution.py:34
  34.2 11.3 %collective-permute-start.3 = (bf16[64,2688]{1,0:T(8,128)(2,1)S(1)}, bf16[64,2688]{1,0:T(8,128)(2,1)S(1)}, u32[]{:S(2)}, u32[]{:S(2)}) collective-permute-start(bf16[64,2688]{1,0:T(8,128)(2,1)S(1)} %get-tuple-element.57), channel_id=1, source_target_pairs={{0,12},{4,0},{8,4},{12,8},{1,5},{5,9},{9,13},{13,1},{2,14},{6,2},{... | collective-permute-start | bytes 1032200 | tf_op jit(solution)/shard_map/ppermute | solution.py:45
  50.0 17.0 %collective-permute-start.19 = (bf16[256,1024]{1,0:T(8,128)(2,1)S(1)}, bf16[256,1024]{1,0:T(8,128)(2,1)S(1)}, u32[]{:S(2)}, u32[]{:S(2)}) collective-permute-start(bf16[256,1024]{1,0:T(8,128)(2,1)S(1)} %turn.5.refs_3_), channel_id=1, source_target_pairs={{0,1},{1,0},{2,3},{3,2},{4,5},{5,4},{6,7},{7,6},{8,9},{9,8},{10,11... | collective-permute-start | bytes 1572872 | tf_op jit(solution)/shard_map/ppermute | solution.py:34
  50.5 13.4 %collective-permute-start.9 = (f32[32,2688]{1,0:T(8,128)S(1)}, f32[32,2688]{1,0:T(8,128)S(1)}, u32[]{:S(2)}, u32[]{:S(2)}) collective-permute-start(f32[32,2688]{1,0:T(8,128)S(1)} %get-tuple-element.62.refs_7_), channel_id=1, source_target_pairs={{0,2},{2,0},{1,3},{3,1},{4,6},{6,4},{5,7},{7,5},{8,10},{10,8},{9,1... | collective-permute-start | bytes 1032200 | tf_op jit(solution)/shard_map/ppermute | solution.py:34
  52.0 14.3 %collective-permute-start.15 = (bf16[64,2688]{1,0:T(8,128)(2,1)S(1)}, bf16[64,2688]{1,0:T(8,128)(2,1)S(1)}, u32[]{:S(2)}, u32[]{:S(2)}) collective-permute-start(bf16[64,2688]{1,0:T(8,128)(2,1)S(1)} %get-tuple-element.68), channel_id=1, source_target_pairs={{0,4},{4,8},{8,12},{12,0},{1,13},{5,1},{9,5},{13,9},{2,6},{6,10},{... | collective-permute-start | bytes 1032200 | tf_op jit(solution)/shard_map/ppermute | solution.py:45
  53.6 18.5 %collective-permute-start.17 = (bf16[64,2688]{1,0:T(8,128)(2,1)S(1)}, bf16[64,2688]{1,0:T(8,128)(2,1)S(1)}, u32[]{:S(2)}, u32[]{:S(2)}) collective-permute-start(bf16[64,2688]{1,0:T(8,128)(2,1)S(1)} %get-tuple-element.69), channel_id=1, source_target_pairs={{0,12},{4,0},{8,4},{12,8},{1,5},{5,9},{9,13},{13,1},{2,14},{6,2},{... | collective-permute-start | bytes 1032200 | tf_op jit(solution)/shard_map/ppermute | solution.py:45
  58.9 16.6 %collective-permute-start.14 = (bf16[64,2688]{1,0:T(8,128)(2,1)S(1)}, bf16[64,2688]{1,0:T(8,128)(2,1)S(1)}, u32[]{:S(2)}, u32[]{:S(2)}) collective-permute-start(bf16[64,2688]{1,0:T(8,128)(2,1)S(1)} %get-tuple-element.66), channel_id=1, source_target_pairs={{0,12},{4,0},{8,4},{12,8},{1,5},{5,9},{9,13},{13,1},{2,14},{6,2},{... | collective-permute-start | bytes 1032200 | tf_op jit(solution)/shard_map/ppermute | solution.py:45
  66.9 10.1 %collective-permute-start.16 = (bf16[64,2688]{1,0:T(8,128)(2,1)S(1)}, bf16[64,2688]{1,0:T(8,128)(2,1)S(1)}, u32[]{:S(2)}, u32[]{:S(2)}) collective-permute-start(bf16[64,2688]{1,0:T(8,128)(2,1)S(1)} %add.10.refs_7_), channel_id=1, source_target_pairs={{0,4},{4,8},{8,12},{12,0},{1,13},{5,1},{9,5},{13,9},{2,6},{6,10},{... | collective-permute-start | bytes 1032200 | tf_op jit(solution)/shard_map/ppermute | solution.py:45
  67.0 10.7 %collective-permute-start.13 = (bf16[32,2688]{1,0:T(8,128)(2,1)S(1)}, bf16[32,2688]{1,0:T(8,128)(2,1)S(1)}, u32[]{:S(2)}, u32[]{:S(2)}) collective-permute-start(bf16[32,2688]{1,0:T(8,128)(2,1)S(1)} %activate.4.refs_3_.refs_1_), channel_id=1, source_target_pairs={{0,2},{2,0},{1,3},{3,1},{4,6},{6,4},{5,7},{7,5},{8,10},{10,8},{9,1... | collective-permute-start | bytes 516104 | tf_op jit(solution)/shard_map/ppermute | solution.py:34
  74.0 9.9 %collective-permute-start.23 = (f32[32,2688]{1,0:T(8,128)S(1)}, f32[32,2688]{1,0:T(8,128)S(1)}, u32[]{:S(2)}, u32[]{:S(2)}) collective-permute-start(f32[32,2688]{1,0:T(8,128)S(1)} %get-tuple-element.71.refs_4_), channel_id=1, source_target_pairs={{0,2},{2,0},{1,3},{3,1},{4,6},{6,4},{5,7},{7,5},{8,10},{10,8},{9,1... | collective-permute-start | bytes 1032200 | tf_op jit(solution)/shard_map/ppermute | solution.py:34
  78.3 11.3 %collective-permute-start.21 = (bf16[64,2688]{1,0:T(8,128)(2,1)S(1)}, bf16[64,2688]{1,0:T(8,128)(2,1)S(1)}, u32[]{:S(2)}, u32[]{:S(2)}) collective-permute-start(bf16[64,2688]{1,0:T(8,128)(2,1)S(1)} %both.4.refs_3_.refs_1_), channel_id=1, source_target_pairs={{0,4},{4,8},{8,12},{12,0},{1,13},{5,1},{9,5},{13,9},{2,6},{6,10},{... | collective-permute-start | bytes 1032200 | tf_op jit(solution)/shard_map/ppermute | solution.py:45
  79.3 11.3 %collective-permute-start.27 = (bf16[64,2688]{1,0:T(8,128)(2,1)S(1)}, bf16[64,2688]{1,0:T(8,128)(2,1)S(1)}, u32[]{:S(2)}, u32[]{:S(2)}) collective-permute-start(bf16[64,2688]{1,0:T(8,128)(2,1)S(1)} %get-tuple-element.77), channel_id=1, source_target_pairs={{0,12},{4,0},{8,4},{12,8},{1,5},{5,9},{9,13},{13,1},{2,14},{6,2},{... | collective-permute-start | bytes 1032200 | tf_op jit(solution)/shard_map/ppermute | solution.py:45
  82.2 14.8 %collective-permute-start.28 = (bf16[64,2688]{1,0:T(8,128)(2,1)S(1)}, bf16[64,2688]{1,0:T(8,128)(2,1)S(1)}, u32[]{:S(2)}, u32[]{:S(2)}) collective-permute-start(bf16[64,2688]{1,0:T(8,128)(2,1)S(1)} %add.11.refs_3_), channel_id=1, source_target_pairs={{0,4},{4,8},{8,12},{12,0},{1,13},{5,1},{9,5},{13,9},{2,6},{6,10},{... | collective-permute-start | bytes 1032200 | tf_op jit(solution)/shard_map/ppermute | solution.py:45
  82.3 15.4 %collective-permute-start.26 = (f32[32,2688]{1,0:T(8,128)S(1)}, f32[32,2688]{1,0:T(8,128)S(1)}, u32[]{:S(2)}, u32[]{:S(2)}) collective-permute-start(f32[32,2688]{1,0:T(8,128)S(1)} %get-tuple-element.72.refs_3_), channel_id=1, source_target_pairs={{0,2},{2,0},{1,3},{3,1},{4,6},{6,4},{5,7},{7,5},{8,10},{10,8},{9,1... | collective-permute-start | bytes 1032200 | tf_op jit(solution)/shard_map/ppermute | solution.py:34
  83.8 15.0 %collective-permute-start.20 = (bf16[64,2688]{1,0:T(8,128)(2,1)S(1)}, bf16[64,2688]{1,0:T(8,128)(2,1)S(1)}, u32[]{:S(2)}, u32[]{:S(2)}) collective-permute-start(bf16[64,2688]{1,0:T(8,128)(2,1)S(1)} %both.4.refs_3_.refs_1_), channel_id=1, source_target_pairs={{0,12},{4,0},{8,4},{12,8},{1,5},{5,9},{9,13},{13,1},{2,14},{6,2},{... | collective-permute-start | bytes 1032200 | tf_op jit(solution)/shard_map/ppermute | solution.py:45
  89.6 11.9 %collective-permute-start.22 = (bf16[64,2688]{1,0:T(8,128)(2,1)S(1)}, bf16[64,2688]{1,0:T(8,128)(2,1)S(1)}, u32[]{:S(2)}, u32[]{:S(2)}) collective-permute-start(bf16[64,2688]{1,0:T(8,128)(2,1)S(1)} %collective-permute-done.21.refs_4_), channel_id=1, source_target_pairs={{0,4},{4,8},{8,12},{12,0},{1,13},{5,1},{9,5},{13,9},{2,6},{6,10},{... | collective-permute-start | bytes 1032200 | tf_op jit(solution)/shard_map/ppermute | solution.py:45
  102.3 17.8 %collective-permute-start.29 = (bf16[256,2688]{1,0:T(8,128)(2,1)S(1)}, bf16[256,2688]{1,0:T(8,128)(2,1)S(1)}, u32[]{:S(2)}, u32[]{:S(2)}) collective-permute-start(bf16[256,2688]{1,0:T(8,128)(2,1)S(1)} %get-tuple-element.80), channel_id=1, source_target_pairs={{0,1},{1,0},{2,3},{3,2},{4,5},{5,4},{6,7},{7,6},{8,9},{9,8},{10,11... | collective-permute-start | bytes 4128776 | tf_op jit(solution)/shard_map/ppermute | solution.py:34
  102.4 11.3 %collective-permute-start.33 = (bf16[64,2688]{1,0:T(8,128)(2,1)S(1)}, bf16[64,2688]{1,0:T(8,128)(2,1)S(1)}, u32[]{:S(2)}, u32[]{:S(2)}) collective-permute-start(bf16[64,2688]{1,0:T(8,128)(2,1)S(1)} %both.5.refs_5_.refs_1_), channel_id=1, source_target_pairs={{0,4},{4,8},{8,12},{12,0},{1,13},{5,1},{9,5},{13,9},{2,6},{6,10},{... | collective-permute-start | bytes 1032200 | tf_op jit(solution)/shard_map/ppermute | solution.py:45
  102.4 13.6 %collective-permute-start.31 = (f32[32,2688]{1,0:T(8,128)S(1)}, f32[32,2688]{1,0:T(8,128)S(1)}, u32[]{:S(2)}, u32[]{:S(2)}) collective-permute-start(f32[32,2688]{1,0:T(8,128)S(1)} %get-tuple-element.78.refs_3_), channel_id=1, source_target_pairs={{0,2},{2,0},{1,3},{3,1},{4,6},{6,4},{5,7},{7,5},{8,10},{10,8},{9,1... | collective-permute-start | bytes 1032200 | tf_op jit(solution)/shard_map/ppermute | solution.py:34
  104.0 17.8 %collective-permute-start.32 = (bf16[64,2688]{1,0:T(8,128)(2,1)S(1)}, bf16[64,2688]{1,0:T(8,128)(2,1)S(1)}, u32[]{:S(2)}, u32[]{:S(2)}) collective-permute-start(bf16[64,2688]{1,0:T(8,128)(2,1)S(1)} %both.5.refs_5_.refs_1_), channel_id=1, source_target_pairs={{0,12},{4,0},{8,4},{12,8},{1,5},{5,9},{9,13},{13,1},{2,14},{6,2},{... | collective-permute-start | bytes 1032200 | tf_op jit(solution)/shard_map/ppermute | solution.py:45
  122.8 29.5 %collective-permute-start.35 = (bf16[256,2688]{1,0:T(8,128)(2,1)S(1)}, bf16[256,2688]{1,0:T(8,128)(2,1)S(1)}, u32[]{:S(2)}, u32[]{:S(2)}) collective-permute-start(bf16[256,2688]{1,0:T(8,128)(2,1)S(1)} %get-tuple-element.84), channel_id=1, source_target_pairs={{0,1},{1,0},{2,3},{3,2},{4,5},{5,4},{6,7},{7,6},{8,9},{9,8},{10,11... | collective-permute-start | bytes 4128776 | tf_op jit(solution)/shard_map/ppermute | solution.py:34
  125.5 9.8 %collective-permute-start.36 = (bf16[64,2688]{1,0:T(8,128)(2,1)S(1)}, bf16[64,2688]{1,0:T(8,128)(2,1)S(1)}, u32[]{:S(2)}, u32[]{:S(2)}) collective-permute-start(bf16[64,2688]{1,0:T(8,128)(2,1)S(1)} %both.6.refs_5_.refs_1_), channel_id=1, source_target_pairs={{0,12},{4,0},{8,4},{12,8},{1,5},{5,9},{9,13},{13,1},{2,14},{6,2},{... | collective-permute-start | bytes 1032200 | tf_op jit(solution)/shard_map/ppermute | solution.py:45
  132.0 12.6 %collective-permute-start.44 = (bf16[64,2688]{1,0:T(8,128)(2,1)S(1)}, bf16[64,2688]{1,0:T(8,128)(2,1)S(1)}, u32[]{:S(2)}, u32[]{:S(2)}) collective-permute-start(bf16[64,2688]{1,0:T(8,128)(2,1)S(1)} %both.7.refs_5_.refs_1_), channel_id=1, source_target_pairs={{0,4},{4,8},{8,12},{12,0},{1,13},{5,1},{9,5},{13,9},{2,6},{6,10},{... | collective-permute-start | bytes 1032200 | tf_op jit(solution)/shard_map/ppermute | solution.py:45
  141.7 18.7 %collective-permute-start.42 = (bf16[256,2688]{1,0:T(8,128)(2,1)S(1)}, bf16[256,2688]{1,0:T(8,128)(2,1)S(1)}, u32[]{:S(2)}, u32[]{:S(2)}) collective-permute-start(bf16[256,2688]{1,0:T(8,128)(2,1)S(1)} %get-tuple-element.88), channel_id=1, source_target_pairs={{0,1},{1,0},{2,3},{3,2},{4,5},{5,4},{6,7},{7,6},{8,9},{9,8},{10,11... | collective-permute-start | bytes 4128776 | tf_op jit(solution)/shard_map/ppermute | solution.py:34
  141.8 12.4 %collective-permute-start.43 = (bf16[64,2688]{1,0:T(8,128)(2,1)S(1)}, bf16[64,2688]{1,0:T(8,128)(2,1)S(1)}, u32[]{:S(2)}, u32[]{:S(2)}) collective-permute-start(bf16[64,2688]{1,0:T(8,128)(2,1)S(1)} %both.7.refs_5_.refs_1_), channel_id=1, source_target_pairs={{0,12},{4,0},{8,4},{12,8},{1,5},{5,9},{9,13},{13,1},{2,14},{6,2},{... | collective-permute-start | bytes 1032200 | tf_op jit(solution)/shard_map/ppermute | solution.py:45
  144.6 9.5 %collective-permute-start.45 = (bf16[64,2688]{1,0:T(8,128)(2,1)S(1)}, bf16[64,2688]{1,0:T(8,128)(2,1)S(1)}, u32[]{:S(2)}, u32[]{:S(2)}) collective-permute-start(bf16[64,2688]{1,0:T(8,128)(2,1)S(1)} %collective-permute-done.44.refs_4_), channel_id=1, source_target_pairs={{0,4},{4,8},{8,12},{12,0},{1,13},{5,1},{9,5},{13,9},{2,6},{6,10},{... | collective-permute-start | bytes 1032200 | tf_op jit(solution)/shard_map/ppermute | solution.py:45
  154.9 23.6 %collective-permute-start.48 = (bf16[256,2688]{1,0:T(8,128)(2,1)S(1)}, bf16[256,2688]{1,0:T(8,128)(2,1)S(1)}, u32[]{:S(2)}, u32[]{:S(2)}) collective-permute-start(bf16[256,2688]{1,0:T(8,128)(2,1)S(1)} %get-tuple-element.92), channel_id=1, source_target_pairs={{0,1},{1,0},{2,3},{3,2},{4,5},{5,4},{6,7},{7,6},{8,9},{9,8},{10,11... | collective-permute-start | bytes 4128776 | tf_op jit(solution)/shard_map/ppermute | solution.py:34
  180.3 9.6 %collective-permute-start.51 = (bf16[128,512]{1,0:T(8,128)(2,1)S(1)}, bf16[128,512]{1,0:T(8,128)(2,1)S(1)}, u32[]{:S(2)}, u32[]{:S(2)}) collective-permute-start(bf16[128,512]{1,0:T(8,128)(2,1)S(1)} %get-tuple-element.96), channel_id=1, source_target_pairs={{0,80},{16,64},{32,112},{48,96},{64,16},{80,0},{96,48},{112,32},{1... | collective-permute-start | bytes 393224 | tf_op jit(solution)/shard_map/ppermute | solution.py:39
  (28 other events, 185.2 us)

commit v3 on v2

--- a/solution.py
+++ b/solution.py
@@ -17,15 +17,17 @@
 contract_last = (((1,), (1,)), ((), ()))
 vmem = pl.BlockSpec(memory_space=pltpu.VMEM)
 anywhere = pl.BlockSpec(memory_space=pl.ANY)
+hbm = pl.BlockSpec(memory_space=pltpu.HBM)
 smem = pl.BlockSpec(memory_space=pltpu.SMEM)
 
-AWAY = (0, 1, 2, 3)
-ACROSS = f32
+CHUNKS = ((0,), (3,), (1,), (2,))
+GROUPS = ((0,), (1,), (2,), (3,))
+LAG = 3
 ORDER = (
-    ("F", 0), ("C", 3), ("C", 1), ("S1", 0), ("F", 3), ("S2", 0), ("F", 1), ("C", 2),
-    ("S1", 3), ("ACT", 0), ("S1", 1), ("F", 2), ("S2", 3), ("S2", 1), ("PAIR", 0), ("S1", 2),
-    ("ACT", 3), ("S2", 2), ("ACT", 1), ("PAIR", 3), ("ASM", 0), ("ACT", 2), ("PAIR", 1), ("BACK", 0),
-    ("ASM", 3), ("PAIR", 2), ("ASM", 1), ("BACK", 3), ("ASM", 2), ("BACK", 1), ("WG", 0), ("BACK", 2),
+    ("F", 0), ("C", 1), ("C", 2), ("S1", 0), ("F", 1), ("S2", 0), ("F", 2), ("C", 3),
+    ("S1", 1), ("ACT", 0), ("S1", 2), ("F", 3), ("S2", 1), ("S2", 2), ("S1", 3), ("ACT", 1),
+    ("S2", 3), ("ASM", 0), ("ACT", 2), ("ASM", 1), ("BACK", 0), ("ACT", 3), ("ASM", 2), ("BACK", 1),
+    ("ASM", 3), ("BACK", 2), ("WG", 0), ("BACK", 3),
 )
 
 
@@ -64,7 +66,7 @@
         out_specs=[vmem] * len(outs),
         out_shape=outs,
         scratch_shapes=scratch,
-        cost_estimate=pl.CostEstimate(flops=flops, bytes_accessed=size, transcendentals=0),
+        cost_estimate=pl.CostEstimate(flops=flops if name == "pair" else 0, bytes_accessed=0, transcendentals=0),
         compiler_params=pltpu.CompilerParams(vmem_limit_bytes=limit << 20),
         name=name,
     )(ids, *args, *after)
@@ -105,11 +107,17 @@
         turned[32 * t : 32 * t + 32, :] = both
 
 
-def turn_kernel(ids, rows, out):
-    n = rows.shape[0] // 4
-    for j in range(4):
-        t = (4 - j) % 4
-        out[t * n : t * n + n, :] = rows[j * n : j * n + n, :]
+def turn_kernel(ids, *refs):
+    parts, (out, turned) = refs[:-2], refs[-2:]
+    n = len(parts)
+    for b in range(8):
+        t = (4 - b // 2) % 4 * 2 + b % 2
+        for m, p in enumerate(parts):
+            rows = p[32 * b : 32 * b + 32, :]
+            at = 32 * (n * b + m)
+            out[at : at + 32, :] = rows
+            at = 32 * (n * t + m)
+            turned[at : at + 32, :] = rows
 
 
 def send_kernel(ids, wg, wu, wd, out, turn, sems):
@@ -130,7 +138,7 @@
 def send_weights(ids, wg, wu, wd, after):
     return pl.pallas_call(
         lambda *r: send_kernel(*r[:4], *r[5:]),
-        in_specs=[smem] + [anywhere] * 4,
+        in_specs=[smem] + [hbm] * 3 + [anywhere],
         out_specs=vmem,
         out_shape=shape(D, WIDE),
         scratch_shapes=[pltpu.VMEM((HALF, D), bf16), pltpu.SemaphoreType.DMA((3,))],
@@ -163,50 +171,60 @@
     out[...] = (second[...] + got[...].astype(f32)).astype(bf16)
 
 
-def beside_kernel(ids, keep, ahead, got, out, base):
-    u = out.shape[0]
-    for rows, dst in ((slice(0, u), base), (slice(u, 2 * u), out)):
-        dst[...] = (keep[rows] + ahead[rows].astype(f32) + got[rows].astype(f32)).astype(dst.dtype)
+def beside_kernel(ids, keep, ahead, got, out):
+    out[...] = keep[...] + ahead[...].astype(f32) + got[...].astype(f32)
 
 
 def activate_kernel(ids, base, across, out):
-    def total(j):
-        cols = slice(j * HALF, (j + 1) * HALF)
-        return base[:, cols] + across[:, cols].astype(f32)
-
-    gate, upper, hidden_grad = total(0), total(1), total(2)
-    sig = jax.nn.sigmoid(gate)
-    silu = gate * sig
-    out[:, :HALF] = (silu * upper).astype(bf16)
-    out[:, HALF : 2 * HALF] = (hidden_grad * upper * sig * (1.0 + gate * (1.0 - sig))).astype(bf16)
-    out[:, 2 * HALF :] = (hidden_grad * silu).astype(bf16)
-
-
-def both_kernel(ids, a, b, out):
-    out[: a.shape[0]] = a[...]
-    out[a.shape[0] :] = b[...]
-
-
-def whole_kernel(ids, p0, p1, p2, p3, out, turned):
-    n = p0.shape[0]
-    for j, (a, b) in enumerate(((p0, p0), (p1, p3), (p2, p2), (p3, p1))):
-        out[n * j : n * j + n] = a[...]
-        turned[n * j : n * j + n] = b[...]
-
-
-def back_kernel(ids, mine, other, wg, wu, near, far):
+    u = out.shape[0] // 2
+    for h in range(2):
+        mine, theirs = slice(h * u, h * u + u), slice((1 - h) * u, (1 - h) * u + u)
+
+        def total(j):
+            cols = slice(j * HALF, (j + 1) * HALF)
+            return base[mine, cols] + across[theirs, cols].astype(f32)
+
+        gate, upper, hidden_grad = total(0), total(1), total(2)
+        sig = jax.nn.sigmoid(gate)
+        silu = gate * sig
+        out[mine, :HALF] = (silu * upper).astype(bf16)
+        out[mine, HALF : 2 * HALF] = (hidden_grad * upper * sig * (1.0 + gate * (1.0 - sig))).astype(bf16)
+        out[mine, 2 * HALF :] = (hidden_grad * silu).astype(bf16)
+
+
+def whole_kernel(sizes, ids, p0, p1, p2, p3, out, turned):
+    at = 0
+    for n in sizes:
+        for j, (a, b) in enumerate(((p0, p0), (p1, p3), (p2, p2), (p3, p1))):
+            dst = slice(4 * at + n * j, 4 * at + n * j + n)
+            out[dst] = a[at : at + n]
+            turned[dst] = b[at : at + n]
+        at += n
+
+
+def back_kernel(parts, ids, mine, other, wg, wu, *outs):
     a, b = pl.ds(offset(ids), HALF), pl.ds(offset(ids, True), HALF)
     total = dot(mine[:, HALF : 2 * HALF], wg[:, a], contract_last)
     total += dot(mine[:, 2 * HALF :], wu[:, a], contract_last)
     total += dot(other[:, HALF : 2 * HALF], wg[:, b], contract_last)
     total += dot(other[:, 2 * HALF :], wu[:, b], contract_last)
-    for k in range(8):
-        near[16 * k : 16 * k + 16, :] = total[32 * k : 32 * k + 16].astype(near.dtype)
-        far[16 * k : 16 * k + 16, :] = total[32 * k + 16 : 32 * k + 32].astype(far.dtype)
-
-
-def weights_kernel(n, second, ids, *refs):
-    parts, rows, refs = refs[:n], refs[n : 2 * n], refs[2 * n :]
+    for i, (at, apart) in enumerate(parts):
+        near, far = outs[2 * i : 2 * i + 2]
+        for k in range(8):
+            rows = at + apart * k
+            near[16 * k : 16 * k + 16, :] = total[rows : rows + 16].astype(near.dtype)
+            far[16 * k : 16 * k + 16, :] = total[rows + 16 : rows + 32].astype(far.dtype)
+
+
+def weights_kernel(n, groups, second, ids, *refs):
+    whole, rows, refs = refs[: len(groups)], refs[len(groups) : len(groups) + n], refs[len(groups) + n :]
+    parts = []
+    for w, group in zip(whole, groups):
+        at = 0
+        for i in group:
+            parts.append(w.at[at : at + rows[i].shape[0]])
+            at += rows[i].shape[0]
+    rows = [rows[i] for group in groups for i in group]
     refs = refs[3:] if second else refs
     gate_out, up_out, down_out, done, gate_buf, up_buf, down_buf, sems = refs
     copies = []
@@ -235,21 +253,22 @@
 
 
 def weight_grads(ids, parts, rows, old, after):
-    n, second = len(parts), bool(old)
+    n, second = len(rows), bool(old)
+    given = len(parts) + n
     whole = [shape(D, 2 * HALF), shape(D, 2 * HALF), shape(2 * HALF, D)]
 
     def kernel(*refs):
-        at = 1 + 2 * n + len(old)
-        weights_kernel(n, second, *refs[:at], *refs[at + len(after) :])
+        at = 1 + given + len(old)
+        weights_kernel(n, GROUPS, second, *refs[:at], *refs[at + len(after) :])
 
     return pl.pallas_call(
         kernel,
-        in_specs=[smem] + [vmem] * (2 * n) + [anywhere] * (len(old) + len(after)),
-        out_specs=[pl.BlockSpec(memory_space=pltpu.HBM)] * 3 + [vmem],
+        in_specs=[smem] + [vmem] * given + [anywhere] * (len(old) + len(after)),
+        out_specs=[hbm] * 3 + [vmem],
         out_shape=whole + [shape(8, 128, f32)],
-        input_output_aliases={1 + 2 * n + i: i for i in range(len(old))},
+        input_output_aliases={1 + given + i: i for i in range(len(old))},
         scratch_shapes=[pltpu.VMEM((D, HALF), bf16)] * 2 + [pltpu.VMEM((HALF, D), bf16), pltpu.SemaphoreType.DMA((3,))],
-        cost_estimate=pl.CostEstimate(flops=6 * 1024 * D * HALF, bytes_accessed=10 << 20, transcendentals=0),
+        cost_estimate=pl.CostEstimate(flops=0, bytes_accessed=0, transcendentals=0),
         compiler_params=pltpu.CompilerParams(vmem_limit_bytes=24 << 20),
         name="weight_grads",
     )(ids, *parts, *rows, *old, *after)
@@ -270,29 +289,37 @@
 
     (rows,) = call(
         "rows", rows_kernel, ids, [tokens, out_grad], [shape(128, 2 * D)],
-        scratch=[pltpu.SemaphoreType.DMA((16,))], in_space=anywhere,
+        scratch=[pltpu.SemaphoreType.DMA((16,))], in_space=hbm,
     )
     partner = move(rows, "xh", 1)
     wr = move(send_weights(ids, wg, wu, wd, rows), "core", 1)
     pair, turned = call("pair", pair_kernel, ids, [rows, partner], [shape(256, 2 * D)] * 2, flops=20 << 30)
-    oth = {0: move(turned, "core", 1)}
-    own = {0: pair, 1: move(pair, "z", 3), 3: move(pair, "z", 1), 2: move(pair, "z", 2)}
-
-    n = len(AWAY)
+    placed = {0: pair, 1: move(pair, "z", 3), 3: move(pair, "z", 1), 2: move(pair, "z", 2)}
+    own, oth = {0: pair}, {0: move(turned, "core", 1)}
+
+    n = len(CHUNKS)
     st = [{} for _ in range(n)]
+    gr = [{} for _ in GROUPS]
     last = ()
-    near, far = [], []
-    for stage, k in ORDER:
-        s = st[k]
-        count = own[k].shape[0]
-        u = count // 8
+    near, far, due = [], [], []
+    for at, (stage, k) in enumerate(ORDER):
+        if due and due[0][0] == at:
+            last += due.pop(0)[1]
+        if stage in ("C", "F", "S1", "S2", "ACT"):
+            s = st[k]
+            u = 32 * len(CHUNKS[k])
+        else:
+            s = gr[k]
+            us = [32 * len(CHUNKS[i]) for i in GROUPS[k]]
+            count = 8 * sum(us)
         if stage == "C":
-            outs = call("turn", turn_kernel, ids, [own[k]], [shape(count, 2 * D)], last)
-            oth[k] = move(outs[0], "core", 1)
+            parts = [placed[a] for a in CHUNKS[k]]
+            outs = call("turn", turn_kernel, ids, parts, [shape(8 * u, 2 * D)] * 2, last)
+            own[k], oth[k] = outs[0], move(outs[1], "core", 1)
         elif stage == "F":
             outs = call(
                 "forward", forward_kernel, ids, [own[k], oth[k], wg, wu, wd, wr],
-                [shape(2 * u, WIDE, f32)] * 2 + [shape(2 * u, WIDE)] * 2, last, limit=24, flops=4 * count * D * WIDE,
+                [shape(2 * u, WIDE, f32)] * 2 + [shape(2 * u, WIDE)] * 2, last, limit=32, flops=32 * u * D * WIDE,
             )
             s["keep"], s["second"] = outs[:2]
             s["got"], s["ahead"] = step(outs[2], 1), step(outs[3], -1)
@@ -302,36 +329,46 @@
         elif stage == "S2":
             outs = call(
                 "beside", beside_kernel, ids, [s["keep"], s["ahead"], s["got2"]],
-                [shape(u, WIDE, ACROSS), shape(u, WIDE, f32)], last,
-            )
-            s["across"], s["base"] = move(outs[0], "xl", 1), outs[1]
+                [shape(2 * u, WIDE, f32)], last,
+            )
+            s["across"], s["base"] = move(outs[0], "xl", 1), outs[0]
         elif stage == "ACT":
-            outs = call("activate", activate_kernel, ids, [s["base"], s["across"]], [shape(u, WIDE)], last)
-            s["b0"], s["b1"] = outs[0], move(outs[0], "xl", 1)
-        elif stage == "PAIR":
-            outs = call("both", both_kernel, ids, [s["b0"], s["b1"]], [shape(2 * u, WIDE)], last)
+            outs = call("activate", activate_kernel, ids, [s["base"], s["across"]], [shape(2 * u, WIDE)], last)
+            s = gr[k]
             s["p0"] = outs[0]
             s["p3"], s["p1"] = step(outs[0], 1), step(outs[0], -1)
             s["p2"] = step(s["p3"], 1)
         elif stage == "ASM":
             parts = [s["p0"], s["p1"], s["p2"], s["p3"]]
-            outs = call("whole", whole_kernel, ids, parts, [shape(count, WIDE)] * 2, last)
+            sizes = [2 * u for u in us]
+            outs = call(
+                "whole", lambda *r, sizes=sizes: whole_kernel(sizes, *r), ids, parts, [shape(count, WIDE)] * 2, last, limit=16
+            )
             s["mine"], s["other"] = outs[0], move(outs[1], "core", 1)
         elif stage == "WG":
-            grads = weight_grads(ids, [s["mine"] for s in st], [own[k] for k in range(n)], (), last)
+            grads = weight_grads(ids, [g["mine"] for g in gr], [own[i] for i in range(n)], (), last)
             outs = (grads[3],)
         else:
-            last += tuple(near[-1:] + far[-1:])
+            parts, owners, start = [], [], 0
+            for i in GROUPS[k]:
+                for m, a in enumerate(CHUNKS[i]):
+                    parts.append((start + 32 * m, 32 * len(CHUNKS[i])))
+                    owners.append(a)
+                start += 256 * len(CHUNKS[i])
             outs = call(
-                "back", back_kernel, ids, [s["mine"], s["other"], wg, wu],
-                [shape(128, D, f32 if AWAY[k] == 0 else bf16), shape(128, D)],
-                last, limit=16, flops=8 * count * D * HALF,
-            )
-            near.append(outs[0] if AWAY[k] == 0 else move(outs[0], "z", AWAY[k]))
-            far.append(move2(outs[1], AWAY[k], 1))
+                "back", lambda *r, parts=parts: back_kernel(parts, *r), ids, [s["mine"], s["other"], wg, wu],
+                [shape(128, D, f32 if a == 0 and x == 0 else bf16) for a in owners for x in (0, 1)],
+                last, limit=24, flops=8 * count * D * HALF,
+            )
+            sent = ()
+            for i, a in enumerate(owners):
+                near.append(outs[2 * i] if a == 0 else move(outs[2 * i], "z", a))
+                far.append(move2(outs[2 * i + 1], a, 1))
+                sent += (far[-1],) if a == 0 else (near[-1], far[-1])
+            due.append((at + LAG, sent))
         last = (outs[0],)
 
-    rest = weight_grads(ids, [s["other"] for s in st], [own[k] for k in range(n)], grads[:3], last)
+    rest = weight_grads(ids, [g["other"] for g in gr], [own[i] for i in range(n)], grads[:3], last)
     gate_grad, up_grad, down_grad, done = rest
     (tokens_grad,) = call("total", sum_kernel, ids, near + far, [shape(128, D)], (done,))
     return tokens_grad, gate_grad, up_grad, down_grad

time: 195 us -> 178 us (0.913); the launches traced: 192 us -> 177 us
  starting transfers between devices: 74.2 us -> 60.7 us
  Pallas kernels: 45.4 us -> 43.4 us
    ppermute x24 -> x20, waiting for transfers between devices: 16.2 us -> 27.6 us  [move(): return lax.ppermute(a, axis, [(i, (i + by) % n) for i in range(n)])]
    ppermute x24 -> x20, starting transfers between devices: 30.5 us -> 20 us  [move(): return lax.ppermute(a, axis, [(i, (i + by) % n) for i in range(n)])]
    ppermute x4, waiting for transfers between devices: 8.64 us -> 0.09 us  [move2(): return lax.ppermute(a, ('z', 'xh'), pairs)]
    ppermute x24, waiting for transfers between devices: 39.8 us -> 37.7 us  [step(): return lax.ppermute(a, ('y', 'core'), pairs)]
    ppermute x24, starting transfers between devices: 32.4 us -> 30.2 us  [step(): return lax.ppermute(a, ('y', 'core'), pairs)]
    pallas_call x34 -> x30, Pallas kernels: 33.9 us -> 32 us  [call(): pl.pallas_call(kernel, in_specs=[smem] + [in_space] * n + [anywhere] * m,...]
  transfers between devices with their start and end apart: 52 -> 48, of which waited for: 24 -> 24; matrix products, arithmetic and copies ran while one was open for 0% -> 0% of each run, Pallas kernels for 20% -> 23%
where the time goes in v3:
time: 178 us; the launch traced here: 177 us
  waiting for transfers between devices  65.4 us (37%)
  starting transfers between devices  60.7 us (34%)
  Pallas kernels  43.4 us (24%)
  local copies, waits for them, and re-layouts  6.33 us (4%)
    ppermute x24, waiting for transfers between devices, step(): return lax.ppermute(a, ('y', 'core'), pairs)  37.7 us
    pallas_call x30, Pallas kernels, call(): pl.pallas_call(kernel, in_specs=[smem] + [in_space] * n + [anywhere] * m,...  32 us
    ppermute x24, starting transfers between devices, step(): return lax.ppermute(a, ('y', 'core'), pairs)  30.2 us
    ppermute x20, waiting for transfers between devices, move(): return lax.ppermute(a, axis, [(i, (i + by) % n) for i in range(n)])  27.6 us
    ppermute x20, starting transfers between devices, move(): return lax.ppermute(a, axis, [(i, (i + by) % n) for i in range(n)])  20 us
    ppermute x4, starting transfers between devices, move2(): return lax.ppermute(a, ('z', 'xh'), pairs)  10.5 us
    pallas_call x2, Pallas kernels, weight_grads(): pl.pallas_call(kernel, in_specs=[smem] + [vmem] * given + [anywhere] * (l...  10.2 us
    unnamed x16, local copies, waits for them, and re-layouts  6.33 us
  transfers between devices with their start and end apart: 48, of which 24 were waited for; matrix products, arithmetic and copies ran while one was open for 0% of the time, Pallas kernels for 23%

profile of v3, /device:TPU:0, one launch (start us, length us, event | category | flops | bytes accessed | tf_op | source)
XLA Modules:
  0.0 177.0 jit_solution(11926877961318368499)
XLA Ops:
  3.4 3.2 %collective-permute-start = (bf16[128,1024]{1,0:T(8,128)(2,1)S(1)}, bf16[128,1024]{1,0:T(8,128)(2,1)S(1)}, u32[]{:S(2)}, u32[]{:S(2)}) collective-permute-start(bf16[128,1024]{1,0:T(8,128)(2,1)S(1)} %rows.1.refs_1_.r_4_), channel_id=1, source_target_pairs={{0,16},{16,0},{1,17},{17,1},{2,18},{18,2},{3,19},{19,3},{4,20},{20... | collective-permute-start | bytes 786440 | tf_op jit(solution)/shard_map/ppermute | solution.py:36
  13.7 2.1 %collective-permute-start.6 = (bf16[256,1024]{1,0:T(8,128)(2,1)S(1)}, bf16[256,1024]{1,0:T(8,128)(2,1)S(1)}, u32[]{:S(2)}, u32[]{:S(2)}) collective-permute-start(bf16[256,1024]{1,0:T(8,128)(2,1)S(1)} %get-tuple-element.52.refs_1_.refs_5_), channel_id=1, source_target_pairs={{0,32},{32,64},{64,96},{96,0},{1,33},{33,65},{65,97},{97,1},{2,34}... | collective-permute-start | bytes 1572872 | tf_op jit(solution)/shard_map/ppermute | solution.py:36
  15.9 2.2 %collective-permute-start.5 = (bf16[256,1024]{1,0:T(8,128)(2,1)S(1)}, bf16[256,1024]{1,0:T(8,128)(2,1)S(1)}, u32[]{:S(2)}, u32[]{:S(2)}) collective-permute-start(bf16[256,1024]{1,0:T(8,128)(2,1)S(1)} %get-tuple-element.52.refs_1_.refs_5_), channel_id=1, source_target_pairs={{0,96},{32,0},{64,32},{96,64},{1,97},{33,1},{65,33},{97,65},{2,98}... | collective-permute-start | bytes 1572872 | tf_op jit(solution)/shard_map/ppermute | solution.py:36
  18.4 2.4 %forward.4 = (f32[64,2688]{1,0:T(8,128)S(1)}, f32[64,2688]{1,0:T(8,128)S(1)}, bf16[64,2688]{1,0:T(8,128)(2,1)S(1)}, bf16[64,2688]{1,0:T(8,128)(2,1)S(1)}) custom-call(s32[3]{0:T(128)S(1)} %pad_add_fusion.refs_0_.r_0_, bf16[256,1024]{1,0:T(8,128)(2,1)S(1)} %get-tuple-element.52.refs_1_.refs_5_, bf16[256,1024]{1,0:T(8,128)(2,1)S(1)} %collective-permute-done.1.refs_2_, ...), custom_call_target="tpu_custom_call" | custom-call | tf_op jit(solution)/shard_map/forward/pallas_call | solution.py:63
  22.4 8.1 %collective-permute-done.6.refs_1_ = bf16[256,1024]{1,0:T(8,128)(2,1)S(1)} collective-permute-done((bf16[256,1024]{1,0:T(8,128)(2,1)S(1)}, bf16[256,1024]{1,0:T(8,128)(2,1)S(1)}, u32[]{:S(2)}, u32[]{:S(2)}) %collective-permute-start.6) | collective-permute-done | bytes 524320 | tf_op jit(solution)/shard_map/ppermute | solution.py:36
  34.2 3.0 %collective-permute-start.3 = (bf16[64,2688]{1,0:T(8,128)(2,1)S(1)}, bf16[64,2688]{1,0:T(8,128)(2,1)S(1)}, u32[]{:S(2)}, u32[]{:S(2)}) collective-permute-start(bf16[64,2688]{1,0:T(8,128)(2,1)S(1)} %get-tuple-element.55), channel_id=1, source_target_pairs={{0,12},{4,0},{8,4},{12,8},{1,5},{5,9},{9,13},{13,1},{2,14},{6,2},{... | collective-permute-start | bytes 1032200 | tf_op jit(solution)/shard_map/ppermute | solution.py:47
  37.9 2.3 %forward.5 = (f32[64,2688]{1,0:T(8,128)S(1)}, f32[64,2688]{1,0:T(8,128)S(1)}, bf16[64,2688]{1,0:T(8,128)(2,1)S(1)}, bf16[64,2688]{1,0:T(8,128)(2,1)S(1)}) custom-call(s32[3]{0:T(128)S(1)} %pad_add_fusion.refs_0_.r_0_, bf16[256,1024]{1,0:T(8,128)(2,1)S(1)} %get-tuple-element.58.refs_2_.refs_1_.refs_6_, bf16[256,1024]{1,0:T(8,128)(2,1)S(1)} %collective-permute-done.8.refs_2_, ...), custom_call_target="tpu_custom_call" | custom-call | tf_op jit(solution)/shard_map/forward/pallas_call | solution.py:63
  40.3 5.3 %collective-permute-done.3.refs_2_ = bf16[64,2688]{1,0:T(8,128)(2,1)S(1)} collective-permute-done((bf16[64,2688]{1,0:T(8,128)(2,1)S(1)}, bf16[64,2688]{1,0:T(8,128)(2,1)S(1)}, u32[]{:S(2)}, u32[]{:S(2)}) %collective-permute-start.3) | collective-permute-done | bytes 344096 | tf_op jit(solution)/shard_map/ppermute | solution.py:47
  48.6 2.4 %forward.6 = (f32[64,2688]{1,0:T(8,128)S(1)}, f32[64,2688]{1,0:T(8,128)S(1)}, bf16[64,2688]{1,0:T(8,128)(2,1)S(1)}, bf16[64,2688]{1,0:T(8,128)(2,1)S(1)}) custom-call(s32[3]{0:T(128)S(1)} %pad_add_fusion.refs_0_.r_0_, bf16[256,1024]{1,0:T(8,128)(2,1)S(1)} %get-tuple-element.59.refs_3_.refs_1_.refs_7_, bf16[256,1024]{1,0:T(8,128)(2,1)S(1)} %collective-permute-done.12.refs_2_, ...), custom_call_target="tpu_custom_call" | custom-call | tf_op jit(solution)/shard_map/forward/pallas_call | solution.py:63
  51.6 2.4 %collective-permute-start.16 = (bf16[256,1024]{1,0:T(8,128)(2,1)S(1)}, bf16[256,1024]{1,0:T(8,128)(2,1)S(1)}, u32[]{:S(2)}, u32[]{:S(2)}) collective-permute-start(bf16[256,1024]{1,0:T(8,128)(2,1)S(1)} %get-tuple-element.67), channel_id=1, source_target_pairs={{0,1},{1,0},{2,3},{3,2},{4,5},{5,4},{6,7},{7,6},{8,9},{9,8},{10,11... | collective-permute-start | bytes 1572872 | tf_op jit(solution)/shard_map/ppermute | solution.py:36
  54.0 3.2 %collective-permute-start.22 = (bf16[64,2688]{1,0:T(8,128)(2,1)S(1)}, bf16[64,2688]{1,0:T(8,128)(2,1)S(1)}, u32[]{:S(2)}, u32[]{:S(2)}) collective-permute-start(bf16[64,2688]{1,0:T(8,128)(2,1)S(1)} %get-tuple-element.75), channel_id=1, source_target_pairs={{0,12},{4,0},{8,4},{12,8},{1,5},{5,9},{9,13},{13,1},{2,14},{6,2},{... | collective-permute-start | bytes 1032200 | tf_op jit(solution)/shard_map/ppermute | solution.py:47
  57.9 5.7 %collective-permute-done.9.refs_2_ = f32[64,2688]{1,0:T(8,128)S(1)} collective-permute-done((f32[64,2688]{1,0:T(8,128)S(1)}, f32[64,2688]{1,0:T(8,128)S(1)}, u32[]{:S(2)}, u32[]{:S(2)}) %collective-permute-start.9) | collective-permute-done | bytes 688160 | tf_op jit(solution)/shard_map/ppermute | solution.py:36
  63.6 3.7 %collective-permute-start.20 = (bf16[64,2688]{1,0:T(8,128)(2,1)S(1)}, bf16[64,2688]{1,0:T(8,128)(2,1)S(1)}, u32[]{:S(2)}, u32[]{:S(2)}) collective-permute-start(bf16[64,2688]{1,0:T(8,128)(2,1)S(1)} %get-tuple-element.74), channel_id=1, source_target_pairs={{0,12},{4,0},{8,4},{12,8},{1,5},{5,9},{9,13},{13,1},{2,14},{6,2},{... | collective-permute-start | bytes 1032200 | tf_op jit(solution)/shard_map/ppermute | solution.py:47
  68.9 2.4 %forward.7 = (f32[64,2688]{1,0:T(8,128)S(1)}, f32[64,2688]{1,0:T(8,128)S(1)}, bf16[64,2688]{1,0:T(8,128)(2,1)S(1)}, bf16[64,2688]{1,0:T(8,128)(2,1)S(1)}) custom-call(s32[3]{0:T(128)S(1)} %pad_add_fusion.refs_0_.r_0_, bf16[256,1024]{1,0:T(8,128)(2,1)S(1)} %get-tuple-element.66.refs_3_.refs_1_.refs_8_, bf16[256,1024]{1,0:T(8,128)(2,1)S(1)} %collective-permute-done.16.refs_2_, ...), custom_call_target="tpu_custom_call" | custom-call | tf_op jit(solution)/shard_map/forward/pallas_call | solution.py:63
  75.7 3.7 %collective-permute-start.18 = (bf16[64,2688]{1,0:T(8,128)(2,1)S(1)}, bf16[64,2688]{1,0:T(8,128)(2,1)S(1)}, u32[]{:S(2)}, u32[]{:S(2)}) collective-permute-start(bf16[64,2688]{1,0:T(8,128)(2,1)S(1)} %get-tuple-element.71), channel_id=1, source_target_pairs={{0,12},{4,0},{8,4},{12,8},{1,5},{5,9},{9,13},{13,1},{2,14},{6,2},{... | collective-permute-start | bytes 1032200 | tf_op jit(solution)/shard_map/ppermute | solution.py:47
  80.1 5.1 %collective-permute-done.19.refs_2_ = bf16[64,2688]{1,0:T(8,128)(2,1)S(1)} collective-permute-done((bf16[64,2688]{1,0:T(8,128)(2,1)S(1)}, bf16[64,2688]{1,0:T(8,128)(2,1)S(1)}, u32[]{:S(2)}, u32[]{:S(2)}) %collective-permute-start.19) | collective-permute-done | bytes 344096 | tf_op jit(solution)/shard_map/ppermute | solution.py:47
  85.9 3.2 %collective-permute-start.13 = (bf16[64,2688]{1,0:T(8,128)(2,1)S(1)}, bf16[64,2688]{1,0:T(8,128)(2,1)S(1)}, u32[]{:S(2)}, u32[]{:S(2)}) collective-permute-start(bf16[64,2688]{1,0:T(8,128)(2,1)S(1)} %activate.4.refs_3_.refs_1_), channel_id=1, source_target_pairs={{0,12},{4,0},{8,4},{12,8},{1,5},{5,9},{9,13},{13,1},{2,14},{6,2},{... | collective-permute-start | bytes 1032200 | tf_op jit(solution)/shard_map/ppermute | solution.py:47
  93.9 2.3 %collective-permute-done.24.refs_3_ = bf16[64,2688]{1,0:T(8,128)(2,1)S(1)} collective-permute-done((bf16[64,2688]{1,0:T(8,128)(2,1)S(1)}, bf16[64,2688]{1,0:T(8,128)(2,1)S(1)}, u32[]{:S(2)}, u32[]{:S(2)}) %collective-permute-start.24) | collective-permute-done | bytes 344096 | tf_op jit(solution)/shard_map/ppermute | solution.py:47
  97.6 2.3 %collective-permute-done.15.refs_3_ = bf16[64,2688]{1,0:T(8,128)(2,1)S(1)} collective-permute-done((bf16[64,2688]{1,0:T(8,128)(2,1)S(1)}, bf16[64,2688]{1,0:T(8,128)(2,1)S(1)}, u32[]{:S(2)}, u32[]{:S(2)}) %collective-permute-start.15) | collective-permute-done | bytes 344096 | tf_op jit(solution)/shard_map/ppermute | solution.py:47
  106.7 4.7 %collective-permute-done.27.refs_2_ = bf16[64,2688]{1,0:T(8,128)(2,1)S(1)} collective-permute-done((bf16[64,2688]{1,0:T(8,128)(2,1)S(1)}, bf16[64,2688]{1,0:T(8,128)(2,1)S(1)}, u32[]{:S(2)}, u32[]{:S(2)}) %collective-permute-start.27) | collective-permute-done | bytes 344096 | tf_op jit(solution)/shard_map/ppermute | solution.py:47
  115.2 6.7 %collective-permute-done.35.refs_2_ = f32[64,2688]{1,0:T(8,128)S(1)} collective-permute-done((f32[64,2688]{1,0:T(8,128)S(1)}, f32[64,2688]{1,0:T(8,128)S(1)}, u32[]{:S(2)}, u32[]{:S(2)}) %collective-permute-start.35) | collective-permute-done | bytes 688160 | tf_op jit(solution)/shard_map/ppermute | solution.py:36
  122.6 3.2 %collective-permute-start.32 = (bf16[64,2688]{1,0:T(8,128)(2,1)S(1)}, bf16[64,2688]{1,0:T(8,128)(2,1)S(1)}, u32[]{:S(2)}, u32[]{:S(2)}) collective-permute-start(bf16[64,2688]{1,0:T(8,128)(2,1)S(1)} %activate.6.refs_5_.refs_1_), channel_id=1, source_target_pairs={{0,12},{4,0},{8,4},{12,8},{1,5},{5,9},{9,13},{13,1},{2,14},{6,2},{... | collective-permute-start | bytes 1032200 | tf_op jit(solution)/shard_map/ppermute | solution.py:47
  125.9 3.2 %collective-permute-start.39 = (bf16[64,2688]{1,0:T(8,128)(2,1)S(1)}, bf16[64,2688]{1,0:T(8,128)(2,1)S(1)}, u32[]{:S(2)}, u32[]{:S(2)}) collective-permute-start(bf16[64,2688]{1,0:T(8,128)(2,1)S(1)} %activate.7.refs_5_.refs_1_), channel_id=1, source_target_pairs={{0,12},{4,0},{8,4},{12,8},{1,5},{5,9},{9,13},{13,1},{2,14},{6,2},{... | collective-permute-start | bytes 1032200 | tf_op jit(solution)/shard_map/ppermute | solution.py:47
  129.1 5.6 %collective-permute-done.40.refs_4_ = bf16[64,2688]{1,0:T(8,128)(2,1)S(1)} collective-permute-done((bf16[64,2688]{1,0:T(8,128)(2,1)S(1)}, bf16[64,2688]{1,0:T(8,128)(2,1)S(1)}, u32[]{:S(2)}, u32[]{:S(2)}) %collective-permute-start.40) | collective-permute-done | bytes 344096 | tf_op jit(solution)/shard_map/ppermute | solution.py:47
  134.7 2.5 %collective-permute-start.36 = (bf16[128,512]{1,0:T(8,128)(2,1)S(1)}, bf16[128,512]{1,0:T(8,128)(2,1)S(1)}, u32[]{:S(2)}, u32[]{:S(2)}) collective-permute-start(bf16[128,512]{1,0:T(8,128)(2,1)S(1)} %get-tuple-element.82), channel_id=1, source_target_pairs={{0,16},{16,0},{32,48},{48,32},{64,80},{80,64},{96,112},{112,96},{1... | collective-permute-start | bytes 393224 | tf_op jit(solution)/shard_map/ppermute | solution.py:41
  137.3 4.0 %collective-permute-done.34.refs_3_ = bf16[64,2688]{1,0:T(8,128)(2,1)S(1)} collective-permute-done((bf16[64,2688]{1,0:T(8,128)(2,1)S(1)}, bf16[64,2688]{1,0:T(8,128)(2,1)S(1)}, u32[]{:S(2)}, u32[]{:S(2)}) %collective-permute-start.34) | collective-permute-done | bytes 344096 | tf_op jit(solution)/shard_map/ppermute | solution.py:47
  145.8 3.2 %collective-permute-start.44 = (bf16[128,512]{1,0:T(8,128)(2,1)S(1)}, bf16[128,512]{1,0:T(8,128)(2,1)S(1)}, u32[]{:S(2)}, u32[]{:S(2)}) collective-permute-start(bf16[128,512]{1,0:T(8,128)(2,1)S(1)} %get-tuple-element.88), channel_id=1, source_target_pairs={{0,112},{16,96},{32,16},{48,0},{64,48},{80,32},{96,80},{112,64},{1... | collective-permute-start | bytes 393224 | tf_op jit(solution)/shard_map/ppermute | solution.py:41
  154.2 2.7 %collective-permute-done.37.refs_10_.refs_2_ = bf16[128,512]{1,0:T(8,128)(2,1)S(1)} collective-permute-done((bf16[128,512]{1,0:T(8,128)(2,1)S(1)}, bf16[128,512]{1,0:T(8,128)(2,1)S(1)}, u32[]{:S(2)}, u32[]{:S(2)}) %collective-permute-start.37) | collective-permute-done | bytes 131104 | tf_op jit(solution)/shard_map/ppermute | solution.py:36
  156.9 5.1 %weight_grads.2 = (bf16[512,1792]{1,0:T(8,128)(2,1)}, bf16[512,1792]{1,0:T(8,128)(2,1)}, bf16[1792,512]{1,0:T(8,128)(2,1)}, f32[8,128]{1,0:T(8,128)S(1)}) custom-call(s32[3]{0:T(128)S(1)} %pad_add_fusion.refs_0_.r_0_, bf16[256,2688]{1,0:T(8,128)(2,1)S(1)} %get-tuple-element.76.refs_3_.refs_1_, ...), custom_call_target="tpu_custom_call" | custom-call | tf_op jit(solution)/shard_map/weight_grads/pallas_call | solution.py:264
  163.9 2.8 %collective-permute-start.47 = (bf16[128,512]{1,0:T(8,128)(2,1)S(1)}, bf16[128,512]{1,0:T(8,128)(2,1)S(1)}, u32[]{:S(2)}, u32[]{:S(2)}) collective-permute-start(bf16[128,512]{1,0:T(8,128)(2,1)S(1)} %get-tuple-element.92), channel_id=1, source_target_pairs={{0,80},{16,64},{32,112},{48,96},{64,16},{80,0},{96,48},{112,32},{1... | collective-permute-start | bytes 393224 | tf_op jit(solution)/shard_map/ppermute | solution.py:41
  168.2 5.1 %weight_grads.3 = (bf16[512,1792]{1,0:T(8,128)(2,1)}, bf16[512,1792]{1,0:T(8,128)(2,1)}, bf16[1792,512]{1,0:T(8,128)(2,1)}, f32[8,128]{1,0:T(8,128)S(1)}) custom-call(s32[3]{0:T(128)S(1)} %pad_add_fusion.refs_0_.r_0_, bf16[256,2688]{1,0:T(8,128)(2,1)S(1)} %collective-permute-done.26.refs_2_.refs_1_, ...), custom_call_target="tpu_custom_call", output_to_operand_aliasing={{0}: (9, {}), {1}: (10, {}), {2}: (11, {})} | custom-call | tf_op jit(solution)/shard_map/weight_grads/pallas_call | solution.py:264
  173.4 2.3 %collective-permute-done.45.refs_4_ = bf16[128,512]{1,0:T(8,128)(2,1)S(1)} collective-permute-done((bf16[128,512]{1,0:T(8,128)(2,1)S(1)}, bf16[128,512]{1,0:T(8,128)(2,1)S(1)}, u32[]{:S(2)}, u32[]{:S(2)}) %collective-permute-start.45) | collective-permute-done | bytes 131104 | tf_op jit(solution)/shard_map/ppermute | solution.py:36
  (114 shorter events, 59.7 us)
Async XLA Ops:
  13.7 16.8 %collective-permute-start.6 = (bf16[256,1024]{1,0:T(8,128)(2,1)S(1)}, bf16[256,1024]{1,0:T(8,128)(2,1)S(1)}, u32[]{:S(2)}, u32[]{:S(2)}) collective-permute-start(bf16[256,1024]{1,0:T(8,128)(2,1)S(1)} %get-tuple-element.52.refs_1_.refs_5_), channel_id=1, source_target_pairs={{0,32},{32,64},{64,96},{96,0},{1,33},{33,65},{65,97},{97,1},{2,34}... | collective-permute-start | bytes 1572872 | tf_op jit(solution)/shard_map/ppermute | solution.py:36
  15.9 15.3 %collective-permute-start.5 = (bf16[256,1024]{1,0:T(8,128)(2,1)S(1)}, bf16[256,1024]{1,0:T(8,128)(2,1)S(1)}, u32[]{:S(2)}, u32[]{:S(2)}) collective-permute-start(bf16[256,1024]{1,0:T(8,128)(2,1)S(1)} %get-tuple-element.52.refs_1_.refs_5_), channel_id=1, source_target_pairs={{0,96},{32,0},{64,32},{96,64},{1,97},{33,1},{65,33},{97,65},{2,98}... | collective-permute-start | bytes 1572872 | tf_op jit(solution)/shard_map/ppermute | solution.py:36
  20.7 16.5 %collective-permute-start.4 = (bf16[64,2688]{1,0:T(8,128)(2,1)S(1)}, bf16[64,2688]{1,0:T(8,128)(2,1)S(1)}, u32[]{:S(2)}, u32[]{:S(2)}) collective-permute-start(bf16[64,2688]{1,0:T(8,128)(2,1)S(1)} %get-tuple-element.57), channel_id=1, source_target_pairs={{0,4},{4,8},{8,12},{12,0},{1,13},{5,1},{9,5},{13,9},{2,6},{6,10},{... | collective-permute-start | bytes 1032200 | tf_op jit(solution)/shard_map/ppermute | solution.py:47
  31.8 16.8 %collective-permute-start.12 = (bf16[256,1024]{1,0:T(8,128)(2,1)S(1)}, bf16[256,1024]{1,0:T(8,128)(2,1)S(1)}, u32[]{:S(2)}, u32[]{:S(2)}) collective-permute-start(bf16[256,1024]{1,0:T(8,128)(2,1)S(1)} %get-tuple-element.64), channel_id=1, source_target_pairs={{0,1},{1,0},{2,3},{3,2},{4,5},{5,4},{6,7},{7,6},{8,9},{9,8},{10,11... | collective-permute-start | bytes 1572872 | tf_op jit(solution)/shard_map/ppermute | solution.py:36
  32.4 18.6 %collective-permute-start.11 = (bf16[256,1024]{1,0:T(8,128)(2,1)S(1)}, bf16[256,1024]{1,0:T(8,128)(2,1)S(1)}, u32[]{:S(2)}, u32[]{:S(2)}) collective-permute-start(bf16[256,1024]{1,0:T(8,128)(2,1)S(1)} %get-tuple-element.52.refs_1_.refs_5_), channel_id=1, source_target_pairs={{0,64},{32,96},{64,0},{96,32},{1,65},{33,97},{65,1},{97,33},{2,66}... | collective-permute-start | bytes 1572872 | tf_op jit(solution)/shard_map/ppermute | solution.py:36
  34.2 11.3 %collective-permute-start.3 = (bf16[64,2688]{1,0:T(8,128)(2,1)S(1)}, bf16[64,2688]{1,0:T(8,128)(2,1)S(1)}, u32[]{:S(2)}, u32[]{:S(2)}) collective-permute-start(bf16[64,2688]{1,0:T(8,128)(2,1)S(1)} %get-tuple-element.55), channel_id=1, source_target_pairs={{0,12},{4,0},{8,4},{12,8},{1,5},{5,9},{9,13},{13,1},{2,14},{6,2},{... | collective-permute-start | bytes 1032200 | tf_op jit(solution)/shard_map/ppermute | solution.py:47
  47.0 16.6 %collective-permute-start.9 = (f32[64,2688]{1,0:T(8,128)S(1)}, f32[64,2688]{1,0:T(8,128)S(1)}, u32[]{:S(2)}, u32[]{:S(2)}) collective-permute-start(f32[64,2688]{1,0:T(8,128)S(1)} %beside.4.refs_7_.refs_1_), channel_id=1, source_target_pairs={{0,2},{2,0},{1,3},{3,1},{4,6},{6,4},{5,7},{7,5},{8,10},{10,8},{9,1... | collective-permute-start | bytes 2064392 | tf_op jit(solution)/shard_map/ppermute | solution.py:36
  51.6 17.3 %collective-permute-start.16 = (bf16[256,1024]{1,0:T(8,128)(2,1)S(1)}, bf16[256,1024]{1,0:T(8,128)(2,1)S(1)}, u32[]{:S(2)}, u32[]{:S(2)}) collective-permute-start(bf16[256,1024]{1,0:T(8,128)(2,1)S(1)} %get-tuple-element.67), channel_id=1, source_target_pairs={{0,1},{1,0},{2,3},{3,2},{4,5},{5,4},{6,7},{7,6},{8,9},{9,8},{10,11... | collective-permute-start | bytes 1572872 | tf_op jit(solution)/shard_map/ppermute | solution.py:36
  54.0 14.0 %collective-permute-start.17 = (bf16[64,2688]{1,0:T(8,128)(2,1)S(1)}, bf16[64,2688]{1,0:T(8,128)(2,1)S(1)}, u32[]{:S(2)}, u32[]{:S(2)}) collective-permute-start(bf16[64,2688]{1,0:T(8,128)(2,1)S(1)} %get-tuple-element.69), channel_id=1, source_target_pairs={{0,4},{4,8},{8,12},{12,0},{1,13},{5,1},{9,5},{13,9},{2,6},{6,10},{... | collective-permute-start | bytes 1032200 | tf_op jit(solution)/shard_map/ppermute | solution.py:47
  54.0 17.3 %collective-permute-start.22 = (bf16[64,2688]{1,0:T(8,128)(2,1)S(1)}, bf16[64,2688]{1,0:T(8,128)(2,1)S(1)}, u32[]{:S(2)}, u32[]{:S(2)}) collective-permute-start(bf16[64,2688]{1,0:T(8,128)(2,1)S(1)} %get-tuple-element.75), channel_id=1, source_target_pairs={{0,12},{4,0},{8,4},{12,8},{1,5},{5,9},{9,13},{13,1},{2,14},{6,2},{... | collective-permute-start | bytes 1032200 | tf_op jit(solution)/shard_map/ppermute | solution.py:47
  57.8 14.5 %collective-permute-start.23 = (bf16[64,2688]{1,0:T(8,128)(2,1)S(1)}, bf16[64,2688]{1,0:T(8,128)(2,1)S(1)}, u32[]{:S(2)}, u32[]{:S(2)}) collective-permute-start(bf16[64,2688]{1,0:T(8,128)(2,1)S(1)} %add.9.refs_3_), channel_id=1, source_target_pairs={{0,4},{4,8},{8,12},{12,0},{1,13},{5,1},{9,5},{13,9},{2,6},{6,10},{... | collective-permute-start | bytes 1032200 | tf_op jit(solution)/shard_map/ppermute | solution.py:47
  63.6 12.1 %collective-permute-start.20 = (bf16[64,2688]{1,0:T(8,128)(2,1)S(1)}, bf16[64,2688]{1,0:T(8,128)(2,1)S(1)}, u32[]{:S(2)}, u32[]{:S(2)}) collective-permute-start(bf16[64,2688]{1,0:T(8,128)(2,1)S(1)} %get-tuple-element.74), channel_id=1, source_target_pairs={{0,12},{4,0},{8,4},{12,8},{1,5},{5,9},{9,13},{13,1},{2,14},{6,2},{... | collective-permute-start | bytes 1032200 | tf_op jit(solution)/shard_map/ppermute | solution.py:47
  68.6 10.8 %collective-permute-start.21 = (bf16[64,2688]{1,0:T(8,128)(2,1)S(1)}, bf16[64,2688]{1,0:T(8,128)(2,1)S(1)}, u32[]{:S(2)}, u32[]{:S(2)}) collective-permute-start(bf16[64,2688]{1,0:T(8,128)(2,1)S(1)} %add.10.refs_7_), channel_id=1, source_target_pairs={{0,4},{4,8},{8,12},{12,0},{1,13},{5,1},{9,5},{13,9},{2,6},{6,10},{... | collective-permute-start | bytes 1032200 | tf_op jit(solution)/shard_map/ppermute | solution.py:47
  72.9 17.9 %collective-permute-start.25 = (f32[64,2688]{1,0:T(8,128)S(1)}, f32[64,2688]{1,0:T(8,128)S(1)}, u32[]{:S(2)}, u32[]{:S(2)}) collective-permute-start(f32[64,2688]{1,0:T(8,128)S(1)} %beside.5.refs_4_.refs_1_), channel_id=1, source_target_pairs={{0,2},{2,0},{1,3},{3,1},{4,6},{6,4},{5,7},{7,5},{8,10},{10,8},{9,1... | collective-permute-start | bytes 2064392 | tf_op jit(solution)/shard_map/ppermute | solution.py:36
  73.5 11.7 %collective-permute-start.19 = (bf16[64,2688]{1,0:T(8,128)(2,1)S(1)}, bf16[64,2688]{1,0:T(8,128)(2,1)S(1)}, u32[]{:S(2)}, u32[]{:S(2)}) collective-permute-start(bf16[64,2688]{1,0:T(8,128)(2,1)S(1)} %get-tuple-element.73), channel_id=1, source_target_pairs={{0,4},{4,8},{8,12},{12,0},{1,13},{5,1},{9,5},{13,9},{2,6},{6,10},{... | collective-permute-start | bytes 1032200 | tf_op jit(solution)/shard_map/ppermute | solution.py:47
  73.5 17.3 %collective-permute-start.14 = (bf16[64,2688]{1,0:T(8,128)(2,1)S(1)}, bf16[64,2688]{1,0:T(8,128)(2,1)S(1)}, u32[]{:S(2)}, u32[]{:S(2)}) collective-permute-start(bf16[64,2688]{1,0:T(8,128)(2,1)S(1)} %activate.4.refs_3_.refs_1_), channel_id=1, source_target_pairs={{0,4},{4,8},{8,12},{12,0},{1,13},{5,1},{9,5},{13,9},{2,6},{6,10},{... | collective-permute-start | bytes 1032200 | tf_op jit(solution)/shard_map/ppermute | solution.py:47
  75.7 16.4 %collective-permute-start.18 = (bf16[64,2688]{1,0:T(8,128)(2,1)S(1)}, bf16[64,2688]{1,0:T(8,128)(2,1)S(1)}, u32[]{:S(2)}, u32[]{:S(2)}) collective-permute-start(bf16[64,2688]{1,0:T(8,128)(2,1)S(1)} %get-tuple-element.71), channel_id=1, source_target_pairs={{0,12},{4,0},{8,4},{12,8},{1,5},{5,9},{9,13},{13,1},{2,14},{6,2},{... | collective-permute-start | bytes 1032200 | tf_op jit(solution)/shard_map/ppermute | solution.py:47
  85.9 11.7 %collective-permute-start.13 = (bf16[64,2688]{1,0:T(8,128)(2,1)S(1)}, bf16[64,2688]{1,0:T(8,128)(2,1)S(1)}, u32[]{:S(2)}, u32[]{:S(2)}) collective-permute-start(bf16[64,2688]{1,0:T(8,128)(2,1)S(1)} %activate.4.refs_3_.refs_1_), channel_id=1, source_target_pairs={{0,12},{4,0},{8,4},{12,8},{1,5},{5,9},{9,13},{13,1},{2,14},{6,2},{... | collective-permute-start | bytes 1032200 | tf_op jit(solution)/shard_map/ppermute | solution.py:47
  90.8 15.2 %collective-permute-start.30 = (f32[64,2688]{1,0:T(8,128)S(1)}, f32[64,2688]{1,0:T(8,128)S(1)}, u32[]{:S(2)}, u32[]{:S(2)}) collective-permute-start(f32[64,2688]{1,0:T(8,128)S(1)} %beside.6.refs_3_.refs_1_), channel_id=1, source_target_pairs={{0,2},{2,0},{1,3},{3,1},{4,6},{6,4},{5,7},{7,5},{8,10},{10,8},{9,1... | collective-permute-start | bytes 2064392 | tf_op jit(solution)/shard_map/ppermute | solution.py:36
  92.1 11.5 %collective-permute-start.28 = (bf16[64,2688]{1,0:T(8,128)(2,1)S(1)}, bf16[64,2688]{1,0:T(8,128)(2,1)S(1)}, u32[]{:S(2)}, u32[]{:S(2)}) collective-permute-start(bf16[64,2688]{1,0:T(8,128)(2,1)S(1)} %activate.5.refs_4_.refs_1_), channel_id=1, source_target_pairs={{0,4},{4,8},{8,12},{12,0},{1,13},{5,1},{9,5},{13,9},{2,6},{6,10},{... | collective-permute-start | bytes 1032200 | tf_op jit(solution)/shard_map/ppermute | solution.py:47
  100.6 12.7 %collective-permute-start.26 = (bf16[256,2688]{1,0:T(8,128)(2,1)S(1)}, bf16[256,2688]{1,0:T(8,128)(2,1)S(1)}, u32[]{:S(2)}, u32[]{:S(2)}) collective-permute-start(bf16[256,2688]{1,0:T(8,128)(2,1)S(1)} %get-tuple-element.77), channel_id=1, source_target_pairs={{0,1},{1,0},{2,3},{3,2},{4,5},{5,4},{6,7},{7,6},{8,9},{9,8},{10,11... | collective-permute-start | bytes 4128776 | tf_op jit(solution)/shard_map/ppermute | solution.py:36
  100.7 10.6 %collective-permute-start.27 = (bf16[64,2688]{1,0:T(8,128)(2,1)S(1)}, bf16[64,2688]{1,0:T(8,128)(2,1)S(1)}, u32[]{:S(2)}, u32[]{:S(2)}) collective-permute-start(bf16[64,2688]{1,0:T(8,128)(2,1)S(1)} %activate.5.refs_4_.refs_1_), channel_id=1, source_target_pairs={{0,12},{4,0},{8,4},{12,8},{1,5},{5,9},{9,13},{13,1},{2,14},{6,2},{... | collective-permute-start | bytes 1032200 | tf_op jit(solution)/shard_map/ppermute | solution.py:47
  103.6 18.2 %collective-permute-start.35 = (f32[64,2688]{1,0:T(8,128)S(1)}, f32[64,2688]{1,0:T(8,128)S(1)}, u32[]{:S(2)}, u32[]{:S(2)}) collective-permute-start(f32[64,2688]{1,0:T(8,128)S(1)} %beside.7.refs_5_.refs_1_), channel_id=1, source_target_pairs={{0,2},{2,0},{1,3},{3,1},{4,6},{6,4},{5,7},{7,5},{8,10},{10,8},{9,1... | collective-permute-start | bytes 2064392 | tf_op jit(solution)/shard_map/ppermute | solution.py:36
  113.1 29.2 %collective-permute-start.31 = (bf16[256,2688]{1,0:T(8,128)(2,1)S(1)}, bf16[256,2688]{1,0:T(8,128)(2,1)S(1)}, u32[]{:S(2)}, u32[]{:S(2)}) collective-permute-start(bf16[256,2688]{1,0:T(8,128)(2,1)S(1)} %get-tuple-element.80), channel_id=1, source_target_pairs={{0,1},{1,0},{2,3},{3,2},{4,5},{5,4},{6,7},{7,6},{8,9},{9,8},{10,11... | collective-permute-start | bytes 4128776 | tf_op jit(solution)/shard_map/ppermute | solution.py:36
  113.2 12.6 %collective-permute-start.33 = (bf16[64,2688]{1,0:T(8,128)(2,1)S(1)}, bf16[64,2688]{1,0:T(8,128)(2,1)S(1)}, u32[]{:S(2)}, u32[]{:S(2)}) collective-permute-start(bf16[64,2688]{1,0:T(8,128)(2,1)S(1)} %activate.6.refs_5_.refs_1_), channel_id=1, source_target_pairs={{0,4},{4,8},{8,12},{12,0},{1,13},{5,1},{9,5},{13,9},{2,6},{6,10},{... | collective-permute-start | bytes 1032200 | tf_op jit(solution)/shard_map/ppermute | solution.py:47
  122.5 12.2 %collective-permute-start.40 = (bf16[64,2688]{1,0:T(8,128)(2,1)S(1)}, bf16[64,2688]{1,0:T(8,128)(2,1)S(1)}, u32[]{:S(2)}, u32[]{:S(2)}) collective-permute-start(bf16[64,2688]{1,0:T(8,128)(2,1)S(1)} %activate.7.refs_5_.refs_1_), channel_id=1, source_target_pairs={{0,4},{4,8},{8,12},{12,0},{1,13},{5,1},{9,5},{13,9},{2,6},{6,10},{... | collective-permute-start | bytes 1032200 | tf_op jit(solution)/shard_map/ppermute | solution.py:47
  122.6 12.1 %collective-permute-start.32 = (bf16[64,2688]{1,0:T(8,128)(2,1)S(1)}, bf16[64,2688]{1,0:T(8,128)(2,1)S(1)}, u32[]{:S(2)}, u32[]{:S(2)}) collective-permute-start(bf16[64,2688]{1,0:T(8,128)(2,1)S(1)} %activate.6.refs_5_.refs_1_), channel_id=1, source_target_pairs={{0,12},{4,0},{8,4},{12,8},{1,5},{5,9},{9,13},{13,1},{2,14},{6,2},{... | collective-permute-start | bytes 1032200 | tf_op jit(solution)/shard_map/ppermute | solution.py:47
  125.8 15.4 %collective-permute-start.34 = (bf16[64,2688]{1,0:T(8,128)(2,1)S(1)}, bf16[64,2688]{1,0:T(8,128)(2,1)S(1)}, u32[]{:S(2)}, u32[]{:S(2)}) collective-permute-start(bf16[64,2688]{1,0:T(8,128)(2,1)S(1)} %collective-permute-done.33.refs_4_), channel_id=1, source_target_pairs={{0,4},{4,8},{8,12},{12,0},{1,13},{5,1},{9,5},{13,9},{2,6},{6,10},{... | collective-permute-start | bytes 1032200 | tf_op jit(solution)/shard_map/ppermute | solution.py:47
  125.9 18.3 %collective-permute-start.39 = (bf16[64,2688]{1,0:T(8,128)(2,1)S(1)}, bf16[64,2688]{1,0:T(8,128)(2,1)S(1)}, u32[]{:S(2)}, u32[]{:S(2)}) collective-permute-start(bf16[64,2688]{1,0:T(8,128)(2,1)S(1)} %activate.7.refs_5_.refs_1_), channel_id=1, source_target_pairs={{0,12},{4,0},{8,4},{12,8},{1,5},{5,9},{9,13},{13,1},{2,14},{6,2},{... | collective-permute-start | bytes 1032200 | tf_op jit(solution)/shard_map/ppermute | solution.py:47
  145.7 16.3 %collective-permute-start.43 = (bf16[256,2688]{1,0:T(8,128)(2,1)S(1)}, bf16[256,2688]{1,0:T(8,128)(2,1)S(1)}, u32[]{:S(2)}, u32[]{:S(2)}) collective-permute-start(bf16[256,2688]{1,0:T(8,128)(2,1)S(1)} %get-tuple-element.87), channel_id=1, source_target_pairs={{0,1},{1,0},{2,3},{3,2},{4,5},{5,4},{6,7},{7,6},{8,9},{9,8},{10,11... | collective-permute-start | bytes 4128776 | tf_op jit(solution)/shard_map/ppermute | solution.py:36
  151.3 22.0 %collective-permute-start.46 = (bf16[128,512]{1,0:T(8,128)(2,1)S(1)}, bf16[128,512]{1,0:T(8,128)(2,1)S(1)}, u32[]{:S(2)}, u32[]{:S(2)}) collective-permute-start(bf16[128,512]{1,0:T(8,128)(2,1)S(1)} %get-tuple-element.91), channel_id=1, source_target_pairs={{0,48},{16,32},{32,80},{48,64},{64,112},{80,96},{96,16},{112,0},{1... | collective-permute-start | bytes 393224 | tf_op jit(solution)/shard_map/ppermute | solution.py:41
  153.2 20.1 %collective-permute-start.42 = (bf16[128,512]{1,0:T(8,128)(2,1)S(1)}, bf16[128,512]{1,0:T(8,128)(2,1)S(1)}, u32[]{:S(2)}, u32[]{:S(2)}) collective-permute-start(bf16[128,512]{1,0:T(8,128)(2,1)S(1)} %get-tuple-element.86.refs_9_), channel_id=1, source_target_pairs={{0,32},{32,64},{64,96},{96,0},{1,33},{33,65},{65,97},{97,1},{2,34}... | collective-permute-start | bytes 393224 | tf_op jit(solution)/shard_map/ppermute | solution.py:36
  (24 other events, 157.0 us)

commit v4 on v3

--- a/solution.py
+++ b/solution.py
@@ -22,12 +22,11 @@
 
 CHUNKS = ((0,), (3,), (1,), (2,))
 GROUPS = ((0,), (1,), (2,), (3,))
-LAG = 3
 ORDER = (
     ("F", 0), ("C", 1), ("C", 2), ("S1", 0), ("F", 1), ("S2", 0), ("F", 2), ("C", 3),
     ("S1", 1), ("ACT", 0), ("S1", 2), ("F", 3), ("S2", 1), ("S2", 2), ("S1", 3), ("ACT", 1),
     ("S2", 3), ("ASM", 0), ("ACT", 2), ("ASM", 1), ("BACK", 0), ("ACT", 3), ("ASM", 2), ("BACK", 1),
-    ("ASM", 3), ("BACK", 2), ("WG", 0), ("BACK", 3),
+    ("ASM", 3), ("BACK", 2), ("BACK", 3), ("WG", 0),
 )
 
 
@@ -301,10 +300,8 @@
     st = [{} for _ in range(n)]
     gr = [{} for _ in GROUPS]
     last = ()
-    near, far, due = [], [], []
-    for at, (stage, k) in enumerate(ORDER):
-        if due and due[0][0] == at:
-            last += due.pop(0)[1]
+    near, far = [], []
+    for stage, k in ORDER:
         if stage in ("C", "F", "S1", "S2", "ACT"):
             s = st[k]
             u = 32 * len(CHUNKS[k])
@@ -360,12 +357,9 @@
                 [shape(128, D, f32 if a == 0 and x == 0 else bf16) for a in owners for x in (0, 1)],
                 last, limit=24, flops=8 * count * D * HALF,
             )
-            sent = ()
             for i, a in enumerate(owners):
                 near.append(outs[2 * i] if a == 0 else move(outs[2 * i], "z", a))
                 far.append(move2(outs[2 * i + 1], a, 1))
-                sent += (far[-1],) if a == 0 else (near[-1], far[-1])
-            due.append((at + LAG, sent))
         last = (outs[0],)
 
     rest = weight_grads(ids, [g["other"] for g in gr], [own[i] for i in range(n)], grads[:3], last)

time: 178 us -> 174 us (0.978)
  waiting for transfers between devices: 65.4 us -> 62.8 us
    ppermute x20, waiting for transfers between devices: 27.6 us -> 22.6 us  [move(): return lax.ppermute(a, axis, [(i, (i + by) % n) for i in range(n)])]
    ppermute x24, waiting for transfers between devices: 37.7 us -> 40.2 us  [step(): return lax.ppermute(a, ('y', 'core'), pairs)]
  transfers between devices with their start and end apart: 48 -> 48, of which waited for: 24 -> 21; matrix products, arithmetic and copies ran while one was open for 0% -> 0% of each run, Pallas kernels for 23% -> 24%
where the time goes in v4:
time: 174 us
  waiting for transfers between devices  62.8 us (36%)
  starting transfers between devices  60.4 us (35%)
  Pallas kernels  43.5 us (25%)
  local copies, waits for them, and re-layouts  6.33 us (4%)
    ppermute x24, waiting for transfers between devices, step(): return lax.ppermute(a, ('y', 'core'), pairs)  40.2 us
    pallas_call x30, Pallas kernels, call(): pl.pallas_call(kernel, in_specs=[smem] + [in_space] * n + [anywhere] * m,...  32 us
    ppermute x24, starting transfers between devices, step(): return lax.ppermute(a, ('y', 'core'), pairs)  30.2 us
    ppermute x20, waiting for transfers between devices, move(): return lax.ppermute(a, axis, [(i, (i + by) % n) for i in range(n)])  22.6 us
    ppermute x20, starting transfers between devices, move(): return lax.ppermute(a, axis, [(i, (i + by) % n) for i in range(n)])  19.8 us
    ppermute x4, starting transfers between devices, move2(): return lax.ppermute(a, ('z', 'xh'), pairs)  10.3 us
    pallas_call x2, Pallas kernels, weight_grads(): pl.pallas_call(kernel, in_specs=[smem] + [vmem] * given + [anywhere] * (l...  10.2 us
    unnamed x16, local copies, waits for them, and re-layouts  6.33 us
  transfers between devices with their start and end apart: 48, of which 21 were waited for; matrix products, arithmetic and copies ran while one was open for 0% of the time, Pallas kernels for 24%

profile of v4, /device:TPU:0, one launch (start us, length us, event | category | flops | bytes accessed | tf_op | source)
XLA Modules:
  0.0 174.2 jit_solution(6813023241965053237)
XLA Ops:
  3.4 3.2 %collective-permute-start = (bf16[128,1024]{1,0:T(8,128)(2,1)S(1)}, bf16[128,1024]{1,0:T(8,128)(2,1)S(1)}, u32[]{:S(2)}, u32[]{:S(2)}) collective-permute-start(bf16[128,1024]{1,0:T(8,128)(2,1)S(1)} %rows.1.refs_1_.r_4_), channel_id=1, source_target_pairs={{0,16},{16,0},{1,17},{17,1},{2,18},{18,2},{3,19},{19,3},{4,20},{20... | collective-permute-start | bytes 786440 | tf_op jit(solution)/shard_map/ppermute | solution.py:35
  13.7 2.1 %collective-permute-start.6 = (bf16[256,1024]{1,0:T(8,128)(2,1)S(1)}, bf16[256,1024]{1,0:T(8,128)(2,1)S(1)}, u32[]{:S(2)}, u32[]{:S(2)}) collective-permute-start(bf16[256,1024]{1,0:T(8,128)(2,1)S(1)} %get-tuple-element.52.refs_1_.refs_5_), channel_id=1, source_target_pairs={{0,32},{32,64},{64,96},{96,0},{1,33},{33,65},{65,97},{97,1},{2,34}... | collective-permute-start | bytes 1572872 | tf_op jit(solution)/shard_map/ppermute | solution.py:35
  15.9 2.2 %collective-permute-start.5 = (bf16[256,1024]{1,0:T(8,128)(2,1)S(1)}, bf16[256,1024]{1,0:T(8,128)(2,1)S(1)}, u32[]{:S(2)}, u32[]{:S(2)}) collective-permute-start(bf16[256,1024]{1,0:T(8,128)(2,1)S(1)} %get-tuple-element.52.refs_1_.refs_5_), channel_id=1, source_target_pairs={{0,96},{32,0},{64,32},{96,64},{1,97},{33,1},{65,33},{97,65},{2,98}... | collective-permute-start | bytes 1572872 | tf_op jit(solution)/shard_map/ppermute | solution.py:35
  18.4 2.4 %forward.4 = (f32[64,2688]{1,0:T(8,128)S(1)}, f32[64,2688]{1,0:T(8,128)S(1)}, bf16[64,2688]{1,0:T(8,128)(2,1)S(1)}, bf16[64,2688]{1,0:T(8,128)(2,1)S(1)}) custom-call(s32[3]{0:T(128)S(1)} %pad_add_fusion.refs_0_.r_0_, bf16[256,1024]{1,0:T(8,128)(2,1)S(1)} %get-tuple-element.52.refs_1_.refs_5_, bf16[256,1024]{1,0:T(8,128)(2,1)S(1)} %collective-permute-done.1.refs_2_, ...), custom_call_target="tpu_custom_call" | custom-call | tf_op jit(solution)/shard_map/forward/pallas_call | solution.py:62
  22.4 8.1 %collective-permute-done.6.refs_1_ = bf16[256,1024]{1,0:T(8,128)(2,1)S(1)} collective-permute-done((bf16[256,1024]{1,0:T(8,128)(2,1)S(1)}, bf16[256,1024]{1,0:T(8,128)(2,1)S(1)}, u32[]{:S(2)}, u32[]{:S(2)}) %collective-permute-start.6) | collective-permute-done | bytes 524320 | tf_op jit(solution)/shard_map/ppermute | solution.py:35
  34.2 3.0 %collective-permute-start.3 = (bf16[64,2688]{1,0:T(8,128)(2,1)S(1)}, bf16[64,2688]{1,0:T(8,128)(2,1)S(1)}, u32[]{:S(2)}, u32[]{:S(2)}) collective-permute-start(bf16[64,2688]{1,0:T(8,128)(2,1)S(1)} %get-tuple-element.55), channel_id=1, source_target_pairs={{0,12},{4,0},{8,4},{12,8},{1,5},{5,9},{9,13},{13,1},{2,14},{6,2},{... | collective-permute-start | bytes 1032200 | tf_op jit(solution)/shard_map/ppermute | solution.py:46
  37.9 2.3 %forward.5 = (f32[64,2688]{1,0:T(8,128)S(1)}, f32[64,2688]{1,0:T(8,128)S(1)}, bf16[64,2688]{1,0:T(8,128)(2,1)S(1)}, bf16[64,2688]{1,0:T(8,128)(2,1)S(1)}) custom-call(s32[3]{0:T(128)S(1)} %pad_add_fusion.refs_0_.r_0_, bf16[256,1024]{1,0:T(8,128)(2,1)S(1)} %get-tuple-element.58.refs_2_.refs_1_.refs_6_, bf16[256,1024]{1,0:T(8,128)(2,1)S(1)} %collective-permute-done.8.refs_2_, ...), custom_call_target="tpu_custom_call" | custom-call | tf_op jit(solution)/shard_map/forward/pallas_call | solution.py:62
  40.3 5.3 %collective-permute-done.3.refs_2_ = bf16[64,2688]{1,0:T(8,128)(2,1)S(1)} collective-permute-done((bf16[64,2688]{1,0:T(8,128)(2,1)S(1)}, bf16[64,2688]{1,0:T(8,128)(2,1)S(1)}, u32[]{:S(2)}, u32[]{:S(2)}) %collective-permute-start.3) | collective-permute-done | bytes 344096 | tf_op jit(solution)/shard_map/ppermute | solution.py:46
  48.6 2.4 %forward.6 = (f32[64,2688]{1,0:T(8,128)S(1)}, f32[64,2688]{1,0:T(8,128)S(1)}, bf16[64,2688]{1,0:T(8,128)(2,1)S(1)}, bf16[64,2688]{1,0:T(8,128)(2,1)S(1)}) custom-call(s32[3]{0:T(128)S(1)} %pad_add_fusion.refs_0_.r_0_, bf16[256,1024]{1,0:T(8,128)(2,1)S(1)} %get-tuple-element.59.refs_3_.refs_1_.refs_7_, bf16[256,1024]{1,0:T(8,128)(2,1)S(1)} %collective-permute-done.12.refs_2_, ...), custom_call_target="tpu_custom_call" | custom-call | tf_op jit(solution)/shard_map/forward/pallas_call | solution.py:62
  51.6 2.4 %collective-permute-start.16 = (bf16[256,1024]{1,0:T(8,128)(2,1)S(1)}, bf16[256,1024]{1,0:T(8,128)(2,1)S(1)}, u32[]{:S(2)}, u32[]{:S(2)}) collective-permute-start(bf16[256,1024]{1,0:T(8,128)(2,1)S(1)} %get-tuple-element.67), channel_id=1, source_target_pairs={{0,1},{1,0},{2,3},{3,2},{4,5},{5,4},{6,7},{7,6},{8,9},{9,8},{10,11... | collective-permute-start | bytes 1572872 | tf_op jit(solution)/shard_map/ppermute | solution.py:35
  54.0 3.2 %collective-permute-start.22 = (bf16[64,2688]{1,0:T(8,128)(2,1)S(1)}, bf16[64,2688]{1,0:T(8,128)(2,1)S(1)}, u32[]{:S(2)}, u32[]{:S(2)}) collective-permute-start(bf16[64,2688]{1,0:T(8,128)(2,1)S(1)} %get-tuple-element.75), channel_id=1, source_target_pairs={{0,12},{4,0},{8,4},{12,8},{1,5},{5,9},{9,13},{13,1},{2,14},{6,2},{... | collective-permute-start | bytes 1032200 | tf_op jit(solution)/shard_map/ppermute | solution.py:46
  57.9 5.7 %collective-permute-done.9.refs_2_ = f32[64,2688]{1,0:T(8,128)S(1)} collective-permute-done((f32[64,2688]{1,0:T(8,128)S(1)}, f32[64,2688]{1,0:T(8,128)S(1)}, u32[]{:S(2)}, u32[]{:S(2)}) %collective-permute-start.9) | collective-permute-done | bytes 688160 | tf_op jit(solution)/shard_map/ppermute | solution.py:35
  63.6 3.7 %collective-permute-start.20 = (bf16[64,2688]{1,0:T(8,128)(2,1)S(1)}, bf16[64,2688]{1,0:T(8,128)(2,1)S(1)}, u32[]{:S(2)}, u32[]{:S(2)}) collective-permute-start(bf16[64,2688]{1,0:T(8,128)(2,1)S(1)} %get-tuple-element.74), channel_id=1, source_target_pairs={{0,12},{4,0},{8,4},{12,8},{1,5},{5,9},{9,13},{13,1},{2,14},{6,2},{... | collective-permute-start | bytes 1032200 | tf_op jit(solution)/shard_map/ppermute | solution.py:46
  68.9 2.4 %forward.7 = (f32[64,2688]{1,0:T(8,128)S(1)}, f32[64,2688]{1,0:T(8,128)S(1)}, bf16[64,2688]{1,0:T(8,128)(2,1)S(1)}, bf16[64,2688]{1,0:T(8,128)(2,1)S(1)}) custom-call(s32[3]{0:T(128)S(1)} %pad_add_fusion.refs_0_.r_0_, bf16[256,1024]{1,0:T(8,128)(2,1)S(1)} %get-tuple-element.66.refs_3_.refs_1_.refs_8_, bf16[256,1024]{1,0:T(8,128)(2,1)S(1)} %collective-permute-done.16.refs_2_, ...), custom_call_target="tpu_custom_call" | custom-call | tf_op jit(solution)/shard_map/forward/pallas_call | solution.py:62
  75.7 3.7 %collective-permute-start.18 = (bf16[64,2688]{1,0:T(8,128)(2,1)S(1)}, bf16[64,2688]{1,0:T(8,128)(2,1)S(1)}, u32[]{:S(2)}, u32[]{:S(2)}) collective-permute-start(bf16[64,2688]{1,0:T(8,128)(2,1)S(1)} %get-tuple-element.71), channel_id=1, source_target_pairs={{0,12},{4,0},{8,4},{12,8},{1,5},{5,9},{9,13},{13,1},{2,14},{6,2},{... | collective-permute-start | bytes 1032200 | tf_op jit(solution)/shard_map/ppermute | solution.py:46
  80.1 5.1 %collective-permute-done.19.refs_2_ = bf16[64,2688]{1,0:T(8,128)(2,1)S(1)} collective-permute-done((bf16[64,2688]{1,0:T(8,128)(2,1)S(1)}, bf16[64,2688]{1,0:T(8,128)(2,1)S(1)}, u32[]{:S(2)}, u32[]{:S(2)}) %collective-permute-start.19) | collective-permute-done | bytes 344096 | tf_op jit(solution)/shard_map/ppermute | solution.py:46
  85.9 3.2 %collective-permute-start.13 = (bf16[64,2688]{1,0:T(8,128)(2,1)S(1)}, bf16[64,2688]{1,0:T(8,128)(2,1)S(1)}, u32[]{:S(2)}, u32[]{:S(2)}) collective-permute-start(bf16[64,2688]{1,0:T(8,128)(2,1)S(1)} %activate.4.refs_3_.refs_1_), channel_id=1, source_target_pairs={{0,12},{4,0},{8,4},{12,8},{1,5},{5,9},{9,13},{13,1},{2,14},{6,2},{... | collective-permute-start | bytes 1032200 | tf_op jit(solution)/shard_map/ppermute | solution.py:46
  93.9 2.3 %collective-permute-done.24.refs_3_ = bf16[64,2688]{1,0:T(8,128)(2,1)S(1)} collective-permute-done((bf16[64,2688]{1,0:T(8,128)(2,1)S(1)}, bf16[64,2688]{1,0:T(8,128)(2,1)S(1)}, u32[]{:S(2)}, u32[]{:S(2)}) %collective-permute-start.24) | collective-permute-done | bytes 344096 | tf_op jit(solution)/shard_map/ppermute | solution.py:46
  97.6 2.3 %collective-permute-done.15.refs_3_ = bf16[64,2688]{1,0:T(8,128)(2,1)S(1)} collective-permute-done((bf16[64,2688]{1,0:T(8,128)(2,1)S(1)}, bf16[64,2688]{1,0:T(8,128)(2,1)S(1)}, u32[]{:S(2)}, u32[]{:S(2)}) %collective-permute-start.15) | collective-permute-done | bytes 344096 | tf_op jit(solution)/shard_map/ppermute | solution.py:46
  106.7 4.7 %collective-permute-done.27.refs_2_ = bf16[64,2688]{1,0:T(8,128)(2,1)S(1)} collective-permute-done((bf16[64,2688]{1,0:T(8,128)(2,1)S(1)}, bf16[64,2688]{1,0:T(8,128)(2,1)S(1)}, u32[]{:S(2)}, u32[]{:S(2)}) %collective-permute-start.27) | collective-permute-done | bytes 344096 | tf_op jit(solution)/shard_map/ppermute | solution.py:46
  115.2 6.7 %collective-permute-done.35.refs_2_ = f32[64,2688]{1,0:T(8,128)S(1)} collective-permute-done((f32[64,2688]{1,0:T(8,128)S(1)}, f32[64,2688]{1,0:T(8,128)S(1)}, u32[]{:S(2)}, u32[]{:S(2)}) %collective-permute-start.35) | collective-permute-done | bytes 688160 | tf_op jit(solution)/shard_map/ppermute | solution.py:35
  122.6 3.2 %collective-permute-start.32 = (bf16[64,2688]{1,0:T(8,128)(2,1)S(1)}, bf16[64,2688]{1,0:T(8,128)(2,1)S(1)}, u32[]{:S(2)}, u32[]{:S(2)}) collective-permute-start(bf16[64,2688]{1,0:T(8,128)(2,1)S(1)} %activate.6.refs_5_.refs_1_), channel_id=1, source_target_pairs={{0,12},{4,0},{8,4},{12,8},{1,5},{5,9},{9,13},{13,1},{2,14},{6,2},{... | collective-permute-start | bytes 1032200 | tf_op jit(solution)/shard_map/ppermute | solution.py:46
  125.9 3.2 %collective-permute-start.38 = (bf16[64,2688]{1,0:T(8,128)(2,1)S(1)}, bf16[64,2688]{1,0:T(8,128)(2,1)S(1)}, u32[]{:S(2)}, u32[]{:S(2)}) collective-permute-start(bf16[64,2688]{1,0:T(8,128)(2,1)S(1)} %activate.7.refs_5_.refs_1_), channel_id=1, source_target_pairs={{0,12},{4,0},{8,4},{12,8},{1,5},{5,9},{9,13},{13,1},{2,14},{6,2},{... | collective-permute-start | bytes 1032200 | tf_op jit(solution)/shard_map/ppermute | solution.py:46
  129.1 5.6 %collective-permute-done.39.refs_4_ = bf16[64,2688]{1,0:T(8,128)(2,1)S(1)} collective-permute-done((bf16[64,2688]{1,0:T(8,128)(2,1)S(1)}, bf16[64,2688]{1,0:T(8,128)(2,1)S(1)}, u32[]{:S(2)}, u32[]{:S(2)}) %collective-permute-start.39) | collective-permute-done | bytes 344096 | tf_op jit(solution)/shard_map/ppermute | solution.py:46
  134.7 6.5 %collective-permute-done.34.refs_3_ = bf16[64,2688]{1,0:T(8,128)(2,1)S(1)} collective-permute-done((bf16[64,2688]{1,0:T(8,128)(2,1)S(1)}, bf16[64,2688]{1,0:T(8,128)(2,1)S(1)}, u32[]{:S(2)}, u32[]{:S(2)}) %collective-permute-start.34) | collective-permute-done | bytes 344096 | tf_op jit(solution)/shard_map/ppermute | solution.py:46
  142.3 1.8 %back.5 = (bf16[128,512]{1,0:T(8,128)(2,1)S(1)}, bf16[128,512]{1,0:T(8,128)(2,1)S(1)}) custom-call(s32[3]{0:T(128)S(1)} %pad_add_fusion.refs_0_.r_0_, bf16[256,2688]{1,0:T(8,128)(2,1)S(1)} %get-tuple-element.78.refs_5_.refs_1_.refs_2_, bf16[256,2688]{1,0:T(8,128)(2,1)S(1)} %collective-permute-done.31.refs_2_, bf16[512,1792]{1,0:T(8,128)(2,1)S(1)} %copy-done.1, ...), custom_call_target="tpu_custom_call" | custom-call | tf_op jit(solution)/shard_map/back/pallas_call | solution.py:62
  145.8 2.8 %collective-permute-start.44 = (bf16[128,512]{1,0:T(8,128)(2,1)S(1)}, bf16[128,512]{1,0:T(8,128)(2,1)S(1)}, u32[]{:S(2)}, u32[]{:S(2)}) collective-permute-start(bf16[128,512]{1,0:T(8,128)(2,1)S(1)} %get-tuple-element.88), channel_id=1, source_target_pairs={{0,16},{16,0},{32,48},{48,32},{64,80},{80,64},{96,112},{112,96},{1... | collective-permute-start | bytes 393224 | tf_op jit(solution)/shard_map/ppermute | solution.py:40
  151.7 4.3 %collective-permute-start.46 = (bf16[128,512]{1,0:T(8,128)(2,1)S(1)}, bf16[128,512]{1,0:T(8,128)(2,1)S(1)}, u32[]{:S(2)}, u32[]{:S(2)}) collective-permute-start(bf16[128,512]{1,0:T(8,128)(2,1)S(1)} %get-tuple-element.90), channel_id=1, source_target_pairs={{0,48},{16,32},{32,80},{48,64},{64,112},{80,96},{96,16},{112,0},{1... | collective-permute-start | bytes 393224 | tf_op jit(solution)/shard_map/ppermute | solution.py:40
  158.8 2.0 %collective-permute-start.47 = (bf16[128,512]{1,0:T(8,128)(2,1)S(1)}, bf16[128,512]{1,0:T(8,128)(2,1)S(1)}, u32[]{:S(2)}, u32[]{:S(2)}) collective-permute-start(bf16[128,512]{1,0:T(8,128)(2,1)S(1)} %get-tuple-element.91), channel_id=1, source_target_pairs={{0,80},{16,64},{32,112},{48,96},{64,16},{80,0},{96,48},{112,32},{1... | collective-permute-start | bytes 393224 | tf_op jit(solution)/shard_map/ppermute | solution.py:40
  160.8 1.9 %collective-permute-start.43 = (bf16[128,512]{1,0:T(8,128)(2,1)S(1)}, bf16[128,512]{1,0:T(8,128)(2,1)S(1)}, u32[]{:S(2)}, u32[]{:S(2)}) collective-permute-start(bf16[128,512]{1,0:T(8,128)(2,1)S(1)} %get-tuple-element.87.refs_9_), channel_id=1, source_target_pairs={{0,64},{32,96},{64,0},{96,32},{1,65},{33,97},{65,1},{97,33},{2,66}... | collective-permute-start | bytes 393224 | tf_op jit(solution)/shard_map/ppermute | solution.py:35
  162.7 5.1 %weight_grads.2 = (bf16[512,1792]{1,0:T(8,128)(2,1)}, bf16[512,1792]{1,0:T(8,128)(2,1)}, bf16[1792,512]{1,0:T(8,128)(2,1)}, f32[8,128]{1,0:T(8,128)S(1)}) custom-call(s32[3]{0:T(128)S(1)} %pad_add_fusion.refs_0_.r_0_, bf16[256,2688]{1,0:T(8,128)(2,1)S(1)} %get-tuple-element.76.refs_3_.refs_1_, ...), custom_call_target="tpu_custom_call" | custom-call | tf_op jit(solution)/shard_map/weight_grads/pallas_call | solution.py:263
  167.7 5.1 %weight_grads.3 = (bf16[512,1792]{1,0:T(8,128)(2,1)}, bf16[512,1792]{1,0:T(8,128)(2,1)}, bf16[1792,512]{1,0:T(8,128)(2,1)}, f32[8,128]{1,0:T(8,128)S(1)}) custom-call(s32[3]{0:T(128)S(1)} %pad_add_fusion.refs_0_.r_0_, bf16[256,2688]{1,0:T(8,128)(2,1)S(1)} %collective-permute-done.26.refs_2_.refs_1_, ...), custom_call_target="tpu_custom_call", output_to_operand_aliasing={{0}: (9, {}), {1}: (10, {}), {2}: (11, {})} | custom-call | tf_op jit(solution)/shard_map/weight_grads/pallas_call | solution.py:263
  (114 shorter events, 55.1 us)
Async XLA Ops:
  13.7 16.8 %collective-permute-start.6 = (bf16[256,1024]{1,0:T(8,128)(2,1)S(1)}, bf16[256,1024]{1,0:T(8,128)(2,1)S(1)}, u32[]{:S(2)}, u32[]{:S(2)}) collective-permute-start(bf16[256,1024]{1,0:T(8,128)(2,1)S(1)} %get-tuple-element.52.refs_1_.refs_5_), channel_id=1, source_target_pairs={{0,32},{32,64},{64,96},{96,0},{1,33},{33,65},{65,97},{97,1},{2,34}... | collective-permute-start | bytes 1572872 | tf_op jit(solution)/shard_map/ppermute | solution.py:35
  15.9 15.3 %collective-permute-start.5 = (bf16[256,1024]{1,0:T(8,128)(2,1)S(1)}, bf16[256,1024]{1,0:T(8,128)(2,1)S(1)}, u32[]{:S(2)}, u32[]{:S(2)}) collective-permute-start(bf16[256,1024]{1,0:T(8,128)(2,1)S(1)} %get-tuple-element.52.refs_1_.refs_5_), channel_id=1, source_target_pairs={{0,96},{32,0},{64,32},{96,64},{1,97},{33,1},{65,33},{97,65},{2,98}... | collective-permute-start | bytes 1572872 | tf_op jit(solution)/shard_map/ppermute | solution.py:35
  20.7 16.5 %collective-permute-start.4 = (bf16[64,2688]{1,0:T(8,128)(2,1)S(1)}, bf16[64,2688]{1,0:T(8,128)(2,1)S(1)}, u32[]{:S(2)}, u32[]{:S(2)}) collective-permute-start(bf16[64,2688]{1,0:T(8,128)(2,1)S(1)} %get-tuple-element.57), channel_id=1, source_target_pairs={{0,4},{4,8},{8,12},{12,0},{1,13},{5,1},{9,5},{13,9},{2,6},{6,10},{... | collective-permute-start | bytes 1032200 | tf_op jit(solution)/shard_map/ppermute | solution.py:46
  31.8 16.8 %collective-permute-start.12 = (bf16[256,1024]{1,0:T(8,128)(2,1)S(1)}, bf16[256,1024]{1,0:T(8,128)(2,1)S(1)}, u32[]{:S(2)}, u32[]{:S(2)}) collective-permute-start(bf16[256,1024]{1,0:T(8,128)(2,1)S(1)} %get-tuple-element.64), channel_id=1, source_target_pairs={{0,1},{1,0},{2,3},{3,2},{4,5},{5,4},{6,7},{7,6},{8,9},{9,8},{10,11... | collective-permute-start | bytes 1572872 | tf_op jit(solution)/shard_map/ppermute | solution.py:35
  32.4 18.6 %collective-permute-start.11 = (bf16[256,1024]{1,0:T(8,128)(2,1)S(1)}, bf16[256,1024]{1,0:T(8,128)(2,1)S(1)}, u32[]{:S(2)}, u32[]{:S(2)}) collective-permute-start(bf16[256,1024]{1,0:T(8,128)(2,1)S(1)} %get-tuple-element.52.refs_1_.refs_5_), channel_id=1, source_target_pairs={{0,64},{32,96},{64,0},{96,32},{1,65},{33,97},{65,1},{97,33},{2,66}... | collective-permute-start | bytes 1572872 | tf_op jit(solution)/shard_map/ppermute | solution.py:35
  47.0 16.6 %collective-permute-start.9 = (f32[64,2688]{1,0:T(8,128)S(1)}, f32[64,2688]{1,0:T(8,128)S(1)}, u32[]{:S(2)}, u32[]{:S(2)}) collective-permute-start(f32[64,2688]{1,0:T(8,128)S(1)} %beside.4.refs_7_.refs_1_), channel_id=1, source_target_pairs={{0,2},{2,0},{1,3},{3,1},{4,6},{6,4},{5,7},{7,5},{8,10},{10,8},{9,1... | collective-permute-start | bytes 2064392 | tf_op jit(solution)/shard_map/ppermute | solution.py:35
  51.6 17.3 %collective-permute-start.16 = (bf16[256,1024]{1,0:T(8,128)(2,1)S(1)}, bf16[256,1024]{1,0:T(8,128)(2,1)S(1)}, u32[]{:S(2)}, u32[]{:S(2)}) collective-permute-start(bf16[256,1024]{1,0:T(8,128)(2,1)S(1)} %get-tuple-element.67), channel_id=1, source_target_pairs={{0,1},{1,0},{2,3},{3,2},{4,5},{5,4},{6,7},{7,6},{8,9},{9,8},{10,11... | collective-permute-start | bytes 1572872 | tf_op jit(solution)/shard_map/ppermute | solution.py:35
  54.0 14.0 %collective-permute-start.17 = (bf16[64,2688]{1,0:T(8,128)(2,1)S(1)}, bf16[64,2688]{1,0:T(8,128)(2,1)S(1)}, u32[]{:S(2)}, u32[]{:S(2)}) collective-permute-start(bf16[64,2688]{1,0:T(8,128)(2,1)S(1)} %get-tuple-element.69), channel_id=1, source_target_pairs={{0,4},{4,8},{8,12},{12,0},{1,13},{5,1},{9,5},{13,9},{2,6},{6,10},{... | collective-permute-start | bytes 1032200 | tf_op jit(solution)/shard_map/ppermute | solution.py:46
  54.0 17.3 %collective-permute-start.22 = (bf16[64,2688]{1,0:T(8,128)(2,1)S(1)}, bf16[64,2688]{1,0:T(8,128)(2,1)S(1)}, u32[]{:S(2)}, u32[]{:S(2)}) collective-permute-start(bf16[64,2688]{1,0:T(8,128)(2,1)S(1)} %get-tuple-element.75), channel_id=1, source_target_pairs={{0,12},{4,0},{8,4},{12,8},{1,5},{5,9},{9,13},{13,1},{2,14},{6,2},{... | collective-permute-start | bytes 1032200 | tf_op jit(solution)/shard_map/ppermute | solution.py:46
  57.8 14.5 %collective-permute-start.23 = (bf16[64,2688]{1,0:T(8,128)(2,1)S(1)}, bf16[64,2688]{1,0:T(8,128)(2,1)S(1)}, u32[]{:S(2)}, u32[]{:S(2)}) collective-permute-start(bf16[64,2688]{1,0:T(8,128)(2,1)S(1)} %add.9.refs_3_), channel_id=1, source_target_pairs={{0,4},{4,8},{8,12},{12,0},{1,13},{5,1},{9,5},{13,9},{2,6},{6,10},{... | collective-permute-start | bytes 1032200 | tf_op jit(solution)/shard_map/ppermute | solution.py:46
  63.6 12.1 %collective-permute-start.20 = (bf16[64,2688]{1,0:T(8,128)(2,1)S(1)}, bf16[64,2688]{1,0:T(8,128)(2,1)S(1)}, u32[]{:S(2)}, u32[]{:S(2)}) collective-permute-start(bf16[64,2688]{1,0:T(8,128)(2,1)S(1)} %get-tuple-element.74), channel_id=1, source_target_pairs={{0,12},{4,0},{8,4},{12,8},{1,5},{5,9},{9,13},{13,1},{2,14},{6,2},{... | collective-permute-start | bytes 1032200 | tf_op jit(solution)/shard_map/ppermute | solution.py:46
  72.9 17.9 %collective-permute-start.25 = (f32[64,2688]{1,0:T(8,128)S(1)}, f32[64,2688]{1,0:T(8,128)S(1)}, u32[]{:S(2)}, u32[]{:S(2)}) collective-permute-start(f32[64,2688]{1,0:T(8,128)S(1)} %beside.5.refs_4_.refs_1_), channel_id=1, source_target_pairs={{0,2},{2,0},{1,3},{3,1},{4,6},{6,4},{5,7},{7,5},{8,10},{10,8},{9,1... | collective-permute-start | bytes 2064392 | tf_op jit(solution)/shard_map/ppermute | solution.py:35
  73.5 11.7 %collective-permute-start.19 = (bf16[64,2688]{1,0:T(8,128)(2,1)S(1)}, bf16[64,2688]{1,0:T(8,128)(2,1)S(1)}, u32[]{:S(2)}, u32[]{:S(2)}) collective-permute-start(bf16[64,2688]{1,0:T(8,128)(2,1)S(1)} %get-tuple-element.73), channel_id=1, source_target_pairs={{0,4},{4,8},{8,12},{12,0},{1,13},{5,1},{9,5},{13,9},{2,6},{6,10},{... | collective-permute-start | bytes 1032200 | tf_op jit(solution)/shard_map/ppermute | solution.py:46
  73.5 17.3 %collective-permute-start.14 = (bf16[64,2688]{1,0:T(8,128)(2,1)S(1)}, bf16[64,2688]{1,0:T(8,128)(2,1)S(1)}, u32[]{:S(2)}, u32[]{:S(2)}) collective-permute-start(bf16[64,2688]{1,0:T(8,128)(2,1)S(1)} %activate.4.refs_3_.refs_1_), channel_id=1, source_target_pairs={{0,4},{4,8},{8,12},{12,0},{1,13},{5,1},{9,5},{13,9},{2,6},{6,10},{... | collective-permute-start | bytes 1032200 | tf_op jit(solution)/shard_map/ppermute | solution.py:46
  75.7 16.4 %collective-permute-start.18 = (bf16[64,2688]{1,0:T(8,128)(2,1)S(1)}, bf16[64,2688]{1,0:T(8,128)(2,1)S(1)}, u32[]{:S(2)}, u32[]{:S(2)}) collective-permute-start(bf16[64,2688]{1,0:T(8,128)(2,1)S(1)} %get-tuple-element.71), channel_id=1, source_target_pairs={{0,12},{4,0},{8,4},{12,8},{1,5},{5,9},{9,13},{13,1},{2,14},{6,2},{... | collective-permute-start | bytes 1032200 | tf_op jit(solution)/shard_map/ppermute | solution.py:46
  85.9 11.7 %collective-permute-start.13 = (bf16[64,2688]{1,0:T(8,128)(2,1)S(1)}, bf16[64,2688]{1,0:T(8,128)(2,1)S(1)}, u32[]{:S(2)}, u32[]{:S(2)}) collective-permute-start(bf16[64,2688]{1,0:T(8,128)(2,1)S(1)} %activate.4.refs_3_.refs_1_), channel_id=1, source_target_pairs={{0,12},{4,0},{8,4},{12,8},{1,5},{5,9},{9,13},{13,1},{2,14},{6,2},{... | collective-permute-start | bytes 1032200 | tf_op jit(solution)/shard_map/ppermute | solution.py:46
  90.8 15.2 %collective-permute-start.30 = (f32[64,2688]{1,0:T(8,128)S(1)}, f32[64,2688]{1,0:T(8,128)S(1)}, u32[]{:S(2)}, u32[]{:S(2)}) collective-permute-start(f32[64,2688]{1,0:T(8,128)S(1)} %beside.6.refs_3_.refs_1_), channel_id=1, source_target_pairs={{0,2},{2,0},{1,3},{3,1},{4,6},{6,4},{5,7},{7,5},{8,10},{10,8},{9,1... | collective-permute-start | bytes 2064392 | tf_op jit(solution)/shard_map/ppermute | solution.py:35
  100.6 12.7 %collective-permute-start.26 = (bf16[256,2688]{1,0:T(8,128)(2,1)S(1)}, bf16[256,2688]{1,0:T(8,128)(2,1)S(1)}, u32[]{:S(2)}, u32[]{:S(2)}) collective-permute-start(bf16[256,2688]{1,0:T(8,128)(2,1)S(1)} %get-tuple-element.77), channel_id=1, source_target_pairs={{0,1},{1,0},{2,3},{3,2},{4,5},{5,4},{6,7},{7,6},{8,9},{9,8},{10,11... | collective-permute-start | bytes 4128776 | tf_op jit(solution)/shard_map/ppermute | solution.py:35
  103.6 18.2 %collective-permute-start.35 = (f32[64,2688]{1,0:T(8,128)S(1)}, f32[64,2688]{1,0:T(8,128)S(1)}, u32[]{:S(2)}, u32[]{:S(2)}) collective-permute-start(f32[64,2688]{1,0:T(8,128)S(1)} %beside.7.refs_5_.refs_1_), channel_id=1, source_target_pairs={{0,2},{2,0},{1,3},{3,1},{4,6},{6,4},{5,7},{7,5},{8,10},{10,8},{9,1... | collective-permute-start | bytes 2064392 | tf_op jit(solution)/shard_map/ppermute | solution.py:35
  113.1 29.2 %collective-permute-start.31 = (bf16[256,2688]{1,0:T(8,128)(2,1)S(1)}, bf16[256,2688]{1,0:T(8,128)(2,1)S(1)}, u32[]{:S(2)}, u32[]{:S(2)}) collective-permute-start(bf16[256,2688]{1,0:T(8,128)(2,1)S(1)} %get-tuple-element.80), channel_id=1, source_target_pairs={{0,1},{1,0},{2,3},{3,2},{4,5},{5,4},{6,7},{7,6},{8,9},{9,8},{10,11... | collective-permute-start | bytes 4128776 | tf_op jit(solution)/shard_map/ppermute | solution.py:35
  113.2 12.6 %collective-permute-start.33 = (bf16[64,2688]{1,0:T(8,128)(2,1)S(1)}, bf16[64,2688]{1,0:T(8,128)(2,1)S(1)}, u32[]{:S(2)}, u32[]{:S(2)}) collective-permute-start(bf16[64,2688]{1,0:T(8,128)(2,1)S(1)} %activate.6.refs_5_.refs_1_), channel_id=1, source_target_pairs={{0,4},{4,8},{8,12},{12,0},{1,13},{5,1},{9,5},{13,9},{2,6},{6,10},{... | collective-permute-start | bytes 1032200 | tf_op jit(solution)/shard_map/ppermute | solution.py:46
  122.5 12.2 %collective-permute-start.39 = (bf16[64,2688]{1,0:T(8,128)(2,1)S(1)}, bf16[64,2688]{1,0:T(8,128)(2,1)S(1)}, u32[]{:S(2)}, u32[]{:S(2)}) collective-permute-start(bf16[64,2688]{1,0:T(8,128)(2,1)S(1)} %activate.7.refs_5_.refs_1_), channel_id=1, source_target_pairs={{0,4},{4,8},{8,12},{12,0},{1,13},{5,1},{9,5},{13,9},{2,6},{6,10},{... | collective-permute-start | bytes 1032200 | tf_op jit(solution)/shard_map/ppermute | solution.py:46
  122.6 12.1 %collective-permute-start.32 = (bf16[64,2688]{1,0:T(8,128)(2,1)S(1)}, bf16[64,2688]{1,0:T(8,128)(2,1)S(1)}, u32[]{:S(2)}, u32[]{:S(2)}) collective-permute-start(bf16[64,2688]{1,0:T(8,128)(2,1)S(1)} %activate.6.refs_5_.refs_1_), channel_id=1, source_target_pairs={{0,12},{4,0},{8,4},{12,8},{1,5},{5,9},{9,13},{13,1},{2,14},{6,2},{... | collective-permute-start | bytes 1032200 | tf_op jit(solution)/shard_map/ppermute | solution.py:46
  125.8 15.4 %collective-permute-start.34 = (bf16[64,2688]{1,0:T(8,128)(2,1)S(1)}, bf16[64,2688]{1,0:T(8,128)(2,1)S(1)}, u32[]{:S(2)}, u32[]{:S(2)}) collective-permute-start(bf16[64,2688]{1,0:T(8,128)(2,1)S(1)} %collective-permute-done.33.refs_4_), channel_id=1, source_target_pairs={{0,4},{4,8},{8,12},{12,0},{1,13},{5,1},{9,5},{13,9},{2,6},{6,10},{... | collective-permute-start | bytes 1032200 | tf_op jit(solution)/shard_map/ppermute | solution.py:46
  125.9 18.3 %collective-permute-start.38 = (bf16[64,2688]{1,0:T(8,128)(2,1)S(1)}, bf16[64,2688]{1,0:T(8,128)(2,1)S(1)}, u32[]{:S(2)}, u32[]{:S(2)}) collective-permute-start(bf16[64,2688]{1,0:T(8,128)(2,1)S(1)} %activate.7.refs_5_.refs_1_), channel_id=1, source_target_pairs={{0,12},{4,0},{8,4},{12,8},{1,5},{5,9},{9,13},{13,1},{2,14},{6,2},{... | collective-permute-start | bytes 1032200 | tf_op jit(solution)/shard_map/ppermute | solution.py:46
  145.8 13.0 %collective-permute-start.44 = (bf16[128,512]{1,0:T(8,128)(2,1)S(1)}, bf16[128,512]{1,0:T(8,128)(2,1)S(1)}, u32[]{:S(2)}, u32[]{:S(2)}) collective-permute-start(bf16[128,512]{1,0:T(8,128)(2,1)S(1)} %get-tuple-element.88), channel_id=1, source_target_pairs={{0,16},{16,0},{32,48},{48,32},{64,80},{80,64},{96,112},{112,96},{1... | collective-permute-start | bytes 393224 | tf_op jit(solution)/shard_map/ppermute | solution.py:40
  148.6 12.2 %collective-permute-start.45 = (bf16[128,512]{1,0:T(8,128)(2,1)S(1)}, bf16[128,512]{1,0:T(8,128)(2,1)S(1)}, u32[]{:S(2)}, u32[]{:S(2)}) collective-permute-start(bf16[128,512]{1,0:T(8,128)(2,1)S(1)} %get-tuple-element.89), channel_id=1, source_target_pairs={{0,112},{16,96},{32,16},{48,0},{64,48},{80,32},{96,80},{112,64},{1... | collective-permute-start | bytes 393224 | tf_op jit(solution)/shard_map/ppermute | solution.py:40
  149.9 23.0 %collective-permute-start.36 = (bf16[128,512]{1,0:T(8,128)(2,1)S(1)}, bf16[128,512]{1,0:T(8,128)(2,1)S(1)}, u32[]{:S(2)}, u32[]{:S(2)}) collective-permute-start(bf16[128,512]{1,0:T(8,128)(2,1)S(1)} %get-tuple-element.82.refs_5_), channel_id=1, source_target_pairs={{0,96},{32,0},{64,32},{96,64},{1,97},{33,1},{65,33},{97,65},{2,98}... | collective-permute-start | bytes 393224 | tf_op jit(solution)/shard_map/ppermute | solution.py:35
  151.7 21.2 %collective-permute-start.46 = (bf16[128,512]{1,0:T(8,128)(2,1)S(1)}, bf16[128,512]{1,0:T(8,128)(2,1)S(1)}, u32[]{:S(2)}, u32[]{:S(2)}) collective-permute-start(bf16[128,512]{1,0:T(8,128)(2,1)S(1)} %get-tuple-element.90), channel_id=1, source_target_pairs={{0,48},{16,32},{32,80},{48,64},{64,112},{80,96},{96,16},{112,0},{1... | collective-permute-start | bytes 393224 | tf_op jit(solution)/shard_map/ppermute | solution.py:40
  155.9 16.9 %collective-permute-start.41 = (bf16[128,512]{1,0:T(8,128)(2,1)S(1)}, bf16[128,512]{1,0:T(8,128)(2,1)S(1)}, u32[]{:S(2)}, u32[]{:S(2)}) collective-permute-start(bf16[128,512]{1,0:T(8,128)(2,1)S(1)} %get-tuple-element.85.refs_5_), channel_id=1, source_target_pairs={{0,32},{32,64},{64,96},{96,0},{1,33},{33,65},{65,97},{97,1},{2,34}... | collective-permute-start | bytes 393224 | tf_op jit(solution)/shard_map/ppermute | solution.py:35
  158.8 14.1 %collective-permute-start.47 = (bf16[128,512]{1,0:T(8,128)(2,1)S(1)}, bf16[128,512]{1,0:T(8,128)(2,1)S(1)}, u32[]{:S(2)}, u32[]{:S(2)}) collective-permute-start(bf16[128,512]{1,0:T(8,128)(2,1)S(1)} %get-tuple-element.91), channel_id=1, source_target_pairs={{0,80},{16,64},{32,112},{48,96},{64,16},{80,0},{96,48},{112,32},{1... | collective-permute-start | bytes 393224 | tf_op jit(solution)/shard_map/ppermute | solution.py:40
  160.8 12.1 %collective-permute-start.43 = (bf16[128,512]{1,0:T(8,128)(2,1)S(1)}, bf16[128,512]{1,0:T(8,128)(2,1)S(1)}, u32[]{:S(2)}, u32[]{:S(2)}) collective-permute-start(bf16[128,512]{1,0:T(8,128)(2,1)S(1)} %get-tuple-element.87.refs_9_), channel_id=1, source_target_pairs={{0,64},{32,96},{64,0},{96,32},{1,65},{33,97},{65,1},{97,33},{2,66}... | collective-permute-start | bytes 393224 | tf_op jit(solution)/shard_map/ppermute | solution.py:35
  (24 other events, 169.4 us)

commit v5 on v4

--- a/solution.py
+++ b/solution.py
@@ -23,9 +23,9 @@
 CHUNKS = ((0,), (3,), (1,), (2,))
 GROUPS = ((0,), (1,), (2,), (3,))
 ORDER = (
-    ("F", 0), ("C", 1), ("C", 2), ("S1", 0), ("F", 1), ("S2", 0), ("F", 2), ("C", 3),
-    ("S1", 1), ("ACT", 0), ("S1", 2), ("F", 3), ("S2", 1), ("S2", 2), ("S1", 3), ("ACT", 1),
-    ("S2", 3), ("ASM", 0), ("ACT", 2), ("ASM", 1), ("BACK", 0), ("ACT", 3), ("ASM", 2), ("BACK", 1),
+    ("F", 0), ("C", 1), ("S1", 0), ("C", 2), ("F", 1), ("S2", 0), ("F", 2), ("C", 3),
+    ("S1", 1), ("ACT", 0), ("S1", 2), ("F", 3), ("S2", 1), ("S2", 2), ("S1", 3), ("S2", 3),
+    ("ACT", 1), ("ASM", 0), ("ACT", 2), ("ASM", 1), ("BACK", 0), ("ACT", 3), ("ASM", 2), ("BACK", 1),
     ("ASM", 3), ("BACK", 2), ("BACK", 3), ("WG", 0),
 )
 

time: 174 us -> 172 us (0.989)
  starting transfers between devices: 60.4 us -> 58.3 us
    ppermute x20, waiting for transfers between devices: 22.6 us -> 19.3 us  [move(): return lax.ppermute(a, axis, [(i, (i + by) % n) for i in range(n)])]
    ppermute x24, waiting for transfers between devices: 40.2 us -> 42.9 us  [step(): return lax.ppermute(a, ('y', 'core'), pairs)]
  transfers between devices with their start and end apart: 48 -> 48, of which waited for: 21 -> 18; matrix products, arithmetic and copies ran while one was open for 0% -> 0% of each run, Pallas kernels for 24% -> 24%
where the time goes in v5:
time: 172 us
  waiting for transfers between devices  62.2 us (36%)
  starting transfers between devices  58.3 us (34%)
  Pallas kernels  43.5 us (25%)
  local copies, waits for them, and re-layouts  6.33 us (4%)
    ppermute x24, waiting for transfers between devices, step(): return lax.ppermute(a, ('y', 'core'), pairs)  42.9 us
    pallas_call x30, Pallas kernels, call(): pl.pallas_call(kernel, in_specs=[smem] + [in_space] * n + [anywhere] * m,...  32 us
    ppermute x24, starting transfers between devices, step(): return lax.ppermute(a, ('y', 'core'), pairs)  29.8 us
    ppermute x20, waiting for transfers between devices, move(): return lax.ppermute(a, axis, [(i, (i + by) % n) for i in range(n)])  19.3 us
    ppermute x20, starting transfers between devices, move(): return lax.ppermute(a, axis, [(i, (i + by) % n) for i in range(n)])  18.4 us
    pallas_call x2, Pallas kernels, weight_grads(): pl.pallas_call(kernel, in_specs=[smem] + [vmem] * given + [anywhere] * (l...  10.2 us
    ppermute x4, starting transfers between devices, move2(): return lax.ppermute(a, ('z', 'xh'), pairs)  10 us
    unnamed x16, local copies, waits for them, and re-layouts  6.33 us
  transfers between devices with their start and end apart: 48, of which 18 were waited for; matrix products, arithmetic and copies ran while one was open for 0% of the time, Pallas kernels for 24%

profile of v5, /device:TPU:0, one launch (start us, length us, event | category | flops | bytes accessed | tf_op | source)
XLA Modules:
  0.0 171.5 jit_solution(16128369728463142950)
XLA Ops:
  3.4 3.2 %collective-permute-start = (bf16[128,1024]{1,0:T(8,128)(2,1)S(1)}, bf16[128,1024]{1,0:T(8,128)(2,1)S(1)}, u32[]{:S(2)}, u32[]{:S(2)}) collective-permute-start(bf16[128,1024]{1,0:T(8,128)(2,1)S(1)} %rows.1.refs_1_.r_4_), channel_id=1, source_target_pairs={{0,16},{16,0},{1,17},{17,1},{2,18},{18,2},{3,19},{19,3},{4,20},{20... | collective-permute-start | bytes 786440 | tf_op jit(solution)/shard_map/ppermute | solution.py:35
  13.7 2.1 %collective-permute-start.5 = (bf16[256,1024]{1,0:T(8,128)(2,1)S(1)}, bf16[256,1024]{1,0:T(8,128)(2,1)S(1)}, u32[]{:S(2)}, u32[]{:S(2)}) collective-permute-start(bf16[256,1024]{1,0:T(8,128)(2,1)S(1)} %get-tuple-element.52.refs_1_.refs_5_), channel_id=1, source_target_pairs={{0,32},{32,64},{64,96},{96,0},{1,33},{33,65},{65,97},{97,1},{2,34}... | collective-permute-start | bytes 1572872 | tf_op jit(solution)/shard_map/ppermute | solution.py:35
  15.9 2.2 %collective-permute-start.8 = (bf16[256,1024]{1,0:T(8,128)(2,1)S(1)}, bf16[256,1024]{1,0:T(8,128)(2,1)S(1)}, u32[]{:S(2)}, u32[]{:S(2)}) collective-permute-start(bf16[256,1024]{1,0:T(8,128)(2,1)S(1)} %get-tuple-element.52.refs_1_.refs_5_), channel_id=1, source_target_pairs={{0,96},{32,0},{64,32},{96,64},{1,97},{33,1},{65,33},{97,65},{2,98}... | collective-permute-start | bytes 1572872 | tf_op jit(solution)/shard_map/ppermute | solution.py:35
  18.4 2.4 %forward.4 = (f32[64,2688]{1,0:T(8,128)S(1)}, f32[64,2688]{1,0:T(8,128)S(1)}, bf16[64,2688]{1,0:T(8,128)(2,1)S(1)}, bf16[64,2688]{1,0:T(8,128)(2,1)S(1)}) custom-call(s32[3]{0:T(128)S(1)} %pad_add_fusion.refs_0_.r_0_, bf16[256,1024]{1,0:T(8,128)(2,1)S(1)} %get-tuple-element.52.refs_1_.refs_5_, bf16[256,1024]{1,0:T(8,128)(2,1)S(1)} %collective-permute-done.1.refs_2_, ...), custom_call_target="tpu_custom_call" | custom-call | tf_op jit(solution)/shard_map/forward/pallas_call | solution.py:62
  22.4 8.1 %collective-permute-done.5.refs_1_ = bf16[256,1024]{1,0:T(8,128)(2,1)S(1)} collective-permute-done((bf16[256,1024]{1,0:T(8,128)(2,1)S(1)}, bf16[256,1024]{1,0:T(8,128)(2,1)S(1)}, u32[]{:S(2)}, u32[]{:S(2)}) %collective-permute-start.5) | collective-permute-done | bytes 524320 | tf_op jit(solution)/shard_map/ppermute | solution.py:35
  34.6 3.0 %collective-permute-start.3 = (bf16[64,2688]{1,0:T(8,128)(2,1)S(1)}, bf16[64,2688]{1,0:T(8,128)(2,1)S(1)}, u32[]{:S(2)}, u32[]{:S(2)}) collective-permute-start(bf16[64,2688]{1,0:T(8,128)(2,1)S(1)} %get-tuple-element.55), channel_id=1, source_target_pairs={{0,12},{4,0},{8,4},{12,8},{1,5},{5,9},{9,13},{13,1},{2,14},{6,2},{... | collective-permute-start | bytes 1032200 | tf_op jit(solution)/shard_map/ppermute | solution.py:46
  37.6 2.3 %forward.5 = (f32[64,2688]{1,0:T(8,128)S(1)}, f32[64,2688]{1,0:T(8,128)S(1)}, bf16[64,2688]{1,0:T(8,128)(2,1)S(1)}, bf16[64,2688]{1,0:T(8,128)(2,1)S(1)}) custom-call(s32[3]{0:T(128)S(1)} %pad_add_fusion.refs_0_.r_0_, bf16[256,1024]{1,0:T(8,128)(2,1)S(1)} %get-tuple-element.58.refs_3_.refs_1_.refs_6_, bf16[256,1024]{1,0:T(8,128)(2,1)S(1)} %collective-permute-done.7.refs_2_, ...), custom_call_target="tpu_custom_call" | custom-call | tf_op jit(solution)/shard_map/forward/pallas_call | solution.py:62
  40.0 5.5 %collective-permute-done.3.refs_2_ = bf16[64,2688]{1,0:T(8,128)(2,1)S(1)} collective-permute-done((bf16[64,2688]{1,0:T(8,128)(2,1)S(1)}, bf16[64,2688]{1,0:T(8,128)(2,1)S(1)}, u32[]{:S(2)}, u32[]{:S(2)}) %collective-permute-start.3) | collective-permute-done | bytes 344096 | tf_op jit(solution)/shard_map/ppermute | solution.py:46
  49.2 2.3 %forward.6 = (f32[64,2688]{1,0:T(8,128)S(1)}, f32[64,2688]{1,0:T(8,128)S(1)}, bf16[64,2688]{1,0:T(8,128)(2,1)S(1)}, bf16[64,2688]{1,0:T(8,128)(2,1)S(1)}) custom-call(s32[3]{0:T(128)S(1)} %pad_add_fusion.refs_0_.r_0_, bf16[256,1024]{1,0:T(8,128)(2,1)S(1)} %get-tuple-element.60.refs_7_.refs_1_, bf16[256,1024]{1,0:T(8,128)(2,1)S(1)} %collective-permute-done.12.refs_2_, ...), custom_call_target="tpu_custom_call" | custom-call | tf_op jit(solution)/shard_map/forward/pallas_call | solution.py:62
  57.5 6.3 %collective-permute-done.9.refs_2_ = f32[64,2688]{1,0:T(8,128)S(1)} collective-permute-done((f32[64,2688]{1,0:T(8,128)S(1)}, f32[64,2688]{1,0:T(8,128)S(1)}, u32[]{:S(2)}, u32[]{:S(2)}) %collective-permute-start.9) | collective-permute-done | bytes 688160 | tf_op jit(solution)/shard_map/ppermute | solution.py:35
  63.7 2.3 %collective-permute-start.23 = (bf16[64,2688]{1,0:T(8,128)(2,1)S(1)}, bf16[64,2688]{1,0:T(8,128)(2,1)S(1)}, u32[]{:S(2)}, u32[]{:S(2)}) collective-permute-start(bf16[64,2688]{1,0:T(8,128)(2,1)S(1)} %get-tuple-element.75), channel_id=1, source_target_pairs={{0,12},{4,0},{8,4},{12,8},{1,5},{5,9},{9,13},{13,1},{2,14},{6,2},{... | collective-permute-start | bytes 1032200 | tf_op jit(solution)/shard_map/ppermute | solution.py:46
  67.7 2.4 %forward.7 = (f32[64,2688]{1,0:T(8,128)S(1)}, f32[64,2688]{1,0:T(8,128)S(1)}, bf16[64,2688]{1,0:T(8,128)(2,1)S(1)}, bf16[64,2688]{1,0:T(8,128)(2,1)S(1)}) custom-call(s32[3]{0:T(128)S(1)} %pad_add_fusion.refs_0_.r_0_, bf16[256,1024]{1,0:T(8,128)(2,1)S(1)} %get-tuple-element.66.refs_3_.refs_1_.refs_8_, bf16[256,1024]{1,0:T(8,128)(2,1)S(1)} %collective-permute-done.18.refs_2_, ...), custom_call_target="tpu_custom_call" | custom-call | tf_op jit(solution)/shard_map/forward/pallas_call | solution.py:62
  74.8 3.4 %collective-permute-start.21 = (bf16[64,2688]{1,0:T(8,128)(2,1)S(1)}, bf16[64,2688]{1,0:T(8,128)(2,1)S(1)}, u32[]{:S(2)}, u32[]{:S(2)}) collective-permute-start(bf16[64,2688]{1,0:T(8,128)(2,1)S(1)} %get-tuple-element.72), channel_id=1, source_target_pairs={{0,12},{4,0},{8,4},{12,8},{1,5},{5,9},{9,13},{13,1},{2,14},{6,2},{... | collective-permute-start | bytes 1032200 | tf_op jit(solution)/shard_map/ppermute | solution.py:46
  78.9 3.7 %collective-permute-done.22.refs_2_ = bf16[64,2688]{1,0:T(8,128)(2,1)S(1)} collective-permute-done((bf16[64,2688]{1,0:T(8,128)(2,1)S(1)}, bf16[64,2688]{1,0:T(8,128)(2,1)S(1)}, u32[]{:S(2)}, u32[]{:S(2)}) %collective-permute-start.22) | collective-permute-done | bytes 344096 | tf_op jit(solution)/shard_map/ppermute | solution.py:46
  83.8 2.7 %collective-permute-start.13 = (bf16[64,2688]{1,0:T(8,128)(2,1)S(1)}, bf16[64,2688]{1,0:T(8,128)(2,1)S(1)}, u32[]{:S(2)}, u32[]{:S(2)}) collective-permute-start(bf16[64,2688]{1,0:T(8,128)(2,1)S(1)} %activate.4.refs_3_.refs_1_), channel_id=1, source_target_pairs={{0,12},{4,0},{8,4},{12,8},{1,5},{5,9},{9,13},{13,1},{2,14},{6,2},{... | collective-permute-start | bytes 1032200 | tf_op jit(solution)/shard_map/ppermute | solution.py:46
  86.5 1.9 %collective-permute-done.14.refs_4_ = bf16[64,2688]{1,0:T(8,128)(2,1)S(1)} collective-permute-done((bf16[64,2688]{1,0:T(8,128)(2,1)S(1)}, bf16[64,2688]{1,0:T(8,128)(2,1)S(1)}, u32[]{:S(2)}, u32[]{:S(2)}) %collective-permute-start.14) | collective-permute-done | bytes 344096 | tf_op jit(solution)/shard_map/ppermute | solution.py:46
  89.4 5.2 %collective-permute-done.25.refs_3_ = bf16[64,2688]{1,0:T(8,128)(2,1)S(1)} collective-permute-done((bf16[64,2688]{1,0:T(8,128)(2,1)S(1)}, bf16[64,2688]{1,0:T(8,128)(2,1)S(1)}, u32[]{:S(2)}, u32[]{:S(2)}) %collective-permute-start.25) | collective-permute-done | bytes 344096 | tf_op jit(solution)/shard_map/ppermute | solution.py:46
  96.0 2.2 %collective-permute-done.15.refs_3_ = bf16[64,2688]{1,0:T(8,128)(2,1)S(1)} collective-permute-done((bf16[64,2688]{1,0:T(8,128)(2,1)S(1)}, bf16[64,2688]{1,0:T(8,128)(2,1)S(1)}, u32[]{:S(2)}, u32[]{:S(2)}) %collective-permute-start.15) | collective-permute-done | bytes 344096 | tf_op jit(solution)/shard_map/ppermute | solution.py:46
  99.0 1.8 %collective-permute-start.27 = (bf16[64,2688]{1,0:T(8,128)(2,1)S(1)}, bf16[64,2688]{1,0:T(8,128)(2,1)S(1)}, u32[]{:S(2)}, u32[]{:S(2)}) collective-permute-start(bf16[64,2688]{1,0:T(8,128)(2,1)S(1)} %activate.5.refs_5_.refs_1_), channel_id=1, source_target_pairs={{0,12},{4,0},{8,4},{12,8},{1,5},{5,9},{9,13},{13,1},{2,14},{6,2},{... | collective-permute-start | bytes 1032200 | tf_op jit(solution)/shard_map/ppermute | solution.py:46
  100.9 4.5 %collective-permute-done.28.refs_4_ = bf16[64,2688]{1,0:T(8,128)(2,1)S(1)} collective-permute-done((bf16[64,2688]{1,0:T(8,128)(2,1)S(1)}, bf16[64,2688]{1,0:T(8,128)(2,1)S(1)}, u32[]{:S(2)}, u32[]{:S(2)}) %collective-permute-start.28) | collective-permute-done | bytes 344096 | tf_op jit(solution)/shard_map/ppermute | solution.py:46
  107.2 2.4 %collective-permute-done.27.refs_2_ = bf16[64,2688]{1,0:T(8,128)(2,1)S(1)} collective-permute-done((bf16[64,2688]{1,0:T(8,128)(2,1)S(1)}, bf16[64,2688]{1,0:T(8,128)(2,1)S(1)}, u32[]{:S(2)}, u32[]{:S(2)}) %collective-permute-start.27) | collective-permute-done | bytes 344096 | tf_op jit(solution)/shard_map/ppermute | solution.py:46
  109.6 4.3 %collective-permute-done.29.refs_3_ = bf16[64,2688]{1,0:T(8,128)(2,1)S(1)} collective-permute-done((bf16[64,2688]{1,0:T(8,128)(2,1)S(1)}, bf16[64,2688]{1,0:T(8,128)(2,1)S(1)}, u32[]{:S(2)}, u32[]{:S(2)}) %collective-permute-start.29) | collective-permute-done | bytes 344096 | tf_op jit(solution)/shard_map/ppermute | solution.py:46
  116.6 4.2 %collective-permute-done.35.refs_2_ = f32[64,2688]{1,0:T(8,128)S(1)} collective-permute-done((f32[64,2688]{1,0:T(8,128)S(1)}, f32[64,2688]{1,0:T(8,128)S(1)}, u32[]{:S(2)}, u32[]{:S(2)}) %collective-permute-start.35) | collective-permute-done | bytes 688160 | tf_op jit(solution)/shard_map/ppermute | solution.py:35
  121.6 3.2 %collective-permute-start.32 = (bf16[64,2688]{1,0:T(8,128)(2,1)S(1)}, bf16[64,2688]{1,0:T(8,128)(2,1)S(1)}, u32[]{:S(2)}, u32[]{:S(2)}) collective-permute-start(bf16[64,2688]{1,0:T(8,128)(2,1)S(1)} %activate.6.refs_5_.refs_1_), channel_id=1, source_target_pairs={{0,12},{4,0},{8,4},{12,8},{1,5},{5,9},{9,13},{13,1},{2,14},{6,2},{... | collective-permute-start | bytes 1032200 | tf_op jit(solution)/shard_map/ppermute | solution.py:46
  124.8 3.2 %collective-permute-start.38 = (bf16[64,2688]{1,0:T(8,128)(2,1)S(1)}, bf16[64,2688]{1,0:T(8,128)(2,1)S(1)}, u32[]{:S(2)}, u32[]{:S(2)}) collective-permute-start(bf16[64,2688]{1,0:T(8,128)(2,1)S(1)} %activate.7.refs_5_.refs_1_), channel_id=1, source_target_pairs={{0,12},{4,0},{8,4},{12,8},{1,5},{5,9},{9,13},{13,1},{2,14},{6,2},{... | collective-permute-start | bytes 1032200 | tf_op jit(solution)/shard_map/ppermute | solution.py:46
  128.1 5.7 %collective-permute-done.39.refs_4_ = bf16[64,2688]{1,0:T(8,128)(2,1)S(1)} collective-permute-done((bf16[64,2688]{1,0:T(8,128)(2,1)S(1)}, bf16[64,2688]{1,0:T(8,128)(2,1)S(1)}, u32[]{:S(2)}, u32[]{:S(2)}) %collective-permute-start.39) | collective-permute-done | bytes 344096 | tf_op jit(solution)/shard_map/ppermute | solution.py:46
  133.8 4.2 %collective-permute-done.34.refs_3_ = bf16[64,2688]{1,0:T(8,128)(2,1)S(1)} collective-permute-done((bf16[64,2688]{1,0:T(8,128)(2,1)S(1)}, bf16[64,2688]{1,0:T(8,128)(2,1)S(1)}, u32[]{:S(2)}, u32[]{:S(2)}) %collective-permute-start.34) | collective-permute-done | bytes 344096 | tf_op jit(solution)/shard_map/ppermute | solution.py:46
  143.1 2.7 %collective-permute-start.44 = (bf16[128,512]{1,0:T(8,128)(2,1)S(1)}, bf16[128,512]{1,0:T(8,128)(2,1)S(1)}, u32[]{:S(2)}, u32[]{:S(2)}) collective-permute-start(bf16[128,512]{1,0:T(8,128)(2,1)S(1)} %get-tuple-element.88), channel_id=1, source_target_pairs={{0,16},{16,0},{32,48},{48,32},{64,80},{80,64},{96,112},{112,96},{1... | collective-permute-start | bytes 393224 | tf_op jit(solution)/shard_map/ppermute | solution.py:40
  150.2 3.0 %collective-permute-start.46 = (bf16[128,512]{1,0:T(8,128)(2,1)S(1)}, bf16[128,512]{1,0:T(8,128)(2,1)S(1)}, u32[]{:S(2)}, u32[]{:S(2)}) collective-permute-start(bf16[128,512]{1,0:T(8,128)(2,1)S(1)} %get-tuple-element.90), channel_id=1, source_target_pairs={{0,48},{16,32},{32,80},{48,64},{64,112},{80,96},{96,16},{112,0},{1... | collective-permute-start | bytes 393224 | tf_op jit(solution)/shard_map/ppermute | solution.py:40
  156.0 3.2 %collective-permute-start.47 = (bf16[128,512]{1,0:T(8,128)(2,1)S(1)}, bf16[128,512]{1,0:T(8,128)(2,1)S(1)}, u32[]{:S(2)}, u32[]{:S(2)}) collective-permute-start(bf16[128,512]{1,0:T(8,128)(2,1)S(1)} %get-tuple-element.91), channel_id=1, source_target_pairs={{0,80},{16,64},{32,112},{48,96},{64,16},{80,0},{96,48},{112,32},{1... | collective-permute-start | bytes 393224 | tf_op jit(solution)/shard_map/ppermute | solution.py:40
  159.9 5.1 %weight_grads.2 = (bf16[512,1792]{1,0:T(8,128)(2,1)}, bf16[512,1792]{1,0:T(8,128)(2,1)}, bf16[1792,512]{1,0:T(8,128)(2,1)}, f32[8,128]{1,0:T(8,128)S(1)}) custom-call(s32[3]{0:T(128)S(1)} %pad_add_fusion.refs_0_.r_0_, bf16[256,2688]{1,0:T(8,128)(2,1)S(1)} %get-tuple-element.76.refs_3_.refs_1_, ...), custom_call_target="tpu_custom_call" | custom-call | tf_op jit(solution)/shard_map/weight_grads/pallas_call | solution.py:263
  165.0 5.1 %weight_grads.3 = (bf16[512,1792]{1,0:T(8,128)(2,1)}, bf16[512,1792]{1,0:T(8,128)(2,1)}, bf16[1792,512]{1,0:T(8,128)(2,1)}, f32[8,128]{1,0:T(8,128)S(1)}) custom-call(s32[3]{0:T(128)S(1)} %pad_add_fusion.refs_0_.r_0_, bf16[256,2688]{1,0:T(8,128)(2,1)S(1)} %collective-permute-done.26.refs_2_.refs_1_, ...), custom_call_target="tpu_custom_call", output_to_operand_aliasing={{0}: (9, {}), {1}: (10, {}), {2}: (11, {})} | custom-call | tf_op jit(solution)/shard_map/weight_grads/pallas_call | solution.py:263
  (114 shorter events, 56.3 us)
Async XLA Ops:
  13.7 16.8 %collective-permute-start.5 = (bf16[256,1024]{1,0:T(8,128)(2,1)S(1)}, bf16[256,1024]{1,0:T(8,128)(2,1)S(1)}, u32[]{:S(2)}, u32[]{:S(2)}) collective-permute-start(bf16[256,1024]{1,0:T(8,128)(2,1)S(1)} %get-tuple-element.52.refs_1_.refs_5_), channel_id=1, source_target_pairs={{0,32},{32,64},{64,96},{96,0},{1,33},{33,65},{65,97},{97,1},{2,34}... | collective-permute-start | bytes 1572872 | tf_op jit(solution)/shard_map/ppermute | solution.py:35
  15.9 16.0 %collective-permute-start.8 = (bf16[256,1024]{1,0:T(8,128)(2,1)S(1)}, bf16[256,1024]{1,0:T(8,128)(2,1)S(1)}, u32[]{:S(2)}, u32[]{:S(2)}) collective-permute-start(bf16[256,1024]{1,0:T(8,128)(2,1)S(1)} %get-tuple-element.52.refs_1_.refs_5_), channel_id=1, source_target_pairs={{0,96},{32,0},{64,32},{96,64},{1,97},{33,1},{65,33},{97,65},{2,98}... | collective-permute-start | bytes 1572872 | tf_op jit(solution)/shard_map/ppermute | solution.py:35
  32.4 16.8 %collective-permute-start.12 = (bf16[256,1024]{1,0:T(8,128)(2,1)S(1)}, bf16[256,1024]{1,0:T(8,128)(2,1)S(1)}, u32[]{:S(2)}, u32[]{:S(2)}) collective-permute-start(bf16[256,1024]{1,0:T(8,128)(2,1)S(1)} %get-tuple-element.64), channel_id=1, source_target_pairs={{0,1},{1,0},{2,3},{3,2},{4,5},{5,4},{6,7},{7,6},{8,9},{9,8},{10,11... | collective-permute-start | bytes 1572872 | tf_op jit(solution)/shard_map/ppermute | solution.py:35
  33.0 18.5 %collective-permute-start.11 = (bf16[256,1024]{1,0:T(8,128)(2,1)S(1)}, bf16[256,1024]{1,0:T(8,128)(2,1)S(1)}, u32[]{:S(2)}, u32[]{:S(2)}) collective-permute-start(bf16[256,1024]{1,0:T(8,128)(2,1)S(1)} %get-tuple-element.52.refs_1_.refs_5_), channel_id=1, source_target_pairs={{0,64},{32,96},{64,0},{96,32},{1,65},{33,97},{65,1},{97,33},{2,66}... | collective-permute-start | bytes 1572872 | tf_op jit(solution)/shard_map/ppermute | solution.py:35
  46.7 17.0 %collective-permute-start.9 = (f32[64,2688]{1,0:T(8,128)S(1)}, f32[64,2688]{1,0:T(8,128)S(1)}, u32[]{:S(2)}, u32[]{:S(2)}) collective-permute-start(f32[64,2688]{1,0:T(8,128)S(1)} %beside.4.refs_7_.refs_1_), channel_id=1, source_target_pairs={{0,2},{2,0},{1,3},{3,1},{4,6},{6,4},{5,7},{7,5},{8,10},{10,8},{9,1... | collective-permute-start | bytes 2064392 | tf_op jit(solution)/shard_map/ppermute | solution.py:35
  52.2 15.5 %collective-permute-start.18 = (bf16[256,1024]{1,0:T(8,128)(2,1)S(1)}, bf16[256,1024]{1,0:T(8,128)(2,1)S(1)}, u32[]{:S(2)}, u32[]{:S(2)}) collective-permute-start(bf16[256,1024]{1,0:T(8,128)(2,1)S(1)} %get-tuple-element.68), channel_id=1, source_target_pairs={{0,1},{1,0},{2,3},{3,2},{4,5},{5,4},{6,7},{7,6},{8,9},{9,8},{10,11... | collective-permute-start | bytes 1572872 | tf_op jit(solution)/shard_map/ppermute | solution.py:35
  52.3 14.5 %collective-permute-start.19 = (bf16[64,2688]{1,0:T(8,128)(2,1)S(1)}, bf16[64,2688]{1,0:T(8,128)(2,1)S(1)}, u32[]{:S(2)}, u32[]{:S(2)}) collective-permute-start(bf16[64,2688]{1,0:T(8,128)(2,1)S(1)} %get-tuple-element.70), channel_id=1, source_target_pairs={{0,4},{4,8},{8,12},{12,0},{1,13},{5,1},{9,5},{13,9},{2,6},{6,10},{... | collective-permute-start | bytes 1032200 | tf_op jit(solution)/shard_map/ppermute | solution.py:46
  53.9 17.4 %collective-permute-start.16 = (bf16[64,2688]{1,0:T(8,128)(2,1)S(1)}, bf16[64,2688]{1,0:T(8,128)(2,1)S(1)}, u32[]{:S(2)}, u32[]{:S(2)}) collective-permute-start(bf16[64,2688]{1,0:T(8,128)(2,1)S(1)} %get-tuple-element.67), channel_id=1, source_target_pairs={{0,12},{4,0},{8,4},{12,8},{1,5},{5,9},{9,13},{13,1},{2,14},{6,2},{... | collective-permute-start | bytes 1032200 | tf_op jit(solution)/shard_map/ppermute | solution.py:46
  57.4 14.0 %collective-permute-start.17 = (bf16[64,2688]{1,0:T(8,128)(2,1)S(1)}, bf16[64,2688]{1,0:T(8,128)(2,1)S(1)}, u32[]{:S(2)}, u32[]{:S(2)}) collective-permute-start(bf16[64,2688]{1,0:T(8,128)(2,1)S(1)} %add.9.refs_3_), channel_id=1, source_target_pairs={{0,4},{4,8},{8,12},{12,0},{1,13},{5,1},{9,5},{13,9},{2,6},{6,10},{... | collective-permute-start | bytes 1032200 | tf_op jit(solution)/shard_map/ppermute | solution.py:46
  63.7 11.1 %collective-permute-start.23 = (bf16[64,2688]{1,0:T(8,128)(2,1)S(1)}, bf16[64,2688]{1,0:T(8,128)(2,1)S(1)}, u32[]{:S(2)}, u32[]{:S(2)}) collective-permute-start(bf16[64,2688]{1,0:T(8,128)(2,1)S(1)} %get-tuple-element.75), channel_id=1, source_target_pairs={{0,12},{4,0},{8,4},{12,8},{1,5},{5,9},{9,13},{13,1},{2,14},{6,2},{... | collective-permute-start | bytes 1032200 | tf_op jit(solution)/shard_map/ppermute | solution.py:46
  67.4 10.8 %collective-permute-start.24 = (bf16[64,2688]{1,0:T(8,128)(2,1)S(1)}, bf16[64,2688]{1,0:T(8,128)(2,1)S(1)}, u32[]{:S(2)}, u32[]{:S(2)}) collective-permute-start(bf16[64,2688]{1,0:T(8,128)(2,1)S(1)} %add.10.refs_7_), channel_id=1, source_target_pairs={{0,4},{4,8},{8,12},{12,0},{1,13},{5,1},{9,5},{13,9},{2,6},{6,10},{... | collective-permute-start | bytes 1032200 | tf_op jit(solution)/shard_map/ppermute | solution.py:46
  70.0 12.5 %collective-permute-start.22 = (bf16[64,2688]{1,0:T(8,128)(2,1)S(1)}, bf16[64,2688]{1,0:T(8,128)(2,1)S(1)}, u32[]{:S(2)}, u32[]{:S(2)}) collective-permute-start(bf16[64,2688]{1,0:T(8,128)(2,1)S(1)} %get-tuple-element.74), channel_id=1, source_target_pairs={{0,4},{4,8},{8,12},{12,0},{1,13},{5,1},{9,5},{13,9},{2,6},{6,10},{... | collective-permute-start | bytes 1032200 | tf_op jit(solution)/shard_map/ppermute | solution.py:46
  72.0 23.2 %collective-permute-start.20 = (f32[64,2688]{1,0:T(8,128)S(1)}, f32[64,2688]{1,0:T(8,128)S(1)}, u32[]{:S(2)}, u32[]{:S(2)}) collective-permute-start(f32[64,2688]{1,0:T(8,128)S(1)} %beside.5.refs_4_.refs_1_), channel_id=1, source_target_pairs={{0,2},{2,0},{1,3},{3,1},{4,6},{6,4},{5,7},{7,5},{8,10},{10,8},{9,1... | collective-permute-start | bytes 2064392 | tf_op jit(solution)/shard_map/ppermute | solution.py:35
  73.6 14.8 %collective-permute-start.14 = (bf16[64,2688]{1,0:T(8,128)(2,1)S(1)}, bf16[64,2688]{1,0:T(8,128)(2,1)S(1)}, u32[]{:S(2)}, u32[]{:S(2)}) collective-permute-start(bf16[64,2688]{1,0:T(8,128)(2,1)S(1)} %activate.4.refs_3_.refs_1_), channel_id=1, source_target_pairs={{0,4},{4,8},{8,12},{12,0},{1,13},{5,1},{9,5},{13,9},{2,6},{6,10},{... | collective-permute-start | bytes 1032200 | tf_op jit(solution)/shard_map/ppermute | solution.py:46
  74.8 14.1 %collective-permute-start.21 = (bf16[64,2688]{1,0:T(8,128)(2,1)S(1)}, bf16[64,2688]{1,0:T(8,128)(2,1)S(1)}, u32[]{:S(2)}, u32[]{:S(2)}) collective-permute-start(bf16[64,2688]{1,0:T(8,128)(2,1)S(1)} %get-tuple-element.72), channel_id=1, source_target_pairs={{0,12},{4,0},{8,4},{12,8},{1,5},{5,9},{9,13},{13,1},{2,14},{6,2},{... | collective-permute-start | bytes 1032200 | tf_op jit(solution)/shard_map/ppermute | solution.py:46
  83.2 11.4 %collective-permute-start.25 = (bf16[64,2688]{1,0:T(8,128)(2,1)S(1)}, bf16[64,2688]{1,0:T(8,128)(2,1)S(1)}, u32[]{:S(2)}, u32[]{:S(2)}) collective-permute-start(bf16[64,2688]{1,0:T(8,128)(2,1)S(1)} %add.11.refs_4_), channel_id=1, source_target_pairs={{0,4},{4,8},{8,12},{12,0},{1,13},{5,1},{9,5},{13,9},{2,6},{6,10},{... | collective-permute-start | bytes 1032200 | tf_op jit(solution)/shard_map/ppermute | solution.py:46
  83.8 12.2 %collective-permute-start.13 = (bf16[64,2688]{1,0:T(8,128)(2,1)S(1)}, bf16[64,2688]{1,0:T(8,128)(2,1)S(1)}, u32[]{:S(2)}, u32[]{:S(2)}) collective-permute-start(bf16[64,2688]{1,0:T(8,128)(2,1)S(1)} %activate.4.refs_3_.refs_1_), channel_id=1, source_target_pairs={{0,12},{4,0},{8,4},{12,8},{1,5},{5,9},{9,13},{13,1},{2,14},{6,2},{... | collective-permute-start | bytes 1032200 | tf_op jit(solution)/shard_map/ppermute | solution.py:46
  89.0 17.5 %collective-permute-start.30 = (f32[64,2688]{1,0:T(8,128)S(1)}, f32[64,2688]{1,0:T(8,128)S(1)}, u32[]{:S(2)}, u32[]{:S(2)}) collective-permute-start(f32[64,2688]{1,0:T(8,128)S(1)} %beside.6.refs_3_.refs_1_), channel_id=1, source_target_pairs={{0,2},{2,0},{1,3},{3,1},{4,6},{6,4},{5,7},{7,5},{8,10},{10,8},{9,1... | collective-permute-start | bytes 2064392 | tf_op jit(solution)/shard_map/ppermute | solution.py:35
  98.9 15.8 %collective-permute-start.26 = (bf16[256,2688]{1,0:T(8,128)(2,1)S(1)}, bf16[256,2688]{1,0:T(8,128)(2,1)S(1)}, u32[]{:S(2)}, u32[]{:S(2)}) collective-permute-start(bf16[256,2688]{1,0:T(8,128)(2,1)S(1)} %get-tuple-element.77), channel_id=1, source_target_pairs={{0,1},{1,0},{2,3},{3,2},{4,5},{5,4},{6,7},{7,6},{8,9},{9,8},{10,11... | collective-permute-start | bytes 4128776 | tf_op jit(solution)/shard_map/ppermute | solution.py:35
  105.4 15.4 %collective-permute-start.35 = (f32[64,2688]{1,0:T(8,128)S(1)}, f32[64,2688]{1,0:T(8,128)S(1)}, u32[]{:S(2)}, u32[]{:S(2)}) collective-permute-start(f32[64,2688]{1,0:T(8,128)S(1)} %beside.7.refs_3_.refs_1_), channel_id=1, source_target_pairs={{0,2},{2,0},{1,3},{3,1},{4,6},{6,4},{5,7},{7,5},{8,10},{10,8},{9,1... | collective-permute-start | bytes 2064392 | tf_op jit(solution)/shard_map/ppermute | solution.py:35
  114.6 24.4 %collective-permute-start.31 = (bf16[256,2688]{1,0:T(8,128)(2,1)S(1)}, bf16[256,2688]{1,0:T(8,128)(2,1)S(1)}, u32[]{:S(2)}, u32[]{:S(2)}) collective-permute-start(bf16[256,2688]{1,0:T(8,128)(2,1)S(1)} %get-tuple-element.80), channel_id=1, source_target_pairs={{0,1},{1,0},{2,3},{3,2},{4,5},{5,4},{6,7},{7,6},{8,9},{9,8},{10,11... | collective-permute-start | bytes 4128776 | tf_op jit(solution)/shard_map/ppermute | solution.py:35
  121.5 12.3 %collective-permute-start.39 = (bf16[64,2688]{1,0:T(8,128)(2,1)S(1)}, bf16[64,2688]{1,0:T(8,128)(2,1)S(1)}, u32[]{:S(2)}, u32[]{:S(2)}) collective-permute-start(bf16[64,2688]{1,0:T(8,128)(2,1)S(1)} %activate.7.refs_5_.refs_1_), channel_id=1, source_target_pairs={{0,4},{4,8},{8,12},{12,0},{1,13},{5,1},{9,5},{13,9},{2,6},{6,10},{... | collective-permute-start | bytes 1032200 | tf_op jit(solution)/shard_map/ppermute | solution.py:46
  121.6 12.2 %collective-permute-start.32 = (bf16[64,2688]{1,0:T(8,128)(2,1)S(1)}, bf16[64,2688]{1,0:T(8,128)(2,1)S(1)}, u32[]{:S(2)}, u32[]{:S(2)}) collective-permute-start(bf16[64,2688]{1,0:T(8,128)(2,1)S(1)} %activate.6.refs_5_.refs_1_), channel_id=1, source_target_pairs={{0,12},{4,0},{8,4},{12,8},{1,5},{5,9},{9,13},{13,1},{2,14},{6,2},{... | collective-permute-start | bytes 1032200 | tf_op jit(solution)/shard_map/ppermute | solution.py:46
  124.8 13.2 %collective-permute-start.34 = (bf16[64,2688]{1,0:T(8,128)(2,1)S(1)}, bf16[64,2688]{1,0:T(8,128)(2,1)S(1)}, u32[]{:S(2)}, u32[]{:S(2)}) collective-permute-start(bf16[64,2688]{1,0:T(8,128)(2,1)S(1)} %collective-permute-done.33.refs_4_), channel_id=1, source_target_pairs={{0,4},{4,8},{8,12},{12,0},{1,13},{5,1},{9,5},{13,9},{2,6},{6,10},{... | collective-permute-start | bytes 1032200 | tf_op jit(solution)/shard_map/ppermute | solution.py:46
  124.8 16.0 %collective-permute-start.38 = (bf16[64,2688]{1,0:T(8,128)(2,1)S(1)}, bf16[64,2688]{1,0:T(8,128)(2,1)S(1)}, u32[]{:S(2)}, u32[]{:S(2)}) collective-permute-start(bf16[64,2688]{1,0:T(8,128)(2,1)S(1)} %activate.7.refs_5_.refs_1_), channel_id=1, source_target_pairs={{0,12},{4,0},{8,4},{12,8},{1,5},{5,9},{9,13},{13,1},{2,14},{6,2},{... | collective-permute-start | bytes 1032200 | tf_op jit(solution)/shard_map/ppermute | solution.py:46
  143.1 12.9 %collective-permute-start.44 = (bf16[128,512]{1,0:T(8,128)(2,1)S(1)}, bf16[128,512]{1,0:T(8,128)(2,1)S(1)}, u32[]{:S(2)}, u32[]{:S(2)}) collective-permute-start(bf16[128,512]{1,0:T(8,128)(2,1)S(1)} %get-tuple-element.88), channel_id=1, source_target_pairs={{0,16},{16,0},{32,48},{48,32},{64,80},{80,64},{96,112},{112,96},{1... | collective-permute-start | bytes 393224 | tf_op jit(solution)/shard_map/ppermute | solution.py:40
  145.8 13.4 %collective-permute-start.45 = (bf16[128,512]{1,0:T(8,128)(2,1)S(1)}, bf16[128,512]{1,0:T(8,128)(2,1)S(1)}, u32[]{:S(2)}, u32[]{:S(2)}) collective-permute-start(bf16[128,512]{1,0:T(8,128)(2,1)S(1)} %get-tuple-element.89), channel_id=1, source_target_pairs={{0,112},{16,96},{32,16},{48,0},{64,48},{80,32},{96,80},{112,64},{1... | collective-permute-start | bytes 393224 | tf_op jit(solution)/shard_map/ppermute | solution.py:40
  146.9 23.3 %collective-permute-start.36 = (bf16[128,512]{1,0:T(8,128)(2,1)S(1)}, bf16[128,512]{1,0:T(8,128)(2,1)S(1)}, u32[]{:S(2)}, u32[]{:S(2)}) collective-permute-start(bf16[128,512]{1,0:T(8,128)(2,1)S(1)} %get-tuple-element.82.refs_5_), channel_id=1, source_target_pairs={{0,96},{32,0},{64,32},{96,64},{1,97},{33,1},{65,33},{97,65},{2,98}... | collective-permute-start | bytes 393224 | tf_op jit(solution)/shard_map/ppermute | solution.py:35
  150.2 20.0 %collective-permute-start.46 = (bf16[128,512]{1,0:T(8,128)(2,1)S(1)}, bf16[128,512]{1,0:T(8,128)(2,1)S(1)}, u32[]{:S(2)}, u32[]{:S(2)}) collective-permute-start(bf16[128,512]{1,0:T(8,128)(2,1)S(1)} %get-tuple-element.90), channel_id=1, source_target_pairs={{0,48},{16,32},{32,80},{48,64},{64,112},{80,96},{96,16},{112,0},{1... | collective-permute-start | bytes 393224 | tf_op jit(solution)/shard_map/ppermute | solution.py:40
  153.2 17.0 %collective-permute-start.41 = (bf16[128,512]{1,0:T(8,128)(2,1)S(1)}, bf16[128,512]{1,0:T(8,128)(2,1)S(1)}, u32[]{:S(2)}, u32[]{:S(2)}) collective-permute-start(bf16[128,512]{1,0:T(8,128)(2,1)S(1)} %get-tuple-element.85.refs_5_), channel_id=1, source_target_pairs={{0,32},{32,64},{64,96},{96,0},{1,33},{33,65},{65,97},{97,1},{2,34}... | collective-permute-start | bytes 393224 | tf_op jit(solution)/shard_map/ppermute | solution.py:35
  156.0 14.1 %collective-permute-start.47 = (bf16[128,512]{1,0:T(8,128)(2,1)S(1)}, bf16[128,512]{1,0:T(8,128)(2,1)S(1)}, u32[]{:S(2)}, u32[]{:S(2)}) collective-permute-start(bf16[128,512]{1,0:T(8,128)(2,1)S(1)} %get-tuple-element.91), channel_id=1, source_target_pairs={{0,80},{16,64},{32,112},{48,96},{64,16},{80,0},{96,48},{112,32},{1... | collective-permute-start | bytes 393224 | tf_op jit(solution)/shard_map/ppermute | solution.py:40
  159.3 10.9 %collective-permute-start.43 = (bf16[128,512]{1,0:T(8,128)(2,1)S(1)}, bf16[128,512]{1,0:T(8,128)(2,1)S(1)}, u32[]{:S(2)}, u32[]{:S(2)}) collective-permute-start(bf16[128,512]{1,0:T(8,128)(2,1)S(1)} %get-tuple-element.87.refs_9_), channel_id=1, source_target_pairs={{0,64},{32,96},{64,0},{96,32},{1,65},{33,97},{65,1},{97,33},{2,66}... | collective-permute-start | bytes 393224 | tf_op jit(solution)/shard_map/ppermute | solution.py:35
  (24 other events, 165.9 us)

commit v6 on v5

--- a/solution.py
+++ b/solution.py
@@ -106,17 +106,10 @@
         turned[32 * t : 32 * t + 32, :] = both
 
 
-def turn_kernel(ids, *refs):
-    parts, (out, turned) = refs[:-2], refs[-2:]
-    n = len(parts)
-    for b in range(8):
-        t = (4 - b // 2) % 4 * 2 + b % 2
-        for m, p in enumerate(parts):
-            rows = p[32 * b : 32 * b + 32, :]
-            at = 32 * (n * b + m)
-            out[at : at + 32, :] = rows
-            at = 32 * (n * t + m)
-            turned[at : at + 32, :] = rows
+def turn_kernel(ids, rows, turned):
+    for j in range(4):
+        t = (4 - j) % 4
+        turned[64 * t : 64 * t + 64, :] = rows[64 * j : 64 * j + 64, :]
 
 
 def send_kernel(ids, wg, wu, wd, out, turn, sems):
@@ -310,9 +303,9 @@
             us = [32 * len(CHUNKS[i]) for i in GROUPS[k]]
             count = 8 * sum(us)
         if stage == "C":
-            parts = [placed[a] for a in CHUNKS[k]]
-            outs = call("turn", turn_kernel, ids, parts, [shape(8 * u, 2 * D)] * 2, last)
-            own[k], oth[k] = outs[0], move(outs[1], "core", 1)
+            own[k] = placed[CHUNKS[k][0]]
+            outs = call("turn", turn_kernel, ids, [own[k]], [shape(8 * u, 2 * D)], last)
+            oth[k] = move(outs[0], "core", 1)
         elif stage == "F":
             outs = call(
                 "forward", forward_kernel, ids, [own[k], oth[k], wg, wu, wd, wr],

time: 172 us -> 172 us (level)
  no operation moved by 1% of the time
where the time goes in v6:
time: 172 us; the launch traced here: 171 us
  waiting for transfers between devices  62.7 us (36%)
  starting transfers between devices  57.8 us (34%)
  Pallas kernels  43.3 us (25%)
  local copies, waits for them, and re-layouts  6.33 us (4%)
    ppermute x24, waiting for transfers between devices, step(): return lax.ppermute(a, ('y', 'core'), pairs)  43.5 us
    pallas_call x30, Pallas kernels, call(): pl.pallas_call(kernel, in_specs=[smem] + [in_space] * n + [anywhere] * m,...  31.9 us
    ppermute x24, starting transfers between devices, step(): return lax.ppermute(a, ('y', 'core'), pairs)  29.5 us
    ppermute x20, waiting for transfers between devices, move(): return lax.ppermute(a, axis, [(i, (i + by) % n) for i in range(n)])  19.2 us
    ppermute x20, starting transfers between devices, move(): return lax.ppermute(a, axis, [(i, (i + by) % n) for i in range(n)])  18.2 us
    pallas_call x2, Pallas kernels, weight_grads(): pl.pallas_call(kernel, in_specs=[smem] + [vmem] * given + [anywhere] * (l...  10.2 us
    ppermute x4, starting transfers between devices, move2(): return lax.ppermute(a, ('z', 'xh'), pairs)  10.1 us
    unnamed x16, local copies, waits for them, and re-layouts  6.33 us
  transfers between devices with their start and end apart: 48, of which 18 were waited for; matrix products, arithmetic and copies ran while one was open for 0% of the time, Pallas kernels for 24%

profile of v6, /device:TPU:0, one launch (start us, length us, event | category | flops | bytes accessed | tf_op | source)
XLA Modules:
  0.0 171.4 jit_solution(5206009010144257542)
XLA Ops:
  3.4 3.2 %collective-permute-start = (bf16[128,1024]{1,0:T(8,128)(2,1)S(1)}, bf16[128,1024]{1,0:T(8,128)(2,1)S(1)}, u32[]{:S(2)}, u32[]{:S(2)}) collective-permute-start(bf16[128,1024]{1,0:T(8,128)(2,1)S(1)} %rows.1.refs_1_.r_4_), channel_id=1, source_target_pairs={{0,16},{16,0},{1,17},{17,1},{2,18},{18,2},{3,19},{19,3},{4,20},{20... | collective-permute-start | bytes 786440 | tf_op jit(solution)/shard_map/ppermute | solution.py:35
  13.7 2.1 %collective-permute-start.5 = (bf16[256,1024]{1,0:T(8,128)(2,1)S(1)}, bf16[256,1024]{1,0:T(8,128)(2,1)S(1)}, u32[]{:S(2)}, u32[]{:S(2)}) collective-permute-start(bf16[256,1024]{1,0:T(8,128)(2,1)S(1)} %get-tuple-element.46.refs_1_.refs_5_), channel_id=1, source_target_pairs={{0,32},{32,64},{64,96},{96,0},{1,33},{33,65},{65,97},{97,1},{2,34}... | collective-permute-start | bytes 1572872 | tf_op jit(solution)/shard_map/ppermute | solution.py:35
  15.9 2.2 %collective-permute-start.8 = (bf16[256,1024]{1,0:T(8,128)(2,1)S(1)}, bf16[256,1024]{1,0:T(8,128)(2,1)S(1)}, u32[]{:S(2)}, u32[]{:S(2)}) collective-permute-start(bf16[256,1024]{1,0:T(8,128)(2,1)S(1)} %get-tuple-element.46.refs_1_.refs_5_), channel_id=1, source_target_pairs={{0,96},{32,0},{64,32},{96,64},{1,97},{33,1},{65,33},{97,65},{2,98}... | collective-permute-start | bytes 1572872 | tf_op jit(solution)/shard_map/ppermute | solution.py:35
  18.4 2.4 %forward.4 = (f32[64,2688]{1,0:T(8,128)S(1)}, f32[64,2688]{1,0:T(8,128)S(1)}, bf16[64,2688]{1,0:T(8,128)(2,1)S(1)}, bf16[64,2688]{1,0:T(8,128)(2,1)S(1)}) custom-call(s32[3]{0:T(128)S(1)} %pad_add_fusion.refs_0_.r_0_, bf16[256,1024]{1,0:T(8,128)(2,1)S(1)} %get-tuple-element.46.refs_1_.refs_5_, bf16[256,1024]{1,0:T(8,128)(2,1)S(1)} %collective-permute-done.1.refs_2_, ...), custom_call_target="tpu_custom_call" | custom-call | tf_op jit(solution)/shard_map/forward/pallas_call | solution.py:62
  22.4 8.1 %collective-permute-done.5.refs_1_.refs_6_ = bf16[256,1024]{1,0:T(8,128)(2,1)S(1)} collective-permute-done((bf16[256,1024]{1,0:T(8,128)(2,1)S(1)}, bf16[256,1024]{1,0:T(8,128)(2,1)S(1)}, u32[]{:S(2)}, u32[]{:S(2)}) %collective-permute-start.5) | collective-permute-done | bytes 524320 | tf_op jit(solution)/shard_map/ppermute | solution.py:35
  34.5 3.0 %collective-permute-start.3 = (bf16[64,2688]{1,0:T(8,128)(2,1)S(1)}, bf16[64,2688]{1,0:T(8,128)(2,1)S(1)}, u32[]{:S(2)}, u32[]{:S(2)}) collective-permute-start(bf16[64,2688]{1,0:T(8,128)(2,1)S(1)} %get-tuple-element.49), channel_id=1, source_target_pairs={{0,12},{4,0},{8,4},{12,8},{1,5},{5,9},{9,13},{13,1},{2,14},{6,2},{... | collective-permute-start | bytes 1032200 | tf_op jit(solution)/shard_map/ppermute | solution.py:46
  37.6 2.3 %forward.5 = (f32[64,2688]{1,0:T(8,128)S(1)}, f32[64,2688]{1,0:T(8,128)S(1)}, bf16[64,2688]{1,0:T(8,128)(2,1)S(1)}, bf16[64,2688]{1,0:T(8,128)(2,1)S(1)}) custom-call(s32[3]{0:T(128)S(1)} %pad_add_fusion.refs_0_.r_0_, bf16[256,1024]{1,0:T(8,128)(2,1)S(1)} %collective-permute-done.5.refs_1_.refs_6_, bf16[256,1024]{1,0:T(8,128)(2,1)S(1)} %collective-permute-done.7.refs_2_, ...), custom_call_target="tpu_custom_call" | custom-call | tf_op jit(solution)/shard_map/forward/pallas_call | solution.py:62
  39.9 5.4 %collective-permute-done.3.refs_2_ = bf16[64,2688]{1,0:T(8,128)(2,1)S(1)} collective-permute-done((bf16[64,2688]{1,0:T(8,128)(2,1)S(1)}, bf16[64,2688]{1,0:T(8,128)(2,1)S(1)}, u32[]{:S(2)}, u32[]{:S(2)}) %collective-permute-start.3) | collective-permute-done | bytes 344096 | tf_op jit(solution)/shard_map/ppermute | solution.py:46
  49.1 2.3 %forward.6 = (f32[64,2688]{1,0:T(8,128)S(1)}, f32[64,2688]{1,0:T(8,128)S(1)}, bf16[64,2688]{1,0:T(8,128)(2,1)S(1)}, bf16[64,2688]{1,0:T(8,128)(2,1)S(1)}) custom-call(s32[3]{0:T(128)S(1)} %pad_add_fusion.refs_0_.r_0_, bf16[256,1024]{1,0:T(8,128)(2,1)S(1)} %collective-permute-done.8.refs_1_.refs_7_, bf16[256,1024]{1,0:T(8,128)(2,1)S(1)} %collective-permute-done.12.refs_2_, ...), custom_call_target="tpu_custom_call" | custom-call | tf_op jit(solution)/shard_map/forward/pallas_call | solution.py:62
  57.4 6.3 %collective-permute-done.9.refs_2_ = f32[64,2688]{1,0:T(8,128)S(1)} collective-permute-done((f32[64,2688]{1,0:T(8,128)S(1)}, f32[64,2688]{1,0:T(8,128)S(1)}, u32[]{:S(2)}, u32[]{:S(2)}) %collective-permute-start.9) | collective-permute-done | bytes 688160 | tf_op jit(solution)/shard_map/ppermute | solution.py:35
  63.7 2.5 %collective-permute-start.23 = (bf16[64,2688]{1,0:T(8,128)(2,1)S(1)}, bf16[64,2688]{1,0:T(8,128)(2,1)S(1)}, u32[]{:S(2)}, u32[]{:S(2)}) collective-permute-start(bf16[64,2688]{1,0:T(8,128)(2,1)S(1)} %get-tuple-element.63), channel_id=1, source_target_pairs={{0,12},{4,0},{8,4},{12,8},{1,5},{5,9},{9,13},{13,1},{2,14},{6,2},{... | collective-permute-start | bytes 1032200 | tf_op jit(solution)/shard_map/ppermute | solution.py:46
  67.7 2.4 %forward.7 = (f32[64,2688]{1,0:T(8,128)S(1)}, f32[64,2688]{1,0:T(8,128)S(1)}, bf16[64,2688]{1,0:T(8,128)(2,1)S(1)}, bf16[64,2688]{1,0:T(8,128)(2,1)S(1)}) custom-call(s32[3]{0:T(128)S(1)} %pad_add_fusion.refs_0_.r_0_, bf16[256,1024]{1,0:T(8,128)(2,1)S(1)} %collective-permute-done.11.refs_1_.refs_8_, bf16[256,1024]{1,0:T(8,128)(2,1)S(1)} %collective-permute-done.18.refs_2_, ...), custom_call_target="tpu_custom_call" | custom-call | tf_op jit(solution)/shard_map/forward/pallas_call | solution.py:62
  74.8 3.5 %collective-permute-start.21 = (bf16[64,2688]{1,0:T(8,128)(2,1)S(1)}, bf16[64,2688]{1,0:T(8,128)(2,1)S(1)}, u32[]{:S(2)}, u32[]{:S(2)}) collective-permute-start(bf16[64,2688]{1,0:T(8,128)(2,1)S(1)} %get-tuple-element.60), channel_id=1, source_target_pairs={{0,12},{4,0},{8,4},{12,8},{1,5},{5,9},{9,13},{13,1},{2,14},{6,2},{... | collective-permute-start | bytes 1032200 | tf_op jit(solution)/shard_map/ppermute | solution.py:46
  78.9 3.8 %collective-permute-done.22.refs_2_ = bf16[64,2688]{1,0:T(8,128)(2,1)S(1)} collective-permute-done((bf16[64,2688]{1,0:T(8,128)(2,1)S(1)}, bf16[64,2688]{1,0:T(8,128)(2,1)S(1)}, u32[]{:S(2)}, u32[]{:S(2)}) %collective-permute-start.22) | collective-permute-done | bytes 344096 | tf_op jit(solution)/shard_map/ppermute | solution.py:46
  83.6 3.0 %collective-permute-start.13 = (bf16[64,2688]{1,0:T(8,128)(2,1)S(1)}, bf16[64,2688]{1,0:T(8,128)(2,1)S(1)}, u32[]{:S(2)}, u32[]{:S(2)}) collective-permute-start(bf16[64,2688]{1,0:T(8,128)(2,1)S(1)} %activate.4.refs_3_.refs_1_), channel_id=1, source_target_pairs={{0,12},{4,0},{8,4},{12,8},{1,5},{5,9},{9,13},{13,1},{2,14},{6,2},{... | collective-permute-start | bytes 1032200 | tf_op jit(solution)/shard_map/ppermute | solution.py:46
  86.7 2.0 %collective-permute-done.14.refs_4_ = bf16[64,2688]{1,0:T(8,128)(2,1)S(1)} collective-permute-done((bf16[64,2688]{1,0:T(8,128)(2,1)S(1)}, bf16[64,2688]{1,0:T(8,128)(2,1)S(1)}, u32[]{:S(2)}, u32[]{:S(2)}) %collective-permute-start.14) | collective-permute-done | bytes 344096 | tf_op jit(solution)/shard_map/ppermute | solution.py:46
  89.3 5.3 %collective-permute-done.25.refs_3_ = bf16[64,2688]{1,0:T(8,128)(2,1)S(1)} collective-permute-done((bf16[64,2688]{1,0:T(8,128)(2,1)S(1)}, bf16[64,2688]{1,0:T(8,128)(2,1)S(1)}, u32[]{:S(2)}, u32[]{:S(2)}) %collective-permute-start.25) | collective-permute-done | bytes 344096 | tf_op jit(solution)/shard_map/ppermute | solution.py:46
  96.0 2.2 %collective-permute-done.15.refs_3_ = bf16[64,2688]{1,0:T(8,128)(2,1)S(1)} collective-permute-done((bf16[64,2688]{1,0:T(8,128)(2,1)S(1)}, bf16[64,2688]{1,0:T(8,128)(2,1)S(1)}, u32[]{:S(2)}, u32[]{:S(2)}) %collective-permute-start.15) | collective-permute-done | bytes 344096 | tf_op jit(solution)/shard_map/ppermute | solution.py:46
  100.8 4.7 %collective-permute-done.28.refs_4_ = bf16[64,2688]{1,0:T(8,128)(2,1)S(1)} collective-permute-done((bf16[64,2688]{1,0:T(8,128)(2,1)S(1)}, bf16[64,2688]{1,0:T(8,128)(2,1)S(1)}, u32[]{:S(2)}, u32[]{:S(2)}) %collective-permute-start.28) | collective-permute-done | bytes 344096 | tf_op jit(solution)/shard_map/ppermute | solution.py:46
  107.1 2.8 %collective-permute-done.27.refs_2_ = bf16[64,2688]{1,0:T(8,128)(2,1)S(1)} collective-permute-done((bf16[64,2688]{1,0:T(8,128)(2,1)S(1)}, bf16[64,2688]{1,0:T(8,128)(2,1)S(1)}, u32[]{:S(2)}, u32[]{:S(2)}) %collective-permute-start.27) | collective-permute-done | bytes 344096 | tf_op jit(solution)/shard_map/ppermute | solution.py:46
  109.9 4.1 %collective-permute-done.29.refs_3_ = bf16[64,2688]{1,0:T(8,128)(2,1)S(1)} collective-permute-done((bf16[64,2688]{1,0:T(8,128)(2,1)S(1)}, bf16[64,2688]{1,0:T(8,128)(2,1)S(1)}, u32[]{:S(2)}, u32[]{:S(2)}) %collective-permute-start.29) | collective-permute-done | bytes 344096 | tf_op jit(solution)/shard_map/ppermute | solution.py:46
  116.7 4.0 %collective-permute-done.35.refs_2_ = f32[64,2688]{1,0:T(8,128)S(1)} collective-permute-done((f32[64,2688]{1,0:T(8,128)S(1)}, f32[64,2688]{1,0:T(8,128)S(1)}, u32[]{:S(2)}, u32[]{:S(2)}) %collective-permute-start.35) | collective-permute-done | bytes 688160 | tf_op jit(solution)/shard_map/ppermute | solution.py:35
  121.5 3.2 %collective-permute-start.32 = (bf16[64,2688]{1,0:T(8,128)(2,1)S(1)}, bf16[64,2688]{1,0:T(8,128)(2,1)S(1)}, u32[]{:S(2)}, u32[]{:S(2)}) collective-permute-start(bf16[64,2688]{1,0:T(8,128)(2,1)S(1)} %activate.6.refs_5_.refs_1_), channel_id=1, source_target_pairs={{0,12},{4,0},{8,4},{12,8},{1,5},{5,9},{9,13},{13,1},{2,14},{6,2},{... | collective-permute-start | bytes 1032200 | tf_op jit(solution)/shard_map/ppermute | solution.py:46
  124.7 3.2 %collective-permute-start.38 = (bf16[64,2688]{1,0:T(8,128)(2,1)S(1)}, bf16[64,2688]{1,0:T(8,128)(2,1)S(1)}, u32[]{:S(2)}, u32[]{:S(2)}) collective-permute-start(bf16[64,2688]{1,0:T(8,128)(2,1)S(1)} %activate.7.refs_5_.refs_1_), channel_id=1, source_target_pairs={{0,12},{4,0},{8,4},{12,8},{1,5},{5,9},{9,13},{13,1},{2,14},{6,2},{... | collective-permute-start | bytes 1032200 | tf_op jit(solution)/shard_map/ppermute | solution.py:46
  128.0 5.7 %collective-permute-done.39.refs_4_ = bf16[64,2688]{1,0:T(8,128)(2,1)S(1)} collective-permute-done((bf16[64,2688]{1,0:T(8,128)(2,1)S(1)}, bf16[64,2688]{1,0:T(8,128)(2,1)S(1)}, u32[]{:S(2)}, u32[]{:S(2)}) %collective-permute-start.39) | collective-permute-done | bytes 344096 | tf_op jit(solution)/shard_map/ppermute | solution.py:46
  133.7 4.3 %collective-permute-done.34.refs_3_ = bf16[64,2688]{1,0:T(8,128)(2,1)S(1)} collective-permute-done((bf16[64,2688]{1,0:T(8,128)(2,1)S(1)}, bf16[64,2688]{1,0:T(8,128)(2,1)S(1)}, u32[]{:S(2)}, u32[]{:S(2)}) %collective-permute-start.34) | collective-permute-done | bytes 344096 | tf_op jit(solution)/shard_map/ppermute | solution.py:46
  139.1 1.8 %back.5 = (bf16[128,512]{1,0:T(8,128)(2,1)S(1)}, bf16[128,512]{1,0:T(8,128)(2,1)S(1)}) custom-call(s32[3]{0:T(128)S(1)} %pad_add_fusion.refs_0_.r_0_, bf16[256,2688]{1,0:T(8,128)(2,1)S(1)} %get-tuple-element.66.refs_5_.refs_1_.refs_2_, bf16[256,2688]{1,0:T(8,128)(2,1)S(1)} %collective-permute-done.31.refs_2_, bf16[512,1792]{1,0:T(8,128)(2,1)S(1)} %copy-done.1, ...), custom_call_target="tpu_custom_call" | custom-call | tf_op jit(solution)/shard_map/back/pallas_call | solution.py:62
  143.0 2.8 %collective-permute-start.44 = (bf16[128,512]{1,0:T(8,128)(2,1)S(1)}, bf16[128,512]{1,0:T(8,128)(2,1)S(1)}, u32[]{:S(2)}, u32[]{:S(2)}) collective-permute-start(bf16[128,512]{1,0:T(8,128)(2,1)S(1)} %get-tuple-element.76), channel_id=1, source_target_pairs={{0,16},{16,0},{32,48},{48,32},{64,80},{80,64},{96,112},{112,96},{1... | collective-permute-start | bytes 393224 | tf_op jit(solution)/shard_map/ppermute | solution.py:40
  150.1 3.0 %collective-permute-start.46 = (bf16[128,512]{1,0:T(8,128)(2,1)S(1)}, bf16[128,512]{1,0:T(8,128)(2,1)S(1)}, u32[]{:S(2)}, u32[]{:S(2)}) collective-permute-start(bf16[128,512]{1,0:T(8,128)(2,1)S(1)} %get-tuple-element.78), channel_id=1, source_target_pairs={{0,48},{16,32},{32,80},{48,64},{64,112},{80,96},{96,16},{112,0},{1... | collective-permute-start | bytes 393224 | tf_op jit(solution)/shard_map/ppermute | solution.py:40
  156.0 3.2 %collective-permute-start.47 = (bf16[128,512]{1,0:T(8,128)(2,1)S(1)}, bf16[128,512]{1,0:T(8,128)(2,1)S(1)}, u32[]{:S(2)}, u32[]{:S(2)}) collective-permute-start(bf16[128,512]{1,0:T(8,128)(2,1)S(1)} %get-tuple-element.79), channel_id=1, source_target_pairs={{0,80},{16,64},{32,112},{48,96},{64,16},{80,0},{96,48},{112,32},{1... | collective-permute-start | bytes 393224 | tf_op jit(solution)/shard_map/ppermute | solution.py:40
  159.8 5.1 %weight_grads.2 = (bf16[512,1792]{1,0:T(8,128)(2,1)}, bf16[512,1792]{1,0:T(8,128)(2,1)}, bf16[1792,512]{1,0:T(8,128)(2,1)}, f32[8,128]{1,0:T(8,128)S(1)}) custom-call(s32[3]{0:T(128)S(1)} %pad_add_fusion.refs_0_.r_0_, bf16[256,2688]{1,0:T(8,128)(2,1)S(1)} %get-tuple-element.64.refs_3_.refs_1_, ...), custom_call_target="tpu_custom_call" | custom-call | tf_op jit(solution)/shard_map/weight_grads/pallas_call | solution.py:256
  164.9 5.1 %weight_grads.3 = (bf16[512,1792]{1,0:T(8,128)(2,1)}, bf16[512,1792]{1,0:T(8,128)(2,1)}, bf16[1792,512]{1,0:T(8,128)(2,1)}, f32[8,128]{1,0:T(8,128)S(1)}) custom-call(s32[3]{0:T(128)S(1)} %pad_add_fusion.refs_0_.r_0_, bf16[256,2688]{1,0:T(8,128)(2,1)S(1)} %collective-permute-done.26.refs_2_.refs_1_, ...), custom_call_target="tpu_custom_call", output_to_operand_aliasing={{0}: (9, {}), {1}: (10, {}), {2}: (11, {})} | custom-call | tf_op jit(solution)/shard_map/weight_grads/pallas_call | solution.py:256
  (114 shorter events, 54.9 us)
Async XLA Ops:
  13.7 16.8 %collective-permute-start.5 = (bf16[256,1024]{1,0:T(8,128)(2,1)S(1)}, bf16[256,1024]{1,0:T(8,128)(2,1)S(1)}, u32[]{:S(2)}, u32[]{:S(2)}) collective-permute-start(bf16[256,1024]{1,0:T(8,128)(2,1)S(1)} %get-tuple-element.46.refs_1_.refs_5_), channel_id=1, source_target_pairs={{0,32},{32,64},{64,96},{96,0},{1,33},{33,65},{65,97},{97,1},{2,34}... | collective-permute-start | bytes 1572872 | tf_op jit(solution)/shard_map/ppermute | solution.py:35
  15.9 15.9 %collective-permute-start.8 = (bf16[256,1024]{1,0:T(8,128)(2,1)S(1)}, bf16[256,1024]{1,0:T(8,128)(2,1)S(1)}, u32[]{:S(2)}, u32[]{:S(2)}) collective-permute-start(bf16[256,1024]{1,0:T(8,128)(2,1)S(1)} %get-tuple-element.46.refs_1_.refs_5_), channel_id=1, source_target_pairs={{0,96},{32,0},{64,32},{96,64},{1,97},{33,1},{65,33},{97,65},{2,98}... | collective-permute-start | bytes 1572872 | tf_op jit(solution)/shard_map/ppermute | solution.py:35
  32.4 16.8 %collective-permute-start.12 = (bf16[256,1024]{1,0:T(8,128)(2,1)S(1)}, bf16[256,1024]{1,0:T(8,128)(2,1)S(1)}, u32[]{:S(2)}, u32[]{:S(2)}) collective-permute-start(bf16[256,1024]{1,0:T(8,128)(2,1)S(1)} %turn.4.refs_7_), channel_id=1, source_target_pairs={{0,1},{1,0},{2,3},{3,2},{4,5},{5,4},{6,7},{7,6},{8,9},{9,8},{10,11... | collective-permute-start | bytes 1572872 | tf_op jit(solution)/shard_map/ppermute | solution.py:35
  32.9 18.5 %collective-permute-start.11 = (bf16[256,1024]{1,0:T(8,128)(2,1)S(1)}, bf16[256,1024]{1,0:T(8,128)(2,1)S(1)}, u32[]{:S(2)}, u32[]{:S(2)}) collective-permute-start(bf16[256,1024]{1,0:T(8,128)(2,1)S(1)} %get-tuple-element.46.refs_1_.refs_5_), channel_id=1, source_target_pairs={{0,64},{32,96},{64,0},{96,32},{1,65},{33,97},{65,1},{97,33},{2,66}... | collective-permute-start | bytes 1572872 | tf_op jit(solution)/shard_map/ppermute | solution.py:35
  46.7 17.0 %collective-permute-start.9 = (f32[64,2688]{1,0:T(8,128)S(1)}, f32[64,2688]{1,0:T(8,128)S(1)}, u32[]{:S(2)}, u32[]{:S(2)}) collective-permute-start(f32[64,2688]{1,0:T(8,128)S(1)} %beside.4.refs_7_.refs_1_), channel_id=1, source_target_pairs={{0,2},{2,0},{1,3},{3,1},{4,6},{6,4},{5,7},{7,5},{8,10},{10,8},{9,1... | collective-permute-start | bytes 2064392 | tf_op jit(solution)/shard_map/ppermute | solution.py:35
  52.1 15.6 %collective-permute-start.18 = (bf16[256,1024]{1,0:T(8,128)(2,1)S(1)}, bf16[256,1024]{1,0:T(8,128)(2,1)S(1)}, u32[]{:S(2)}, u32[]{:S(2)}) collective-permute-start(bf16[256,1024]{1,0:T(8,128)(2,1)S(1)} %turn.5.refs_3_), channel_id=1, source_target_pairs={{0,1},{1,0},{2,3},{3,2},{4,5},{5,4},{6,7},{7,6},{8,9},{9,8},{10,11... | collective-permute-start | bytes 1572872 | tf_op jit(solution)/shard_map/ppermute | solution.py:35
  52.2 14.7 %collective-permute-start.19 = (bf16[64,2688]{1,0:T(8,128)(2,1)S(1)}, bf16[64,2688]{1,0:T(8,128)(2,1)S(1)}, u32[]{:S(2)}, u32[]{:S(2)}) collective-permute-start(bf16[64,2688]{1,0:T(8,128)(2,1)S(1)} %get-tuple-element.58), channel_id=1, source_target_pairs={{0,4},{4,8},{8,12},{12,0},{1,13},{5,1},{9,5},{13,9},{2,6},{6,10},{... | collective-permute-start | bytes 1032200 | tf_op jit(solution)/shard_map/ppermute | solution.py:46
  53.8 17.5 %collective-permute-start.16 = (bf16[64,2688]{1,0:T(8,128)(2,1)S(1)}, bf16[64,2688]{1,0:T(8,128)(2,1)S(1)}, u32[]{:S(2)}, u32[]{:S(2)}) collective-permute-start(bf16[64,2688]{1,0:T(8,128)(2,1)S(1)} %get-tuple-element.56), channel_id=1, source_target_pairs={{0,12},{4,0},{8,4},{12,8},{1,5},{5,9},{9,13},{13,1},{2,14},{6,2},{... | collective-permute-start | bytes 1032200 | tf_op jit(solution)/shard_map/ppermute | solution.py:46
  57.3 14.0 %collective-permute-start.17 = (bf16[64,2688]{1,0:T(8,128)(2,1)S(1)}, bf16[64,2688]{1,0:T(8,128)(2,1)S(1)}, u32[]{:S(2)}, u32[]{:S(2)}) collective-permute-start(bf16[64,2688]{1,0:T(8,128)(2,1)S(1)} %add.9.refs_3_), channel_id=1, source_target_pairs={{0,4},{4,8},{8,12},{12,0},{1,13},{5,1},{9,5},{13,9},{2,6},{6,10},{... | collective-permute-start | bytes 1032200 | tf_op jit(solution)/shard_map/ppermute | solution.py:46
  63.7 11.1 %collective-permute-start.23 = (bf16[64,2688]{1,0:T(8,128)(2,1)S(1)}, bf16[64,2688]{1,0:T(8,128)(2,1)S(1)}, u32[]{:S(2)}, u32[]{:S(2)}) collective-permute-start(bf16[64,2688]{1,0:T(8,128)(2,1)S(1)} %get-tuple-element.63), channel_id=1, source_target_pairs={{0,12},{4,0},{8,4},{12,8},{1,5},{5,9},{9,13},{13,1},{2,14},{6,2},{... | collective-permute-start | bytes 1032200 | tf_op jit(solution)/shard_map/ppermute | solution.py:46
  67.5 10.8 %collective-permute-start.24 = (bf16[64,2688]{1,0:T(8,128)(2,1)S(1)}, bf16[64,2688]{1,0:T(8,128)(2,1)S(1)}, u32[]{:S(2)}, u32[]{:S(2)}) collective-permute-start(bf16[64,2688]{1,0:T(8,128)(2,1)S(1)} %add.10.refs_7_), channel_id=1, source_target_pairs={{0,4},{4,8},{8,12},{12,0},{1,13},{5,1},{9,5},{13,9},{2,6},{6,10},{... | collective-permute-start | bytes 1032200 | tf_op jit(solution)/shard_map/ppermute | solution.py:46
  70.1 12.7 %collective-permute-start.22 = (bf16[64,2688]{1,0:T(8,128)(2,1)S(1)}, bf16[64,2688]{1,0:T(8,128)(2,1)S(1)}, u32[]{:S(2)}, u32[]{:S(2)}) collective-permute-start(bf16[64,2688]{1,0:T(8,128)(2,1)S(1)} %get-tuple-element.62), channel_id=1, source_target_pairs={{0,4},{4,8},{8,12},{12,0},{1,13},{5,1},{9,5},{13,9},{2,6},{6,10},{... | collective-permute-start | bytes 1032200 | tf_op jit(solution)/shard_map/ppermute | solution.py:46
  71.9 23.3 %collective-permute-start.20 = (f32[64,2688]{1,0:T(8,128)S(1)}, f32[64,2688]{1,0:T(8,128)S(1)}, u32[]{:S(2)}, u32[]{:S(2)}) collective-permute-start(f32[64,2688]{1,0:T(8,128)S(1)} %beside.5.refs_4_.refs_1_), channel_id=1, source_target_pairs={{0,2},{2,0},{1,3},{3,1},{4,6},{6,4},{5,7},{7,5},{8,10},{10,8},{9,1... | collective-permute-start | bytes 2064392 | tf_op jit(solution)/shard_map/ppermute | solution.py:35
  73.5 15.2 %collective-permute-start.14 = (bf16[64,2688]{1,0:T(8,128)(2,1)S(1)}, bf16[64,2688]{1,0:T(8,128)(2,1)S(1)}, u32[]{:S(2)}, u32[]{:S(2)}) collective-permute-start(bf16[64,2688]{1,0:T(8,128)(2,1)S(1)} %activate.4.refs_3_.refs_1_), channel_id=1, source_target_pairs={{0,4},{4,8},{8,12},{12,0},{1,13},{5,1},{9,5},{13,9},{2,6},{6,10},{... | collective-permute-start | bytes 1032200 | tf_op jit(solution)/shard_map/ppermute | solution.py:46
  74.8 14.1 %collective-permute-start.21 = (bf16[64,2688]{1,0:T(8,128)(2,1)S(1)}, bf16[64,2688]{1,0:T(8,128)(2,1)S(1)}, u32[]{:S(2)}, u32[]{:S(2)}) collective-permute-start(bf16[64,2688]{1,0:T(8,128)(2,1)S(1)} %get-tuple-element.60), channel_id=1, source_target_pairs={{0,12},{4,0},{8,4},{12,8},{1,5},{5,9},{9,13},{13,1},{2,14},{6,2},{... | collective-permute-start | bytes 1032200 | tf_op jit(solution)/shard_map/ppermute | solution.py:46
  83.4 11.2 %collective-permute-start.25 = (bf16[64,2688]{1,0:T(8,128)(2,1)S(1)}, bf16[64,2688]{1,0:T(8,128)(2,1)S(1)}, u32[]{:S(2)}, u32[]{:S(2)}) collective-permute-start(bf16[64,2688]{1,0:T(8,128)(2,1)S(1)} %add.11.refs_4_), channel_id=1, source_target_pairs={{0,4},{4,8},{8,12},{12,0},{1,13},{5,1},{9,5},{13,9},{2,6},{6,10},{... | collective-permute-start | bytes 1032200 | tf_op jit(solution)/shard_map/ppermute | solution.py:46
  83.6 12.4 %collective-permute-start.13 = (bf16[64,2688]{1,0:T(8,128)(2,1)S(1)}, bf16[64,2688]{1,0:T(8,128)(2,1)S(1)}, u32[]{:S(2)}, u32[]{:S(2)}) collective-permute-start(bf16[64,2688]{1,0:T(8,128)(2,1)S(1)} %activate.4.refs_3_.refs_1_), channel_id=1, source_target_pairs={{0,12},{4,0},{8,4},{12,8},{1,5},{5,9},{9,13},{13,1},{2,14},{6,2},{... | collective-permute-start | bytes 1032200 | tf_op jit(solution)/shard_map/ppermute | solution.py:46
  88.9 17.5 %collective-permute-start.30 = (f32[64,2688]{1,0:T(8,128)S(1)}, f32[64,2688]{1,0:T(8,128)S(1)}, u32[]{:S(2)}, u32[]{:S(2)}) collective-permute-start(f32[64,2688]{1,0:T(8,128)S(1)} %beside.6.refs_3_.refs_1_), channel_id=1, source_target_pairs={{0,2},{2,0},{1,3},{3,1},{4,6},{6,4},{5,7},{7,5},{8,10},{10,8},{9,1... | collective-permute-start | bytes 2064392 | tf_op jit(solution)/shard_map/ppermute | solution.py:35
  99.0 15.8 %collective-permute-start.26 = (bf16[256,2688]{1,0:T(8,128)(2,1)S(1)}, bf16[256,2688]{1,0:T(8,128)(2,1)S(1)}, u32[]{:S(2)}, u32[]{:S(2)}) collective-permute-start(bf16[256,2688]{1,0:T(8,128)(2,1)S(1)} %get-tuple-element.65), channel_id=1, source_target_pairs={{0,1},{1,0},{2,3},{3,2},{4,5},{5,4},{6,7},{7,6},{8,9},{9,8},{10,11... | collective-permute-start | bytes 4128776 | tf_op jit(solution)/shard_map/ppermute | solution.py:35
  105.5 15.2 %collective-permute-start.35 = (f32[64,2688]{1,0:T(8,128)S(1)}, f32[64,2688]{1,0:T(8,128)S(1)}, u32[]{:S(2)}, u32[]{:S(2)}) collective-permute-start(f32[64,2688]{1,0:T(8,128)S(1)} %beside.7.refs_3_.refs_1_), channel_id=1, source_target_pairs={{0,2},{2,0},{1,3},{3,1},{4,6},{6,4},{5,7},{7,5},{8,10},{10,8},{9,1... | collective-permute-start | bytes 2064392 | tf_op jit(solution)/shard_map/ppermute | solution.py:35
  114.7 24.4 %collective-permute-start.31 = (bf16[256,2688]{1,0:T(8,128)(2,1)S(1)}, bf16[256,2688]{1,0:T(8,128)(2,1)S(1)}, u32[]{:S(2)}, u32[]{:S(2)}) collective-permute-start(bf16[256,2688]{1,0:T(8,128)(2,1)S(1)} %get-tuple-element.68), channel_id=1, source_target_pairs={{0,1},{1,0},{2,3},{3,2},{4,5},{5,4},{6,7},{7,6},{8,9},{9,8},{10,11... | collective-permute-start | bytes 4128776 | tf_op jit(solution)/shard_map/ppermute | solution.py:35
  121.4 12.3 %collective-permute-start.39 = (bf16[64,2688]{1,0:T(8,128)(2,1)S(1)}, bf16[64,2688]{1,0:T(8,128)(2,1)S(1)}, u32[]{:S(2)}, u32[]{:S(2)}) collective-permute-start(bf16[64,2688]{1,0:T(8,128)(2,1)S(1)} %activate.7.refs_5_.refs_1_), channel_id=1, source_target_pairs={{0,4},{4,8},{8,12},{12,0},{1,13},{5,1},{9,5},{13,9},{2,6},{6,10},{... | collective-permute-start | bytes 1032200 | tf_op jit(solution)/shard_map/ppermute | solution.py:46
  121.5 12.2 %collective-permute-start.32 = (bf16[64,2688]{1,0:T(8,128)(2,1)S(1)}, bf16[64,2688]{1,0:T(8,128)(2,1)S(1)}, u32[]{:S(2)}, u32[]{:S(2)}) collective-permute-start(bf16[64,2688]{1,0:T(8,128)(2,1)S(1)} %activate.6.refs_5_.refs_1_), channel_id=1, source_target_pairs={{0,12},{4,0},{8,4},{12,8},{1,5},{5,9},{9,13},{13,1},{2,14},{6,2},{... | collective-permute-start | bytes 1032200 | tf_op jit(solution)/shard_map/ppermute | solution.py:46
  124.7 13.3 %collective-permute-start.34 = (bf16[64,2688]{1,0:T(8,128)(2,1)S(1)}, bf16[64,2688]{1,0:T(8,128)(2,1)S(1)}, u32[]{:S(2)}, u32[]{:S(2)}) collective-permute-start(bf16[64,2688]{1,0:T(8,128)(2,1)S(1)} %collective-permute-done.33.refs_4_), channel_id=1, source_target_pairs={{0,4},{4,8},{8,12},{12,0},{1,13},{5,1},{9,5},{13,9},{2,6},{6,10},{... | collective-permute-start | bytes 1032200 | tf_op jit(solution)/shard_map/ppermute | solution.py:46
  124.7 16.2 %collective-permute-start.38 = (bf16[64,2688]{1,0:T(8,128)(2,1)S(1)}, bf16[64,2688]{1,0:T(8,128)(2,1)S(1)}, u32[]{:S(2)}, u32[]{:S(2)}) collective-permute-start(bf16[64,2688]{1,0:T(8,128)(2,1)S(1)} %activate.7.refs_5_.refs_1_), channel_id=1, source_target_pairs={{0,12},{4,0},{8,4},{12,8},{1,5},{5,9},{9,13},{13,1},{2,14},{6,2},{... | collective-permute-start | bytes 1032200 | tf_op jit(solution)/shard_map/ppermute | solution.py:46
  143.0 13.0 %collective-permute-start.44 = (bf16[128,512]{1,0:T(8,128)(2,1)S(1)}, bf16[128,512]{1,0:T(8,128)(2,1)S(1)}, u32[]{:S(2)}, u32[]{:S(2)}) collective-permute-start(bf16[128,512]{1,0:T(8,128)(2,1)S(1)} %get-tuple-element.76), channel_id=1, source_target_pairs={{0,16},{16,0},{32,48},{48,32},{64,80},{80,64},{96,112},{112,96},{1... | collective-permute-start | bytes 393224 | tf_op jit(solution)/shard_map/ppermute | solution.py:40
  145.8 13.4 %collective-permute-start.45 = (bf16[128,512]{1,0:T(8,128)(2,1)S(1)}, bf16[128,512]{1,0:T(8,128)(2,1)S(1)}, u32[]{:S(2)}, u32[]{:S(2)}) collective-permute-start(bf16[128,512]{1,0:T(8,128)(2,1)S(1)} %get-tuple-element.77), channel_id=1, source_target_pairs={{0,112},{16,96},{32,16},{48,0},{64,48},{80,32},{96,80},{112,64},{1... | collective-permute-start | bytes 393224 | tf_op jit(solution)/shard_map/ppermute | solution.py:40
  146.8 23.2 %collective-permute-start.36 = (bf16[128,512]{1,0:T(8,128)(2,1)S(1)}, bf16[128,512]{1,0:T(8,128)(2,1)S(1)}, u32[]{:S(2)}, u32[]{:S(2)}) collective-permute-start(bf16[128,512]{1,0:T(8,128)(2,1)S(1)} %get-tuple-element.70.refs_5_), channel_id=1, source_target_pairs={{0,96},{32,0},{64,32},{96,64},{1,97},{33,1},{65,33},{97,65},{2,98}... | collective-permute-start | bytes 393224 | tf_op jit(solution)/shard_map/ppermute | solution.py:35
  150.1 20.0 %collective-permute-start.46 = (bf16[128,512]{1,0:T(8,128)(2,1)S(1)}, bf16[128,512]{1,0:T(8,128)(2,1)S(1)}, u32[]{:S(2)}, u32[]{:S(2)}) collective-permute-start(bf16[128,512]{1,0:T(8,128)(2,1)S(1)} %get-tuple-element.78), channel_id=1, source_target_pairs={{0,48},{16,32},{32,80},{48,64},{64,112},{80,96},{96,16},{112,0},{1... | collective-permute-start | bytes 393224 | tf_op jit(solution)/shard_map/ppermute | solution.py:40
  153.1 16.9 %collective-permute-start.41 = (bf16[128,512]{1,0:T(8,128)(2,1)S(1)}, bf16[128,512]{1,0:T(8,128)(2,1)S(1)}, u32[]{:S(2)}, u32[]{:S(2)}) collective-permute-start(bf16[128,512]{1,0:T(8,128)(2,1)S(1)} %get-tuple-element.73.refs_5_), channel_id=1, source_target_pairs={{0,32},{32,64},{64,96},{96,0},{1,33},{33,65},{65,97},{97,1},{2,34}... | collective-permute-start | bytes 393224 | tf_op jit(solution)/shard_map/ppermute | solution.py:35
  156.0 14.1 %collective-permute-start.47 = (bf16[128,512]{1,0:T(8,128)(2,1)S(1)}, bf16[128,512]{1,0:T(8,128)(2,1)S(1)}, u32[]{:S(2)}, u32[]{:S(2)}) collective-permute-start(bf16[128,512]{1,0:T(8,128)(2,1)S(1)} %get-tuple-element.79), channel_id=1, source_target_pairs={{0,80},{16,64},{32,112},{48,96},{64,16},{80,0},{96,48},{112,32},{1... | collective-permute-start | bytes 393224 | tf_op jit(solution)/shard_map/ppermute | solution.py:40
  159.2 10.9 %collective-permute-start.43 = (bf16[128,512]{1,0:T(8,128)(2,1)S(1)}, bf16[128,512]{1,0:T(8,128)(2,1)S(1)}, u32[]{:S(2)}, u32[]{:S(2)}) collective-permute-start(bf16[128,512]{1,0:T(8,128)(2,1)S(1)} %get-tuple-element.75.refs_9_), channel_id=1, source_target_pairs={{0,64},{32,96},{64,0},{96,32},{1,65},{33,97},{65,1},{97,33},{2,66}... | collective-permute-start | bytes 393224 | tf_op jit(solution)/shard_map/ppermute | solution.py:35
  (24 other events, 165.5 us)
